TPU v7x, 32 devices: a whole 2x2x4 slice. The times are simulated.
32 devices in a mesh: ctx: 8 (over z, x), ch: 4 (over y, core).
Axes of the slice: x: 2, y: 2, z: 4, core: 2. Of those that a mesh axis runs over, the one named last changes fastest.
Arguments:
- gate_q: bfloat16 [3072, 4096], P('ctx', 'ch'), may hold values from -6 to 6
- key_k: bfloat16 [3072, 4096], P('ctx', 'ch'), may hold values from -6 to 6
- value_v: bfloat16 [3072, 4096], P('ctx', 'ch'), may hold values from -6 to 6
- long_filter: bfloat16 [3072, 4096], P('ctx', 'ch'), may hold values from -0.109375 to 0.109375
- skip_gain: float32 [4096], P('ch'), may hold values from 0.5 to 1.5
- out_weight: bfloat16 [4096, 4096], P('ch'), may hold values from -0.125 to 0.125
Outputs:
- mixed: bfloat16 [3072, 4096], P('ctx', 'ch')
All inputs are finite; a program needn't handle non-finite values.
Results may differ from a plain program's by a relative error of at most 0.023.
Values may be sent and summed in bfloat16 or wider, within the bound.
No kernel may reach another device: no remote copies, remote signals or barrier semaphores. Data moves between devices by JAX's collectives and lax.ppermute only.
A program may use at most 128 MiB of HBM per device.

v0:
```python
import math

import jax
import jax.numpy as jnp
from jax import lax
from jax.sharding import PartitionSpec as P


def for_sending(value):
    return jax.tree.map(lambda a: a.astype(jnp.bfloat16) if a.dtype == jnp.float32 else a, value)


def angle_table(left_index, right_index, length):
    turns = left_index[:, None] * right_index[None, :] % length
    angles = turns.astype(jnp.float32) * (2.0 * math.pi / length)
    return (jnp.cos(angles), jnp.sin(angles))


def local(gate_q, key_k, value_v, long_filter, skip_gain, out_weight):
    tok_rows, channels = key_k.shape
    group_count = lax.axis_size("ctx")
    position = lax.axis_index("ctx")
    block_rows = tok_rows // group_count
    full_len = 2 * group_count * tok_rows
    highest = lax.Precision.HIGHEST
    gated = (key_k.astype(jnp.float32) * value_v.astype(jnp.float32)).astype(jnp.bfloat16)
    freq_all = jnp.arange(2 * group_count, dtype=jnp.int32)
    block_index = jnp.arange(group_count, dtype=jnp.int32)
    row_index = jnp.arange(tok_rows, dtype=jnp.int32)
    cos_outer, sin_outer = angle_table(freq_all, block_index, 2 * group_count)
    cos_inner, sin_inner = angle_table(row_index, row_index, tok_rows)
    cos_final, sin_final = angle_table(block_index, freq_all, 2 * group_count)
    moved_gated, moved_filter = (
        lax.all_to_all(
            gated.reshape(group_count, block_rows, channels),
            "ctx",
            split_axis=0,
            concat_axis=0,
            tiled=True,
        ),
        lax.all_to_all(
            long_filter.reshape(group_count, block_rows, channels),
            "ctx",
            split_axis=0,
            concat_axis=0,
            tiled=True,
        ),
    )
    signals = jnp.stack([moved_gated, moved_filter]).astype(jnp.float32)
    outer_re = jnp.einsum("ka,sarc->skrc", cos_outer, signals, precision=highest)
    outer_im = -jnp.einsum("ka,sarc->skrc", sin_outer, signals, precision=highest)
    rows_here = position * block_rows + jnp.arange(block_rows, dtype=jnp.int32)
    twist_cos, twist_sin = angle_table(freq_all, rows_here, full_len)
    twist_cos = twist_cos[None, :, :, None]
    twist_sin = twist_sin[None, :, :, None]
    turned_re = outer_re * twist_cos + outer_im * twist_sin
    turned_im = outer_im * twist_cos - outer_re * twist_sin
    spectra = lax.all_to_all(
        jnp.stack([turned_re, turned_im], axis=1).astype(jnp.bfloat16),
        "ctx",
        split_axis=2,
        concat_axis=3,
        tiled=True,
    ).astype(jnp.float32)
    spec_re = jnp.einsum("kb,sebc->sekc", cos_inner, spectra[:, 0], precision=highest) + jnp.einsum(
        "kb,sebc->sekc", sin_inner, spectra[:, 1], precision=highest
    )
    spec_im = jnp.einsum("kb,sebc->sekc", cos_inner, spectra[:, 1], precision=highest) - jnp.einsum(
        "kb,sebc->sekc", sin_inner, spectra[:, 0], precision=highest
    )
    regrouped = lax.all_to_all(
        for_sending(jnp.stack([spec_re, spec_im])), "ctx", split_axis=3, concat_axis=2, tiled=True
    )
    ordered = jnp.swapaxes(regrouped, 2, 3)
    prod_re = ordered[0, 0] * ordered[0, 1] - ordered[1, 0] * ordered[1, 1]
    prod_im = ordered[0, 0] * ordered[1, 1] + ordered[1, 0] * ordered[0, 1]
    restored = lax.all_to_all(
        for_sending(jnp.swapaxes(jnp.stack([prod_re, prod_im]), 1, 2)),
        "ctx",
        split_axis=1,
        concat_axis=2,
        tiled=True,
    )
    prod_re = restored[0]
    prod_im = restored[1]
    back_re = jnp.einsum("bk,ekc->ebc", cos_inner, prod_re, precision=highest) - jnp.einsum(
        "bk,ekc->ebc", sin_inner, prod_im, precision=highest
    )
    back_im = jnp.einsum("bk,ekc->ebc", cos_inner, prod_im, precision=highest) + jnp.einsum(
        "bk,ekc->ebc", sin_inner, prod_re, precision=highest
    )
    own_freq = 2 * position + jnp.arange(2, dtype=jnp.int32)
    undo_cos, undo_sin = angle_table(own_freq, row_index, full_len)
    undo_cos = undo_cos[:, :, None]
    undo_sin = undo_sin[:, :, None]
    wound_re = back_re * undo_cos - back_im * undo_sin
    wound_im = back_im * undo_cos + back_re * undo_sin
    collected = lax.all_to_all(
        for_sending(jnp.stack([wound_re, wound_im])), "ctx", split_axis=2, concat_axis=1, tiled=True
    )
    finished = (
        jnp.einsum("ak,krc->arc", cos_final, collected[0], precision=highest)
        - jnp.einsum("ak,krc->arc", sin_final, collected[1], precision=highest)
    ) * (1.0 / full_len)
    arrived = lax.all_to_all(
        for_sending(finished), "ctx", split_axis=0, concat_axis=0, tiled=True
    ).astype(finished.dtype)
    conv = arrived.reshape(tok_rows, channels)
    hidden = (
        gate_q.astype(jnp.float32) * (conv + skip_gain[None, :] * gated.astype(jnp.float32))
    ).astype(jnp.bfloat16)
    terms = jnp.dot(hidden, out_weight, preferred_element_type=jnp.float32)
    return lax.psum_scatter(terms.astype(jnp.bfloat16), "ch", scatter_dimension=1, tiled=True)


def solution(mesh):
    placed = (
        P("ctx", "ch"),
        P("ctx", "ch"),
        P("ctx", "ch"),
        P("ctx", "ch"),
        P("ch"),
        P("ch", None),
    )
    return jax.shard_map(
        local, mesh=mesh, in_specs=placed, out_specs=P("ctx", "ch"), check_vma=False
    )
```

profile of v0, /device:TPU:20, one launch (start us, length us, event | category | flops | bytes accessed | tf_op | source)
XLA Modules:
  0.0 692.0 jit_solution(5407199291740256094)
XLA Ops:
  9.1 24.2 %all_to_all.81 = bf16[8,48,1024]{2,1,0:T(8,128)(2,1)S(1)} all-to-all(bf16[8,48,1024]{2,1,0:T(8,128)(2,1)S(1)} %bitcast.168), channel_id=1, replica_groups=mesh['ctx'=8,'ch'=4] {'ctx'}, dimensions={0} | all-to-all | bytes 1572864 | tf_op jit(solution)/shard_map/all_to_all | solution.py:34
  33.3 5.4 all-to-all-start.1
  39.4 16.0 %all-to-all-done.1 = bf16[8,48,1024]{2,1,0:T(8,128)(2,1)S(1)} async-done(((bf16[8,48,1024]{2,1,0:T(8,128)(2,1)}), bf16[8,48,1024]{2,1,0:T(8,128)(2,1)S(1)}, u32[]{:S(2)}, u32[]{:S(2)}) %all-to-all-start.1) | async-done | bytes 786464 | tf_op jit(solution)/shard_map/all_to_all | solution.py:41
  55.8 4.2 fusion.16
  60.0 5.0 fusion.7
  65.6 3.5 copy.50
  69.2 143.0 %all_to_all.82 = bf16[2,2,16,48,1024]{4,3,0,1,2:T(8,128)(2,1)S(1)} all-to-all(bf16[2,2,16,48,1024]{4,3,0,1,2:T(8,128)(2,1)S(1)} %copy.50), channel_id=1, replica_groups=mesh['ctx'=8,'ch'=4] {'ctx'}, dimensions={2} | all-to-all | bytes 12582912 | tf_op jit(solution)/shard_map/all_to_all | solution.py:58
  213.5 9.8 %fusion.9 = f32[2,2,1024,384]{3,2,1,0:T(8,128)S(1)} fusion(bf16[2,2,2,384,1024]{4,3,2,1,0:T(8,128)(2,1)S(1)} %bitcast.151), kind=kOutput, calls=%fused_computation.24 | convolution fusion | flops 7249084416 | bytes 9437184 | tf_op jit(solution)/shard_map/kb,sebc->sekc/dot_general | solution.py:65
  223.3 10.0 %fusion.8 = f32[2,2,1024,384]{3,2,1,0:T(8,128)S(1)} fusion(bf16[2,2,2,384,1024]{4,3,2,1,0:T(8,128)(2,1)S(1)} %bitcast.152), kind=kOutput, calls=%fused_computation.23 | convolution fusion | flops 7249084416 | bytes 9437184 | tf_op jit(solution)/shard_map/kb,sebc->sekc/dot_general | solution.py:68
  233.2 9.8 %fusion.4 = bf16[1,2,2,384,1024]{3,4,2,1,0:T(8,128)(2,1)S(1)} fusion(f32[2,2,1024,384]{3,2,1,0:T(8,128)S(1)} %fusion.9, bf16[2,2,2,384,1024]{4,3,2,1,0:T(8,128)(2,1)S(1)} %bitcast.153), kind=kOutput, calls=%fused_computation.13 | convolution fusion | flops 7252230144 | bytes 12582912 | tf_op jit(solution)/shard_map/kb,sebc->sekc/dot_general | solution.py:65
  243.0 9.9 %fusion.5 = bf16[1,2,2,384,1024]{3,4,2,1,0:T(8,128)(2,1)S(1)} fusion(f32[2,2,1024,384]{3,2,1,0:T(8,128)S(1)} %fusion.8, bf16[2,2,2,384,1024]{4,3,2,1,0:T(8,128)(2,1)S(1)} %bitcast.154), kind=kOutput, calls=%fused_computation.14 | convolution fusion | flops 7252230144 | bytes 12582912 | tf_op jit(solution)/shard_map/kb,sebc->sekc/dot_general | solution.py:68
  256.3 16.3 %copy.55 = bf16[2,2,2,384,1024]{4,2,1,0,3:T(2,128)(2,1)} copy(bf16[2,2,2,384,1024]{3,4,2,1,0:T(8,128)(2,1)} %pad_maximum_fusion.1) | data formatting | bytes 12582912 | tf_op jit(solution)/shard_map/stack | solution.py:72
  272.6 141.4 %all_to_all.83 = bf16[2,2,2,384,1024]{4,2,1,0,3:T(2,128)(2,1)S(1)} all-to-all(bf16[2,2,2,384,1024]{4,2,1,0,3:T(2,128)(2,1)} %copy.55), channel_id=1, replica_groups=mesh['ctx'=8,'ch'=4] {'ctx'}, dimensions={3} | all-to-all | bytes 12582912 | tf_op jit(solution)/shard_map/all_to_all | solution.py:71
  421.6 5.7 all-to-all-start.4
  427.6 66.3 %all-to-all-done.4 = bf16[2,16,48,1024]{3,2,0,1:T(8,128)(2,1)S(1)} async-done(((bf16[2,16,48,1024]{3,2,0,1:T(8,128)(2,1)}), bf16[2,16,48,1024]{3,2,0,1:T(8,128)(2,1)S(1)}, u32[]{:S(2)}, u32[]{:S(2)}) %all-to-all-start.4) | async-done | bytes 3145760 | tf_op jit(solution)/shard_map/all_to_all | solution.py:77
  494.9 6.0 fusion.24
  501.1 6.2 fusion.26
  507.3 6.0 convolution_add_fusion
  513.3 6.7 fusion.12
  520.3 6.0 copy.66
  526.4 75.9 %all_to_all.84 = bf16[2,2,384,1024]{3,1,0,2:T(2,128)(2,1)S(1)} all-to-all(bf16[2,2,384,1024]{3,1,0,2:T(2,128)(2,1)} %copy.66), channel_id=1, replica_groups=mesh['ctx'=8,'ch'=4] {'ctx'}, dimensions={2} | all-to-all | bytes 6291456 | tf_op jit(solution)/shard_map/all_to_all | solution.py:98
  615.7 23.2 %all_to_all.85 = bf16[8,48,1024]{2,1,0:T(8,128)(2,1)S(1)} all-to-all(bf16[8,48,1024]{2,1,0:T(8,128)(2,1)S(1)} %copy.70), channel_id=1, replica_groups=mesh['ctx'=8,'ch'=4] {'ctx'}, dimensions={0} | all-to-all | bytes 1572864 | tf_op jit(solution)/shard_map/all_to_all | solution.py:105
  638.9 8.2 %convolution_convert_fusion = bf16[384,4096]{1,0:T(8,128)(2,1)} fusion(bf16[1024,4096]{1,0:T(8,128)(2,1)} %param.11, bf16[384,1024]{1,0:T(8,128)(2,1)S(1)} %bitcast.169, bf16[384,1024]{1,0:T(8,128)(2,1)S(1)} %copy-done.3, bf16[384,1024]{1,0:T(8,128)(2,1)S(1)} %copy-done.4, f32[1024]{0:T(1024)S(1)} %copy-done.5), kind=kOutput, calls=%fused_computation.12 | convolution fusion | flops 3225550848 | bytes 13897728 | tf_op jit(solution)/shard_map/dot_general | solution.py:112
  647.2 37.5 %reduce-scatter.2.cloned.1.call-done = bf16[384,1024]{1,0:T(8,128)(2,1)} async-done(((bf16[384,4096]{1,0:T(8,128)(2,1)}), bf16[384,1024]{1,0:T(8,128)(2,1)}) %reduce-scatter.2.cloned.1.call-update) | async-done | bytes 786448 | tf_op jit(solution)/shard_map/reduce_scatter | solution.py:113
  (43 shorter events, 31.6 us)
Async XLA Ops:
  8.2 0.9 copy-start.2
  33.3 22.1 %all-to-all-start.1 = ((bf16[8,48,1024]{2,1,0:T(8,128)(2,1)}), bf16[8,48,1024]{2,1,0:T(8,128)(2,1)S(1)}, u32[]{:S(2)}, u32[]{:S(2)}) async-start(bf16[8,48,1024]{2,1,0:T(8,128)(2,1)} %bitcast.3), calls=%async_computation.1 | async-start | bytes 1572864 | tf_op jit(solution)/shard_map/all_to_all | solution.py:41
  421.6 72.4 %all-to-all-start.4 = ((bf16[2,16,48,1024]{3,2,0,1:T(8,128)(2,1)}), bf16[2,16,48,1024]{3,2,0,1:T(8,128)(2,1)S(1)}, u32[]{:S(2)}, u32[]{:S(2)}) async-start(bf16[2,16,48,1024]{3,2,0,1:T(8,128)(2,1)} %copy.58), calls=%async_computation.4 | async-start | bytes 6291456 | tf_op jit(solution)/shard_map/all_to_all | solution.py:77
  427.3 257.4 %reduce-scatter.2.cloned.1.call-start = ((), (), s32[]{:S(2)}) async-start(), calls=%async_computation.8 | async-start | bytes 3932160 | tf_op jit(solution)/shard_map/reduce_scatter | solution.py:113
  607.2 2.0 copy-start
  609.2 3.7 copy-start.1
  612.9 26.0 %copy-start.3 = (bf16[384,1024]{1,0:T(8,128)(2,1)S(1)}, bf16[384,1024]{1,0:T(8,128)(2,1)}, u32[]{:S(2)}) copy-start(bf16[384,1024]{1,0:T(8,128)(2,1)} %copy-done.2) | copy-start | bytes 2359300
  612.9 26.0 %copy-start.4 = (bf16[384,1024]{1,0:T(8,128)(2,1)S(1)}, bf16[384,1024]{1,0:T(8,128)(2,1)}, u32[]{:S(2)}) copy-start(bf16[384,1024]{1,0:T(8,128)(2,1)} %param.6) | copy-start | bytes 2359300
  612.9 26.0 %copy-start.5 = (f32[1024]{0:T(1024)S(1)}, f32[1024]{0:T(1024)}, u32[]{:S(2)}) copy-start(f32[1024]{0:T(1024)} %param.10) | copy-start | bytes 12292
Sparse Core Ops, SparseCore 0:
  647.3 37.3 reduce-scatter.1
where the time goes:
time: 704 us; the launch traced here: 692 us
  blocking collectives  408 us (58%)
  waiting for transfers between devices  120 us (17%)
  matrix products  86.2 us (12%)
  local copies, waits for them, and re-layouts  45.9 us (7%)
  between operations  14.1 us (2%)
  starting transfers between devices  11.4 us (2%)
    all_to_all x1, blocking collectives, local(): lax.all_to_all(jnp.stack([turned_re, turned_im], axis=1).astype(jnp.bfloa...  143 us
    all_to_all x1, blocking collectives, local(): lax.all_to_all(for_sending(jnp.stack([spec_re, spec_im])), 'ctx', split_a...  141 us
    all_to_all x1, blocking collectives, local(): lax.all_to_all(for_sending(jnp.stack([wound_re, wound_im])), 'ctx', split...  75.9 us
    all_to_all x1, waiting for transfers between devices, local(): lax.all_to_all(for_sending(jnp.swapaxes(jnp.stack([prod_re, prod_im]), 1,...  66.3 us
    reduce_scatter x1, waiting for transfers between devices, local(): lax.psum_scatter(terms.astype(jnp.bfloat16), 'ch', scatter_dimension=1, t...  37.5 us
    all_to_all x1, blocking collectives, local(): lax.all_to_all(gated.reshape(group_count, block_rows, channels), 'ctx', s...  24.2 us
    all_to_all x1, blocking collectives, local(): lax.all_to_all(for_sending(finished), 'ctx', split_axis=0, concat_axis=0,...  23.2 us
    another operation x1, local copies, waits for them, and re-layouts, local(): jnp.stack([spec_re, spec_im])  16.3 us
  transfers between devices with their start and end apart: 3, of which 3 were waited for; matrix products, arithmetic and copies ran while one was open for 0% of the time, Pallas kernels for 0%

commit v1 on v0

v1 whole, which is shorter than its diff:
```python
import functools
import math

import jax
import jax.numpy as jnp
import numpy as np
from jax import lax
from jax.experimental import pallas as pl
from jax.experimental.pallas import tpu as pltpu
from jax.sharding import PartitionSpec as P

F32 = jnp.float32
BF16 = jnp.bfloat16
VMEM = pl.BlockSpec(memory_space=pltpu.VMEM)
SMEM = pl.BlockSpec(memory_space=pltpu.SMEM)
SUB = 8
PARAMS = pltpu.CompilerParams(vmem_limit_bytes=56 * 2**20)


def tables(total, inner):
    outer = total // inner
    n1 = np.arange(outer)
    eye = np.eye(SUB)
    ang = 2.0 * np.pi * np.outer(n1 + 0.25, n1) / outer
    first = np.stack([np.cos(ang), -np.sin(ang)], axis=1)
    first = np.einsum("kcn,ij->kcinj", first, eye).reshape(2 * outer * SUB, outer * SUB)
    last = np.stack([np.cos(ang), -np.sin(ang)], axis=1) / total
    last = np.einsum("kcn,ij->nikcj", last, eye).reshape(outer * SUB, 2 * outer * SUB)
    n2 = np.arange(inner)
    freq = n1[:, None] + outer * n2[None, :] + 0.25
    ang = 2.0 * np.pi * freq[:, :, None] * n2[None, None, :] / total
    cos, sin = np.cos(ang), np.sin(ang)
    mid = np.concatenate(
        [np.concatenate([cos, sin], axis=2), np.concatenate([-sin, cos], axis=2)], axis=1
    )
    back = np.swapaxes(mid, 1, 2)
    return tuple(jnp.asarray(np.ascontiguousarray(a).astype(jnp.bfloat16)) for a in (first, mid, back, last))


def slices_kernel(idx_ref, *refs, ins, count, width):
    arrays, outs = refs[:ins], refs[ins:]
    me = idx_ref[0]
    for s in range(count):
        at = pl.ds(pl.multiple_of(lax.rem(me + s, count) * width, width), width)
        if ins == 1:
            outs[s][...] = arrays[0][:, at]
        else:
            outs[s][...] = (arrays[0][:, at].astype(F32) * arrays[1][:, at].astype(F32)).astype(BF16)


def send_slices(idx, arrays, count):
    rows, channels = arrays[0].shape
    width = channels // count
    if width % 128:
        value = arrays[0]
        if len(arrays) == 2:
            value = (arrays[0].astype(F32) * arrays[1].astype(F32)).astype(BF16)
        return [
            lax.dynamic_slice_in_dim(value, lax.rem(idx[0] + s, count) * width, width, 1)
            for s in range(count)
        ]
    return pl.pallas_call(
        functools.partial(slices_kernel, ins=len(arrays), count=count, width=width),
        out_shape=[jax.ShapeDtypeStruct((rows, width), BF16)] * count,
        in_specs=[SMEM] + [VMEM] * len(arrays),
        out_specs=[VMEM] * count,
        compiler_params=PARAMS,
        cost_estimate=pl.CostEstimate(flops=rows * channels, bytes_accessed=4 * rows * channels, transcendentals=0),
    )(idx, *arrays)


def exchange(blocks, axis, count):
    out = [blocks[0]]
    for s in range(1, count):
        out.append(lax.ppermute(blocks[s], axis, [(i, (i + s) % count) for i in range(count)]))
    return out


def gather_positions(me, blocks, spot, count):
    outer_here = blocks[0].shape[0] // spot.shape[1]
    for s in range(count):
        src = lax.rem(me + count - s, count)
        spot[pl.ds(src * outer_here, outer_here)] = blocks[s][...].reshape(outer_here, *spot.shape[1:])


def halves(tile):
    tile = tile.astype(F32)
    width = tile.shape[-1]
    return [
        tile[..., at : at + SUB, :].reshape(-1, width).astype(BF16) for at in (0, SUB)
    ]


def forward_first(first_ref, spot, mixed):
    outer, inner, width = spot.shape

    def body(i, carry):
        rows = pl.ds(pl.multiple_of(i * 2 * SUB, 2 * SUB), 2 * SUB)
        parts = [
            jnp.dot(first_ref[...], part, preferred_element_type=F32).reshape(outer, 2, SUB, width)
            for part in halves(spot[:, rows, :])
        ]
        mixed[:, :, rows, :] = jnp.concatenate(parts, axis=2).astype(BF16)
        return carry

    lax.fori_loop(0, inner // (2 * SUB), body, 0)


def filter_kernel(idx_ref, first_ref, mid_ref, *refs, count):
    blocks, (out_ref, spot, mixed) = refs[:count], refs[count:]
    gather_positions(idx_ref[0], blocks, spot, count)
    forward_first(first_ref, spot, mixed)
    outer, _, inner, width = mixed.shape

    def body(k, carry):
        out_ref[k] = jnp.dot(
            mid_ref[k], mixed[k].reshape(2 * inner, width), preferred_element_type=F32
        ).astype(BF16)
        return carry

    lax.fori_loop(0, outer, body, 0)


def conv_kernel(idx_ref, first_ref, mid_ref, back_ref, last_ref, filt_ref, *refs, count):
    blocks, outs, (spot, mixed) = refs[:count], refs[count : 2 * count], refs[2 * count :]
    me = idx_ref[0]
    gather_positions(me, blocks, spot, count)
    forward_first(first_ref, spot, mixed)
    outer, _, inner, width = mixed.shape

    def middle(k, carry):
        spec = jnp.dot(mid_ref[k], mixed[k].reshape(2 * inner, width), preferred_element_type=F32)
        filt = filt_ref[k].astype(F32)
        re, im = spec[:inner], spec[inner:]
        fre, fim = filt[:inner], filt[inner:]
        prod = jnp.concatenate([re * fre - im * fim, re * fim + im * fre], axis=0).astype(BF16)
        turned = jnp.dot(back_ref[k], prod, preferred_element_type=F32)
        mixed[k] = turned.astype(BF16).reshape(2, inner, width)
        return carry

    lax.fori_loop(0, outer, middle, 0)

    def ending(i, carry):
        rows = pl.ds(pl.multiple_of(i * 2 * SUB, 2 * SUB), 2 * SUB)
        parts = [
            jnp.dot(last_ref[...], part, preferred_element_type=F32).reshape(outer, SUB, width)
            for part in halves(mixed[:, :, rows, :])
        ]
        spot[:, rows, :] = jnp.concatenate(parts, axis=1).astype(BF16)
        return carry

    lax.fori_loop(0, inner // (2 * SUB), ending, 0)
    here = outer // count
    for s in range(count):
        dst = lax.rem(me + s, count)
        outs[s][...] = spot[pl.ds(dst * here, here)].reshape(here * inner, width)


def hidden_kernel(idx_ref, gate_ref, key_ref, value_ref, gain_ref, *refs, count):
    blocks, out_ref = refs[:count], refs[count]
    me = idx_ref[0]
    width = blocks[0].shape[1]
    for s in range(count):
        src = lax.rem(me + count - s, count)
        at = pl.ds(pl.multiple_of(src * width, width), width)
        gated = (key_ref[:, at].astype(F32) * value_ref[:, at].astype(F32)).astype(BF16).astype(F32)
        total = blocks[s][...].astype(F32) + gain_ref[:, at] * gated
        out_ref[:, at] = (gate_ref[:, at].astype(F32) * total).astype(BF16)


def make_hidden(idx, gate_q, key_k, value_v, gain, blocks):
    count = len(blocks)
    rows, channels = gate_q.shape
    width = channels // count
    if width % 128:
        conv = jnp.zeros((rows, channels), F32)
        for s in range(count):
            src = lax.rem(idx[0] + count - s, count)
            conv = lax.dynamic_update_slice_in_dim(conv, blocks[s].astype(F32), src * width, 1)
        gated = (key_k.astype(F32) * value_v.astype(F32)).astype(BF16).astype(F32)
        return (gate_q.astype(F32) * (conv + gain * gated)).astype(BF16)
    return pl.pallas_call(
        functools.partial(hidden_kernel, count=count),
        out_shape=jax.ShapeDtypeStruct((rows, channels), BF16),
        in_specs=[SMEM] + [VMEM] * (4 + count),
        out_specs=VMEM,
        compiler_params=PARAMS,
    )(idx, gate_q, key_k, value_v, gain, *blocks)


def project_kernel(group_ref, hid_ref, weight_ref, *refs):
    value = jnp.dot(hid_ref[...], weight_ref[...], preferred_element_type=F32)
    if len(refs) == 2:
        value = value + refs[0][...].astype(F32)
    refs[-1][...] = value.astype(refs[-1].dtype)


def project(hidden, weight, group, groups, extra=None, dtype=BF16):
    rows, channels = hidden.shape
    width = weight.shape[1] // groups
    tile = min(512, width)
    steps = width // tile
    specs = [
        pl.BlockSpec((rows, channels), lambda j, g: (0, 0)),
        pl.BlockSpec((channels, tile), lambda j, g: (0, g[0] * steps + j)),
    ]
    args = [hidden, weight]
    if extra is not None:
        specs.append(pl.BlockSpec((rows, tile), lambda j, g: (0, j)))
        args.append(extra)
    return pl.pallas_call(
        project_kernel,
        out_shape=jax.ShapeDtypeStruct((rows, width), dtype),
        grid_spec=pltpu.PrefetchScalarGridSpec(
            num_scalar_prefetch=1,
            grid=(steps,),
            in_specs=specs,
            out_specs=pl.BlockSpec((rows, tile), lambda j, g: (0, j)),
        ),
        compiler_params=PARAMS,
        cost_estimate=pl.CostEstimate(
            flops=2 * rows * channels * width, bytes_accessed=2 * channels * width, transcendentals=0
        ),
    )(group, *args)


def local(gate_q, key_k, value_v, long_filter, skip_gain, out_weight):
    rows, channels = key_k.shape
    count = lax.axis_size("ctx")
    groups = lax.axis_size("ch")
    chips = groups // 2
    total = rows * count
    inner = next(n for n in range(128, 0, -16) if rows % n == 0)
    outer = total // inner
    width = channels // count
    idx = lax.axis_index("ctx").astype(jnp.int32).reshape(1)
    first, mid, back, last = tables(total, inner)
    spot = pltpu.VMEM((outer, inner, width), BF16)
    mixed = pltpu.VMEM((outer, 2, inner, width), BF16)

    filter_in = exchange(send_slices(idx, [long_filter], count), "ctx", count)
    gated_in = exchange(send_slices(idx, [key_k, value_v], count), "ctx", count)
    spectrum = pl.pallas_call(
        functools.partial(filter_kernel, count=count),
        out_shape=jax.ShapeDtypeStruct((outer, 2 * inner, width), BF16),
        in_specs=[SMEM] + [VMEM] * (2 + count),
        out_specs=VMEM,
        scratch_shapes=[spot, mixed],
        compiler_params=PARAMS,
        cost_estimate=pl.CostEstimate(flops=3 * 10**9, bytes_accessed=8 * 10**6, transcendentals=0),
    )(idx, first, mid, *filter_in)
    conv_out = pl.pallas_call(
        functools.partial(conv_kernel, count=count),
        out_shape=[jax.ShapeDtypeStruct((rows, width), BF16)] * count,
        in_specs=[SMEM] + [VMEM] * (5 + count),
        out_specs=[VMEM] * count,
        scratch_shapes=[spot, mixed],
        compiler_params=PARAMS,
        cost_estimate=pl.CostEstimate(flops=6 * 10**9, bytes_accessed=12 * 10**6, transcendentals=0),
    )(idx, first, mid, back, last, spectrum, *gated_in)
    conv_in = exchange(conv_out, "ctx", count)
    hidden = make_hidden(idx, gate_q, key_k, value_v, skip_gain[None, :], conv_in)

    here = lax.axis_index("ch").astype(jnp.int32)
    chip, core = here // 2, here % 2
    swap = [(i, i ^ 1) for i in range(groups)]

    def group_of(step, which):
        return (lax.rem(chip + step, chips) * 2 + which).reshape(1)

    steps = list(range(1, chips)) + [0]
    crossed = [
        lax.ppermute(project(hidden, out_weight, group_of(step, 1 - core), groups), "ch", swap) for step in steps
    ]
    arrived = []
    for step, extra in zip(steps[:-1], crossed[:-1]):
        part = project(hidden, out_weight, group_of(step, core), groups, extra)
        arrived.append(lax.ppermute(part, "ch", [(i, (i + 2 * step) % groups) for i in range(groups)]))
    result = project(hidden, out_weight, group_of(0, core), groups, crossed[-1], F32)
    for part in arrived:
        result = result + part.astype(F32)
    return result.astype(BF16)


def solution(mesh):
    placed = (
        P("ctx", "ch"),
        P("ctx", "ch"),
        P("ctx", "ch"),
        P("ctx", "ch"),
        P("ch"),
        P("ch", None),
    )
    return jax.shard_map(
        local, mesh=mesh, in_specs=placed, out_specs=P("ctx", "ch"), check_vma=False
    )
```

time: 704 us -> 126 us (0.18); the launches traced: 692 us -> 125 us
  blocking collectives: 408 us -> 0 us
  waiting for transfers between devices: 120 us -> 27.7 us
  matrix products: 86.2 us -> 0 us
  Pallas kernels: 0 us -> 49.8 us
  local copies, waits for them, and re-layouts: 45.9 us -> 3.11 us
  starting transfers between devices: 11.4 us -> 41.2 us
  between operations: 14.1 us -> 0.25 us
    all_to_all x5 -> x0, blocking collectives: 408 us -> none  [the longest x1 143 us: local(): lax.all_to_all(jnp.stack([turned_re, turned_im], axis=1).astype(jnp.bfloa...]
    dot_general x13 -> x0, matrix products: 86.2 us -> none  [the longest x1 9.97 us: local(): jnp.einsum('kb,sebc->sekc', sin_inner, spectra[:, 0], precision=highest)]
    all_to_all x2 -> x0, waiting for transfers between devices: 82.3 us -> none  [the longest x1 66.3 us: local(): lax.all_to_all(for_sending(jnp.swapaxes(jnp.stack([prod_re, prod_im]), 1,...]
    pallas_call x0 -> x9, Pallas kernels: none -> 49.8 us  [the longest x1 17.9 us: local(): pl.pallas_call(functools.partial(conv_kernel, count=count), out_shape=[ja...]
    ppermute x0 -> x24, starting transfers between devices: none -> 41.2 us  [the longest x21 40.2 us: exchange(): lax.ppermute(blocks[s], axis, [(i, (i + s) % count) for i in range(count)])]
    reduce_scatter x1 -> x0, waiting for transfers between devices: 37.5 us -> none  [local(): lax.psum_scatter(terms.astype(jnp.bfloat16), 'ch', scatter_dimension=1, t...]
    ppermute x0 -> x24, waiting for transfers between devices: none -> 27.7 us  [the longest x1 14.6 us: local(): lax.ppermute(part, 'ch', [(i, (i + 2 * step) % groups) for i in range(gro...]
    another operation x3 -> x0, local copies, waits for them, and re-layouts: 25.8 us -> none  [the longest x1 16.3 us: local(): jnp.stack([spec_re, spec_im])]
  transfers between devices with their start and end apart: 3 -> 24, of which waited for: 3 -> 4; matrix products, arithmetic and copies ran while one was open for 0% -> 0% of each run, Pallas kernels for 0% -> 18%
where the time goes in v1:
time: 126 us; the launch traced here: 125 us
  Pallas kernels  49.8 us (40%)
  starting transfers between devices  41.2 us (33%)
  waiting for transfers between devices  27.7 us (22%)
  local copies, waits for them, and re-layouts  3.11 us (2%)
  other arithmetic  2.54 us (2%)
    ppermute x21, starting transfers between devices, exchange(): lax.ppermute(blocks[s], axis, [(i, (i + s) % count) for i in range(count)])  40.2 us
    pallas_call x1, Pallas kernels, local(): pl.pallas_call(functools.partial(conv_kernel, count=count), out_shape=[ja...  17.9 us
    ppermute x1, waiting for transfers between devices, local(): lax.ppermute(part, 'ch', [(i, (i + 2 * step) % groups) for i in range(gro...  14.6 us
    pallas_call x4, Pallas kernels, project(): pl.pallas_call(project_kernel, out_shape=jax.ShapeDtypeStruct((rows, widt...  14.1 us
    ppermute x21, waiting for transfers between devices, exchange(): lax.ppermute(blocks[s], axis, [(i, (i + s) % count) for i in range(count)])  13 us
    pallas_call x1, Pallas kernels, local(): pl.pallas_call(functools.partial(filter_kernel, count=count), out_shape=j...  9.66 us
    pallas_call x2, Pallas kernels, send_slices(): pl.pallas_call(functools.partial(slices_kernel, ins=len(arrays), count=co...  4.82 us
    pallas_call x1, Pallas kernels, make_hidden(): pl.pallas_call(functools.partial(hidden_kernel, count=count), out_shape=j...  3.37 us
  transfers between devices with their start and end apart: 24, of which 4 were waited for; matrix products, arithmetic and copies ran while one was open for 0% of the time, Pallas kernels for 18%

profile of v1, /device:TPU:20, one launch (start us, length us, event | category | flops | bytes accessed | tf_op | source)
XLA Modules:
  0.0 124.6 jit_solution(11524904520865463369)
XLA Ops:
  0.0 2.2 %shard_map.100 = (bf16[384,128]{1,0:T(8,128)(2,1)}, bf16[384,128]{1,0:T(8,128)(2,1)}, bf16[384,128]{1,0:T(8,128)(2,1)}, bf16[384,128]{1,0:T(8,128)(2,1)}, bf16[3...) custom-call(s32[1]{0:T(128)} %bitcast.1.idx_ref, ...), custom_call_target="tpu_custom_call" | custom-call | flops 393216 | bytes 1572864 | tf_op jit(solution)/shard_map/pallas_call | solution.py:62
  2.2 1.5 %collective-permute-start = (bf16[384,128]{1,0:T(8,128)(2,1)}, bf16[384,128]{1,0:T(8,128)(2,1)S(1)}, u32[]{:S(2)}, u32[]{:S(2)}) collective-permute-start(bf16[384,128]{1,0:T(8,128)(2,1)} %get-tuple-element.30), channel_id=1, source_target_pairs={{0,4},{4,8},{8,12},{12,16},{16,20},{20,24},{24,28},{28,0},{1,5},{5... | collective-permute-start | bytes 294920 | tf_op jit(solution)/shard_map/ppermute | solution.py:75
  3.7 1.6 %collective-permute-start.1 = (bf16[384,128]{1,0:T(8,128)(2,1)}, bf16[384,128]{1,0:T(8,128)(2,1)S(1)}, u32[]{:S(2)}, u32[]{:S(2)}) collective-permute-start(bf16[384,128]{1,0:T(8,128)(2,1)} %get-tuple-element.31), channel_id=1, source_target_pairs={{0,8},{4,12},{8,16},{12,20},{16,24},{20,28},{24,0},{28,4},{1,9},{5... | collective-permute-start | bytes 294920 | tf_op jit(solution)/shard_map/ppermute | solution.py:75
  6.5 1.7 %collective-permute-start.3 = (bf16[384,128]{1,0:T(8,128)(2,1)}, bf16[384,128]{1,0:T(8,128)(2,1)S(1)}, u32[]{:S(2)}, u32[]{:S(2)}) collective-permute-start(bf16[384,128]{1,0:T(8,128)(2,1)} %get-tuple-element.33), channel_id=1, source_target_pairs={{0,16},{4,20},{8,24},{12,28},{16,0},{20,4},{24,8},{28,12},{1,17},{... | collective-permute-start | bytes 294920 | tf_op jit(solution)/shard_map/ppermute | solution.py:75
  9.5 2.6 %shard_map.102 = (bf16[384,128]{1,0:T(8,128)(2,1)}, bf16[384,128]{1,0:T(8,128)(2,1)}, bf16[384,128]{1,0:T(8,128)(2,1)}, bf16[384,128]{1,0:T(8,128)(2,1)}, bf16[3...) custom-call(s32[1]{0:T(128)} %bitcast.1.idx_ref, ...), custom_call_target="tpu_custom_call" | custom-call | flops 393216 | bytes 1572864 | tf_op jit(solution)/shard_map/pallas_call | solution.py:62
  12.1 1.4 %collective-permute-start.5 = (bf16[384,128]{1,0:T(8,128)(2,1)S(1)}, bf16[384,128]{1,0:T(8,128)(2,1)S(1)}, u32[]{:S(2)}, u32[]{:S(2)}) collective-permute-start(bf16[384,128]{1,0:T(8,128)(2,1)S(1)} %copy-done.18), channel_id=1, source_target_pairs={{0,24},{4,28},{8,0},{12,4},{16,8},{20,12},{24,16},{28,20},{1,25},{... | collective-permute-start | bytes 294920 | tf_op jit(solution)/shard_map/ppermute | solution.py:75
  13.5 6.4 %collective-permute-start.6 = (bf16[384,128]{1,0:T(8,128)(2,1)S(1)}, bf16[384,128]{1,0:T(8,128)(2,1)S(1)}, u32[]{:S(2)}, u32[]{:S(2)}) collective-permute-start(bf16[384,128]{1,0:T(8,128)(2,1)S(1)} %copy-done.16), channel_id=1, source_target_pairs={{0,28},{4,0},{8,4},{12,8},{16,12},{20,16},{24,20},{28,24},{1,29},{... | collective-permute-start | bytes 294920 | tf_op jit(solution)/shard_map/ppermute | solution.py:75
  20.0 3.5 %collective-permute-start.11 = (bf16[384,128]{1,0:T(8,128)(2,1)}, bf16[384,128]{1,0:T(8,128)(2,1)S(1)}, u32[]{:S(2)}, u32[]{:S(2)}) collective-permute-start(bf16[384,128]{1,0:T(8,128)(2,1)} %get-tuple-element.42), channel_id=1, source_target_pairs={{0,20},{4,24},{8,28},{12,0},{16,4},{20,8},{24,12},{28,16},{1,21},{... | collective-permute-start | bytes 294920 | tf_op jit(solution)/shard_map/ppermute | solution.py:75
  23.5 4.7 %collective-permute-start.12 = (bf16[384,128]{1,0:T(8,128)(2,1)}, bf16[384,128]{1,0:T(8,128)(2,1)S(1)}, u32[]{:S(2)}, u32[]{:S(2)}) collective-permute-start(bf16[384,128]{1,0:T(8,128)(2,1)} %get-tuple-element.43), channel_id=1, source_target_pairs={{0,24},{4,28},{8,0},{12,4},{16,8},{20,12},{24,16},{28,20},{1,25},{... | collective-permute-start | bytes 294920 | tf_op jit(solution)/shard_map/ppermute | solution.py:75
  30.2 4.1 %collective-permute-start.8 = (bf16[384,128]{1,0:T(8,128)(2,1)}, bf16[384,128]{1,0:T(8,128)(2,1)S(1)}, u32[]{:S(2)}, u32[]{:S(2)}) collective-permute-start(bf16[384,128]{1,0:T(8,128)(2,1)} %get-tuple-element.39), channel_id=1, source_target_pairs={{0,8},{4,12},{8,16},{12,20},{16,24},{20,28},{24,0},{28,4},{1,9},{5... | collective-permute-start | bytes 294920 | tf_op jit(solution)/shard_map/ppermute | solution.py:75
  34.3 3.5 %collective-permute-start.9 = (bf16[384,128]{1,0:T(8,128)(2,1)}, bf16[384,128]{1,0:T(8,128)(2,1)S(1)}, u32[]{:S(2)}, u32[]{:S(2)}) collective-permute-start(bf16[384,128]{1,0:T(8,128)(2,1)} %get-tuple-element.40), channel_id=1, source_target_pairs={{0,12},{4,16},{8,20},{12,24},{16,28},{20,0},{24,4},{28,8},{1,13},{... | collective-permute-start | bytes 294920 | tf_op jit(solution)/shard_map/ppermute | solution.py:75
  37.8 9.7 %shard_map.101.filt_ref = bf16[24,256,128]{2,1,0:T(8,128)(2,1)} custom-call(s32[1]{0:T(128)} %bitcast.1.idx_ref, bf16[384,192]{1,0:T(8,128)(2,1)} %constant.46.clone.first_ref, bf16[24,256,256]{2,1,0:T(8,128)(2,1)} %constant.47.clone.mid_ref, bf16[384,128]{1,0:T(8,128)(2,1)} %get-tuple-element.29.refs_0_, bf16[384,128]{1,0:T(8,128)(2,1)} %copy-done.9, ...), custom_call_target="tpu_custom_call" | custom-call | flops 3000000000 | bytes 8000000 | tf_op jit(solution)/shard_map/pallas_call | solution.py:243
  48.3 17.9 %shard_map.103 = (bf16[384,128]{1,0:T(8,128)(2,1)}, bf16[384,128]{1,0:T(8,128)(2,1)}, bf16[384,128]{1,0:T(8,128)(2,1)}, bf16[384,128]{1,0:T(8,128)(2,1)}, bf16[3...) custom-call(s32[1]{0:T(128)} %bitcast.1.idx_ref, ...), custom_call_target="tpu_custom_call" | custom-call | flops 6000000000 | bytes 12000000 | tf_op jit(solution)/shard_map/pallas_call | solution.py:252
  66.8 3.3 %collective-permute-start.16 = (bf16[384,128]{1,0:T(8,128)(2,1)}, bf16[384,128]{1,0:T(8,128)(2,1)S(1)}, u32[]{:S(2)}, u32[]{:S(2)}) collective-permute-start(bf16[384,128]{1,0:T(8,128)(2,1)} %get-tuple-element.48), channel_id=1, source_target_pairs={{0,12},{4,16},{8,20},{12,24},{16,28},{20,0},{24,4},{28,8},{1,13},{... | collective-permute-start | bytes 294920 | tf_op jit(solution)/shard_map/ppermute | solution.py:75
  70.6 1.5 %collective-permute-start.18 = (bf16[384,128]{1,0:T(8,128)(2,1)}, bf16[384,128]{1,0:T(8,128)(2,1)S(1)}, u32[]{:S(2)}, u32[]{:S(2)}) collective-permute-start(bf16[384,128]{1,0:T(8,128)(2,1)} %get-tuple-element.50), channel_id=1, source_target_pairs={{0,20},{4,24},{8,28},{12,0},{16,4},{20,8},{24,12},{28,16},{1,21},{... | collective-permute-start | bytes 294920 | tf_op jit(solution)/shard_map/ppermute | solution.py:75
  72.2 9.3 %collective-permute-done.14.refs_1_ = bf16[384,128]{1,0:T(8,128)(2,1)S(1)} collective-permute-done((bf16[384,128]{1,0:T(8,128)(2,1)}, bf16[384,128]{1,0:T(8,128)(2,1)S(1)}, u32[]{:S(2)}, u32[]{:S(2)}) %collective-permute-start.14) | collective-permute-done | bytes 98336 | tf_op jit(solution)/shard_map/ppermute | solution.py:75
  82.9 3.4 %collective-permute-done.19.refs_6_ = bf16[384,128]{1,0:T(8,128)(2,1)S(1)} collective-permute-done((bf16[384,128]{1,0:T(8,128)(2,1)}, bf16[384,128]{1,0:T(8,128)(2,1)S(1)}, u32[]{:S(2)}, u32[]{:S(2)}) %collective-permute-start.19) | collective-permute-done | bytes 98336 | tf_op jit(solution)/shard_map/ppermute | solution.py:75
  87.2 3.4 %shard_map.104.hid_ref = bf16[384,1024]{1,0:T(8,128)(2,1)} custom-call(s32[1]{0:T(128)} %bitcast.1.idx_ref, bf16[384,1024]{1,0:T(8,128)(2,1)} %gate_ref.1, bf16[384,1024]{1,0:T(8,128)(2,1)} %key_ref.1, bf16[384,1024]{1,0:T(8,128)(2,1)} %value_ref.1, f32[1,1024]{1,0:T(1,128)} %bitcast.6, bf16[384,128]{1,0:T(8,128)(2,1)} %get-tuple-element.45.refs_0_, ...), custom_call_target="tpu_custom_call" | custom-call | tf_op jit(solution)/shard_map/pallas_call | solution.py:182
  90.6 3.4 %shard_map.107 = bf16[384,1024]{1,0:T(8,128)(2,1)} custom-call(s32[1]{0:T(128)} %bitcast.5.group_ref, bf16[384,1024]{1,0:T(8,128)(2,1)} %shard_map.104.hid_ref, bf16[1024,4096]{1,0:T(8,128)(2,1)} %weight_ref.7), custom_call_target="tpu_custom_call" | custom-call | flops 805306368 | bytes 2097152 | tf_op jit(solution)/shard_map/pallas_call | solution.py:211
  94.0 3.4 %shard_map.105 = bf16[384,1024]{1,0:T(8,128)(2,1)} custom-call(s32[1]{0:T(128)} %bitcast.3.group_ref, bf16[384,1024]{1,0:T(8,128)(2,1)} %shard_map.104.hid_ref, bf16[1024,4096]{1,0:T(8,128)(2,1)} %weight_ref.7), custom_call_target="tpu_custom_call" | custom-call | flops 805306368 | bytes 2097152 | tf_op jit(solution)/shard_map/pallas_call | solution.py:211
  98.8 3.6 %shard_map.108 = bf16[384,1024]{1,0:T(8,128)(2,1)} custom-call(s32[1]{0:T(128)} %bitcast.4.group_ref, bf16[384,1024]{1,0:T(8,128)(2,1)} %shard_map.104.hid_ref, bf16[1024,4096]{1,0:T(8,128)(2,1)} %weight_ref.7, bf16[384,1024]{1,0:T(8,128)(2,1)} %copy-done.1), custom_call_target="tpu_custom_call" | custom-call | flops 805306368 | bytes 2097152 | tf_op jit(solution)/shard_map/pallas_call | solution.py:211
  103.7 3.7 %shard_map.106 = f32[384,1024]{1,0:T(8,128)} custom-call(s32[1]{0:T(128)} %bitcast.group_ref, bf16[384,1024]{1,0:T(8,128)(2,1)} %shard_map.104.hid_ref, bf16[1024,4096]{1,0:T(8,128)(2,1)} %weight_ref.7, bf16[384,1024]{1,0:T(8,128)(2,1)} %copy-done), custom_call_target="tpu_custom_call" | custom-call | flops 805306368 | bytes 2097152 | tf_op jit(solution)/shard_map/pallas_call | solution.py:211
  107.4 14.6 %collective-permute-done.23 = bf16[384,1024]{1,0:T(8,128)(2,1)S(1)} collective-permute-done((bf16[384,1024]{1,0:T(8,128)(2,1)}, bf16[384,1024]{1,0:T(8,128)(2,1)S(1)}, u32[]{:S(2)}, u32[]{:S(2)}) %collective-permute-start.23) | collective-permute-done | bytes 786464 | tf_op jit(solution)/shard_map/ppermute | solution.py:278
  122.0 2.5 %add_convert_fusion = bf16[384,1024]{1,0:T(8,128)(2,1)} fusion(f32[384,1024]{1,0:T(8,128)} %shard_map.106, bf16[384,1024]{1,0:T(8,128)(2,1)S(1)} %collective-permute-done.23), kind=kLoop, calls=%fused_computation | loop fusion | flops 1179648 | bytes 3145728 | tf_op jit(solution)/shard_map/convert_element_type | solution.py:282
  (84 shorter events, 11.4 us)
Async XLA Ops:
  2.2 9.9 %collective-permute-start = (bf16[384,128]{1,0:T(8,128)(2,1)}, bf16[384,128]{1,0:T(8,128)(2,1)S(1)}, u32[]{:S(2)}, u32[]{:S(2)}) collective-permute-start(bf16[384,128]{1,0:T(8,128)(2,1)} %get-tuple-element.30), channel_id=1, source_target_pairs={{0,4},{4,8},{8,12},{12,16},{16,20},{20,24},{24,28},{28,0},{1,5},{5... | collective-permute-start | bytes 294920 | tf_op jit(solution)/shard_map/ppermute | solution.py:75
  3.7 9.8 %collective-permute-start.1 = (bf16[384,128]{1,0:T(8,128)(2,1)}, bf16[384,128]{1,0:T(8,128)(2,1)S(1)}, u32[]{:S(2)}, u32[]{:S(2)}) collective-permute-start(bf16[384,128]{1,0:T(8,128)(2,1)} %get-tuple-element.31), channel_id=1, source_target_pairs={{0,8},{4,12},{8,16},{12,20},{16,24},{20,28},{24,0},{28,4},{1,9},{5... | collective-permute-start | bytes 294920 | tf_op jit(solution)/shard_map/ppermute | solution.py:75
  5.3 14.6 %collective-permute-start.2 = (bf16[384,128]{1,0:T(8,128)(2,1)}, bf16[384,128]{1,0:T(8,128)(2,1)S(1)}, u32[]{:S(2)}, u32[]{:S(2)}) collective-permute-start(bf16[384,128]{1,0:T(8,128)(2,1)} %get-tuple-element.32), channel_id=1, source_target_pairs={{0,12},{4,16},{8,20},{12,24},{16,28},{20,0},{24,4},{28,8},{1,13},{... | collective-permute-start | bytes 294920 | tf_op jit(solution)/shard_map/ppermute | solution.py:75
  6.5 13.5 %collective-permute-start.3 = (bf16[384,128]{1,0:T(8,128)(2,1)}, bf16[384,128]{1,0:T(8,128)(2,1)S(1)}, u32[]{:S(2)}, u32[]{:S(2)}) collective-permute-start(bf16[384,128]{1,0:T(8,128)(2,1)} %get-tuple-element.33), channel_id=1, source_target_pairs={{0,16},{4,20},{8,24},{12,28},{16,0},{20,4},{24,8},{28,12},{1,17},{... | collective-permute-start | bytes 294920 | tf_op jit(solution)/shard_map/ppermute | solution.py:75
  8.2 15.3 %collective-permute-start.4 = (bf16[384,128]{1,0:T(8,128)(2,1)}, bf16[384,128]{1,0:T(8,128)(2,1)S(1)}, u32[]{:S(2)}, u32[]{:S(2)}) collective-permute-start(bf16[384,128]{1,0:T(8,128)(2,1)} %get-tuple-element.34), channel_id=1, source_target_pairs={{0,20},{4,24},{8,28},{12,0},{16,4},{20,8},{24,12},{28,16},{1,21},{... | collective-permute-start | bytes 294920 | tf_op jit(solution)/shard_map/ppermute | solution.py:75
  12.1 16.1 %collective-permute-start.5 = (bf16[384,128]{1,0:T(8,128)(2,1)S(1)}, bf16[384,128]{1,0:T(8,128)(2,1)S(1)}, u32[]{:S(2)}, u32[]{:S(2)}) collective-permute-start(bf16[384,128]{1,0:T(8,128)(2,1)S(1)} %copy-done.18), channel_id=1, source_target_pairs={{0,24},{4,28},{8,0},{12,4},{16,8},{20,12},{24,16},{28,20},{1,25},{... | collective-permute-start | bytes 294920 | tf_op jit(solution)/shard_map/ppermute | solution.py:75
  13.5 15.7 %collective-permute-start.6 = (bf16[384,128]{1,0:T(8,128)(2,1)S(1)}, bf16[384,128]{1,0:T(8,128)(2,1)S(1)}, u32[]{:S(2)}, u32[]{:S(2)}) collective-permute-start(bf16[384,128]{1,0:T(8,128)(2,1)S(1)} %copy-done.16), channel_id=1, source_target_pairs={{0,28},{4,0},{8,4},{12,8},{16,12},{20,16},{24,20},{28,24},{1,29},{... | collective-permute-start | bytes 294920 | tf_op jit(solution)/shard_map/ppermute | solution.py:75
  20.0 10.2 %collective-permute-start.10 = (bf16[384,128]{1,0:T(8,128)(2,1)}, bf16[384,128]{1,0:T(8,128)(2,1)S(1)}, u32[]{:S(2)}, u32[]{:S(2)}) collective-permute-start(bf16[384,128]{1,0:T(8,128)(2,1)} %get-tuple-element.41), channel_id=1, source_target_pairs={{0,16},{4,20},{8,24},{12,28},{16,0},{20,4},{24,8},{28,12},{1,17},{... | collective-permute-start | bytes 294920 | tf_op jit(solution)/shard_map/ppermute | solution.py:75
  20.0 14.4 %collective-permute-start.11 = (bf16[384,128]{1,0:T(8,128)(2,1)}, bf16[384,128]{1,0:T(8,128)(2,1)S(1)}, u32[]{:S(2)}, u32[]{:S(2)}) collective-permute-start(bf16[384,128]{1,0:T(8,128)(2,1)} %get-tuple-element.42), channel_id=1, source_target_pairs={{0,20},{4,24},{8,28},{12,0},{16,4},{20,8},{24,12},{28,16},{1,21},{... | collective-permute-start | bytes 294920 | tf_op jit(solution)/shard_map/ppermute | solution.py:75
  23.5 24.0 %collective-permute-start.12 = (bf16[384,128]{1,0:T(8,128)(2,1)}, bf16[384,128]{1,0:T(8,128)(2,1)S(1)}, u32[]{:S(2)}, u32[]{:S(2)}) collective-permute-start(bf16[384,128]{1,0:T(8,128)(2,1)} %get-tuple-element.43), channel_id=1, source_target_pairs={{0,24},{4,28},{8,0},{12,4},{16,8},{20,12},{24,16},{28,20},{1,25},{... | collective-permute-start | bytes 294920 | tf_op jit(solution)/shard_map/ppermute | solution.py:75
  28.2 19.4 %collective-permute-start.13 = (bf16[384,128]{1,0:T(8,128)(2,1)}, bf16[384,128]{1,0:T(8,128)(2,1)S(1)}, u32[]{:S(2)}, u32[]{:S(2)}) collective-permute-start(bf16[384,128]{1,0:T(8,128)(2,1)} %get-tuple-element.44), channel_id=1, source_target_pairs={{0,28},{4,0},{8,4},{12,8},{16,12},{20,16},{24,20},{28,24},{1,29},{... | collective-permute-start | bytes 294920 | tf_op jit(solution)/shard_map/ppermute | solution.py:75
  29.2 18.3 %collective-permute-start.7 = (bf16[384,128]{1,0:T(8,128)(2,1)}, bf16[384,128]{1,0:T(8,128)(2,1)S(1)}, u32[]{:S(2)}, u32[]{:S(2)}) collective-permute-start(bf16[384,128]{1,0:T(8,128)(2,1)} %get-tuple-element.38), channel_id=1, source_target_pairs={{0,4},{4,8},{8,12},{12,16},{16,20},{20,24},{24,28},{28,0},{1,5},{5... | collective-permute-start | bytes 294920 | tf_op jit(solution)/shard_map/ppermute | solution.py:75
  30.2 17.4 %collective-permute-start.8 = (bf16[384,128]{1,0:T(8,128)(2,1)}, bf16[384,128]{1,0:T(8,128)(2,1)S(1)}, u32[]{:S(2)}, u32[]{:S(2)}) collective-permute-start(bf16[384,128]{1,0:T(8,128)(2,1)} %get-tuple-element.39), channel_id=1, source_target_pairs={{0,8},{4,12},{8,16},{12,20},{16,24},{20,28},{24,0},{28,4},{1,9},{5... | collective-permute-start | bytes 294920 | tf_op jit(solution)/shard_map/ppermute | solution.py:75
  34.3 13.3 %collective-permute-start.9 = (bf16[384,128]{1,0:T(8,128)(2,1)}, bf16[384,128]{1,0:T(8,128)(2,1)S(1)}, u32[]{:S(2)}, u32[]{:S(2)}) collective-permute-start(bf16[384,128]{1,0:T(8,128)(2,1)} %get-tuple-element.40), channel_id=1, source_target_pairs={{0,12},{4,16},{8,20},{12,24},{16,28},{20,0},{24,4},{28,8},{1,13},{... | collective-permute-start | bytes 294920 | tf_op jit(solution)/shard_map/ppermute | solution.py:75
  66.2 15.3 %collective-permute-start.14 = (bf16[384,128]{1,0:T(8,128)(2,1)}, bf16[384,128]{1,0:T(8,128)(2,1)S(1)}, u32[]{:S(2)}, u32[]{:S(2)}) collective-permute-start(bf16[384,128]{1,0:T(8,128)(2,1)} %get-tuple-element.46), channel_id=1, source_target_pairs={{0,4},{4,8},{8,12},{12,16},{16,20},{20,24},{24,28},{28,0},{1,5},{5... | collective-permute-start | bytes 294920 | tf_op jit(solution)/shard_map/ppermute | solution.py:75
  66.2 15.3 %collective-permute-start.15 = (bf16[384,128]{1,0:T(8,128)(2,1)}, bf16[384,128]{1,0:T(8,128)(2,1)S(1)}, u32[]{:S(2)}, u32[]{:S(2)}) collective-permute-start(bf16[384,128]{1,0:T(8,128)(2,1)} %get-tuple-element.47), channel_id=1, source_target_pairs={{0,8},{4,12},{8,16},{12,20},{16,24},{20,28},{24,0},{28,4},{1,9},{5... | collective-permute-start | bytes 294920 | tf_op jit(solution)/shard_map/ppermute | solution.py:75
  66.8 16.0 %collective-permute-start.16 = (bf16[384,128]{1,0:T(8,128)(2,1)}, bf16[384,128]{1,0:T(8,128)(2,1)S(1)}, u32[]{:S(2)}, u32[]{:S(2)}) collective-permute-start(bf16[384,128]{1,0:T(8,128)(2,1)} %get-tuple-element.48), channel_id=1, source_target_pairs={{0,12},{4,16},{8,20},{12,24},{16,28},{20,0},{24,4},{28,8},{1,13},{... | collective-permute-start | bytes 294920 | tf_op jit(solution)/shard_map/ppermute | solution.py:75
  70.1 12.7 %collective-permute-start.17 = (bf16[384,128]{1,0:T(8,128)(2,1)}, bf16[384,128]{1,0:T(8,128)(2,1)S(1)}, u32[]{:S(2)}, u32[]{:S(2)}) collective-permute-start(bf16[384,128]{1,0:T(8,128)(2,1)} %get-tuple-element.49), channel_id=1, source_target_pairs={{0,16},{4,20},{8,24},{12,28},{16,0},{20,4},{24,8},{28,12},{1,17},{... | collective-permute-start | bytes 294920 | tf_op jit(solution)/shard_map/ppermute | solution.py:75
  70.6 12.2 %collective-permute-start.18 = (bf16[384,128]{1,0:T(8,128)(2,1)}, bf16[384,128]{1,0:T(8,128)(2,1)S(1)}, u32[]{:S(2)}, u32[]{:S(2)}) collective-permute-start(bf16[384,128]{1,0:T(8,128)(2,1)} %get-tuple-element.50), channel_id=1, source_target_pairs={{0,20},{4,24},{8,28},{12,0},{16,4},{20,8},{24,12},{28,16},{1,21},{... | collective-permute-start | bytes 294920 | tf_op jit(solution)/shard_map/ppermute | solution.py:75
  81.5 4.8 %collective-permute-start.19 = (bf16[384,128]{1,0:T(8,128)(2,1)}, bf16[384,128]{1,0:T(8,128)(2,1)S(1)}, u32[]{:S(2)}, u32[]{:S(2)}) collective-permute-start(bf16[384,128]{1,0:T(8,128)(2,1)} %get-tuple-element.51), channel_id=1, source_target_pairs={{0,24},{4,28},{8,0},{12,4},{16,8},{20,12},{24,16},{28,20},{1,25},{... | collective-permute-start | bytes 294920 | tf_op jit(solution)/shard_map/ppermute | solution.py:75
  81.5 5.1 %collective-permute-start.20 = (bf16[384,128]{1,0:T(8,128)(2,1)}, bf16[384,128]{1,0:T(8,128)(2,1)S(1)}, u32[]{:S(2)}, u32[]{:S(2)}) collective-permute-start(bf16[384,128]{1,0:T(8,128)(2,1)} %get-tuple-element.52), channel_id=1, source_target_pairs={{0,28},{4,0},{8,4},{12,8},{16,12},{20,16},{24,20},{28,24},{1,29},{... | collective-permute-start | bytes 294920 | tf_op jit(solution)/shard_map/ppermute | solution.py:75
  94.0 3.9 %collective-permute-start.22 = (bf16[384,1024]{1,0:T(8,128)(2,1)}, bf16[384,1024]{1,0:T(8,128)(2,1)S(1)}, u32[]{:S(2)}, u32[]{:S(2)}) collective-permute-start(bf16[384,1024]{1,0:T(8,128)(2,1)} %shard_map.107), channel_id=1, source_target_pairs={{0,1},{1,0},{2,3},{3,2},{4,5},{5,4},{6,7},{7,6},{8,9},{9,8},{10,11... | collective-permute-start | bytes 2359304 | tf_op jit(solution)/shard_map/ppermute | solution.py:273
  97.4 5.5 %collective-permute-start.21 = (bf16[384,1024]{1,0:T(8,128)(2,1)}, bf16[384,1024]{1,0:T(8,128)(2,1)S(1)}, u32[]{:S(2)}, u32[]{:S(2)}) collective-permute-start(bf16[384,1024]{1,0:T(8,128)(2,1)} %shard_map.105), channel_id=1, source_target_pairs={{0,1},{1,0},{2,3},{3,2},{4,5},{5,4},{6,7},{7,6},{8,9},{9,8},{10,11... | collective-permute-start | bytes 2359304 | tf_op jit(solution)/shard_map/ppermute | solution.py:273
  102.4 19.7 %collective-permute-start.23 = (bf16[384,1024]{1,0:T(8,128)(2,1)}, bf16[384,1024]{1,0:T(8,128)(2,1)S(1)}, u32[]{:S(2)}, u32[]{:S(2)}) collective-permute-start(bf16[384,1024]{1,0:T(8,128)(2,1)} %shard_map.108), channel_id=1, source_target_pairs={{0,2},{1,3},{2,0},{3,1},{4,6},{5,7},{6,4},{7,5},{8,10},{9,11},{10,... | collective-permute-start | bytes 2359304 | tf_op jit(solution)/shard_map/ppermute | solution.py:278
  (25 other events, 197.6 us)

commit v2 on v1

v2 whole, which is shorter than its diff:
```python
import functools
import math

import jax
import jax.numpy as jnp
import numpy as np
from jax import lax
from jax.experimental import pallas as pl
from jax.experimental.pallas import tpu as pltpu
from jax.sharding import PartitionSpec as P

F32 = jnp.float32
BF16 = jnp.bfloat16
VMEM = pl.BlockSpec(memory_space=pltpu.VMEM)
SMEM = pl.BlockSpec(memory_space=pltpu.SMEM)
HBM = pl.BlockSpec(memory_space=pltpu.HBM)
SUB = 8


def params(nbytes):
    return pltpu.CompilerParams(vmem_limit_bytes=int(min(nbytes + 8 * 2**20, 58 * 2**20)))


def tables(total, inner):
    outer = total // inner
    n1 = np.arange(outer)
    eye = np.eye(SUB)
    ang = 2.0 * np.pi * np.outer(n1 + 0.25, n1) / outer
    first = np.stack([np.cos(ang), -np.sin(ang)], axis=1)
    first = np.einsum("kcn,ij->kcinj", first, eye).reshape(2 * outer * SUB, outer * SUB)
    last = np.stack([np.cos(ang), -np.sin(ang)], axis=1) / total
    last = np.einsum("kcn,ij->nikcj", last, eye).reshape(outer * SUB, 2 * outer * SUB)
    n2 = np.arange(inner)
    freq = n1[:, None] + outer * n2[None, :] + 0.25
    ang = 2.0 * np.pi * freq[:, :, None] * n2[None, None, :] / total
    cos, sin = np.cos(ang), np.sin(ang)
    mid = np.concatenate(
        [np.concatenate([cos, sin], axis=2), np.concatenate([-sin, cos], axis=2)], axis=1
    )
    back = np.swapaxes(mid, 1, 2)
    return tuple(jnp.asarray(np.ascontiguousarray(a).astype(jnp.bfloat16)) for a in (first, mid, back, last))


def split_kernel(idx_ref, array_ref, *refs, count):
    *outs, sems = refs
    width = outs[0].shape[1]
    copies = []
    for s in range(count):
        at = pl.ds(pl.multiple_of(lax.rem(idx_ref[0] + s, count) * width, width), width)
        copies.append(pltpu.make_async_copy(array_ref.at[:, at], outs[s], sems.at[s]))
        copies[-1].start()
    for copy in copies:
        copy.wait()


def gate_kernel(idx_ref, key_ref, value_ref, *outs, count):
    width = outs[0].shape[1]
    for s in range(count):
        at = pl.ds(pl.multiple_of(lax.rem(idx_ref[0] + s, count) * width, width), width)
        outs[s][...] = (key_ref[:, at].astype(F32) * value_ref[:, at].astype(F32)).astype(BF16)


def send_slices(idx, arrays, count):
    rows, channels = arrays[0].shape
    width = channels // count
    if width % 128:
        value = arrays[0]
        if len(arrays) == 2:
            value = (arrays[0].astype(F32) * arrays[1].astype(F32)).astype(BF16)
        return [
            lax.dynamic_slice_in_dim(value, lax.rem(idx[0] + s, count) * width, width, 1)
            for s in range(count)
        ]
    alone = len(arrays) == 1
    if alone:
        arrays = [pltpu.with_memory_space_constraint(arrays[0], pltpu.HBM)]
    return pl.pallas_call(
        functools.partial(split_kernel if alone else gate_kernel, count=count),
        out_shape=[jax.ShapeDtypeStruct((rows, width), BF16)] * count,
        in_specs=[SMEM] + ([HBM] if alone else [VMEM] * 2),
        out_specs=[VMEM] * count,
        scratch_shapes=[pltpu.SemaphoreType.DMA((count,))] if alone else [],
        compiler_params=params(2 * (len(arrays) + 1) * rows * channels),
        cost_estimate=pl.CostEstimate(flops=rows * channels, bytes_accessed=4 * rows * channels, transcendentals=0),
    )(idx, *arrays)


def exchange(blocks, axis, count):
    out = [blocks[0]]
    for s in range(1, count):
        out.append(lax.ppermute(blocks[s], axis, [(i, (i + s) % count) for i in range(count)]))
    return out


def gather_positions(me, blocks, spot, count):
    outer_here = blocks[0].shape[0] // spot.shape[1]
    for s in range(count):
        src = lax.rem(me + count - s, count)
        spot[pl.ds(src * outer_here, outer_here)] = blocks[s][...].reshape(outer_here, *spot.shape[1:])


def halves(tile):
    tile = tile.astype(F32)
    width = tile.shape[-1]
    return jnp.concatenate(
        [tile[..., at : at + SUB, :].reshape(-1, width).astype(BF16) for at in (0, SUB)], axis=1
    )


def joined(value, lead):
    width = value.shape[1] // 2
    parts = [value[:, at : at + width].reshape(*lead, SUB, width) for at in (0, width)]
    return jnp.concatenate(parts, axis=len(lead)).astype(BF16)


def for_each(count, body):
    if count <= 32:
        for i in range(count):
            body(i)
    else:
        lax.fori_loop(0, count, lambda i, c: (body(i), c)[1], 0, unroll=4 if count % 4 == 0 else 1)


def forward_first(first_ref, spot, mixed):
    outer, inner, _ = spot.shape

    def body(i):
        rows = pl.ds(i * 2 * SUB, 2 * SUB)
        value = jnp.dot(first_ref[...], halves(spot[:, rows, :]), preferred_element_type=F32)
        mixed[:, :, rows, :] = joined(value, (outer, 2))

    for_each(inner // (2 * SUB), body)


def filter_kernel(idx_ref, first_ref, mid_ref, *refs, count):
    blocks, (out_ref, spot, mixed) = refs[:count], refs[count:]
    gather_positions(idx_ref[0], blocks, spot, count)
    forward_first(first_ref, spot, mixed)
    outer, _, inner, width = mixed.shape

    def body(k):
        out_ref[k] = jnp.dot(
            mid_ref[k], mixed[k].reshape(2 * inner, width), preferred_element_type=F32
        ).astype(BF16)

    for_each(outer, body)


def conv_kernel(idx_ref, first_ref, mid_ref, back_ref, last_ref, filt_ref, *refs, count):
    blocks, outs, (spot, mixed) = refs[:count], refs[count : 2 * count], refs[2 * count :]
    me = idx_ref[0]
    gather_positions(me, blocks, spot, count)
    forward_first(first_ref, spot, mixed)
    outer, _, inner, width = mixed.shape

    def middle(k):
        spec = jnp.dot(mid_ref[k], mixed[k].reshape(2 * inner, width), preferred_element_type=F32)
        filt = filt_ref[k].astype(F32)
        re, im = spec[:inner], spec[inner:]
        fre, fim = filt[:inner], filt[inner:]
        prod = jnp.concatenate([re * fre - im * fim, re * fim + im * fre], axis=0).astype(BF16)
        turned = jnp.dot(back_ref[k], prod, preferred_element_type=F32)
        mixed[k] = turned.astype(BF16).reshape(2, inner, width)

    for_each(outer, middle)

    def ending(i):
        rows = pl.ds(i * 2 * SUB, 2 * SUB)
        value = jnp.dot(last_ref[...], halves(mixed[:, :, rows, :]), preferred_element_type=F32)
        spot[:, rows, :] = joined(value, (outer,))

    for_each(inner // (2 * SUB), ending)
    here = outer // count
    for s in range(count):
        dst = lax.rem(me + s, count)
        outs[s][...] = spot[pl.ds(dst * here, here)].reshape(here * inner, width)


def prepare_kernel(order_ref, key_ref, value_ref, gain_ref, weight_ref, skip_ref, *refs):
    *outs, sems = refs
    width = outs[0].shape[1]
    copies = []
    for j, out_ref in enumerate(outs):
        at = pl.ds(pl.multiple_of(order_ref[j] * width, width), width)
        copies.append(pltpu.make_async_copy(weight_ref.at[:, at], out_ref, sems.at[j]))
        copies[-1].start()
    gated = (key_ref[...].astype(F32) * value_ref[...].astype(F32)).astype(BF16).astype(F32)
    skip_ref[...] = gain_ref[...] * gated
    for copy in copies:
        copy.wait()


def prepare(order, key_k, value_v, gain, weight):
    groups = order.shape[0]
    width = weight.shape[1] // groups
    return pl.pallas_call(
        prepare_kernel,
        out_shape=[jax.ShapeDtypeStruct(key_k.shape, F32)]
        + [jax.ShapeDtypeStruct((weight.shape[0], width), BF16)] * groups,
        in_specs=[SMEM] + [VMEM] * 3 + [HBM],
        out_specs=[VMEM] * (1 + groups),
        scratch_shapes=[pltpu.SemaphoreType.DMA((groups,))],
        compiler_params=params(8 * key_k.size + 2 * weight.size),
        cost_estimate=pl.CostEstimate(flops=key_k.size, bytes_accessed=2 * weight.size, transcendentals=0),
    )(order, key_k, value_v, gain, pltpu.with_memory_space_constraint(weight, pltpu.HBM))


def hidden_kernel(idx_ref, gate_ref, skip_ref, weight_ref, *refs, count):
    blocks, out_ref, part_refs = refs[:count], refs[count], refs[count + 1 :]
    me = idx_ref[0]
    width = blocks[0].shape[1]
    for s in range(count):
        src = lax.rem(me + count - s, count)
        at = pl.ds(pl.multiple_of(src * width, width), width)
        total = blocks[s][...].astype(F32) + skip_ref[:, at]
        out_ref[:, at] = (gate_ref[:, at].astype(F32) * total).astype(BF16)
    times_columns(out_ref, weight_ref, part_refs)


def times_columns(hid_ref, weight_ref, part_refs, extra_refs=()):
    rows, width = part_refs[0].shape
    tile = min(256, width)
    for r, part_ref in enumerate(part_refs):
        for j in range(width // tile):
            cols = slice(j * tile, (j + 1) * tile)
            value = jnp.dot(
                hid_ref[r * rows : (r + 1) * rows, :], weight_ref[:, cols], preferred_element_type=F32
            )
            if extra_refs:
                value = value + extra_refs[r][:, cols].astype(F32)
            part_ref[:, cols] = value.astype(part_ref.dtype)


def project_kernel(hid_ref, weight_ref, *refs, extra):
    times_columns(hid_ref, weight_ref, refs[extra:], refs[:extra])


def project(hidden, weight, pieces, extra=(), dtype=BF16):
    rows, channels = hidden.shape
    width = weight.shape[1]
    return pl.pallas_call(
        functools.partial(project_kernel, extra=len(extra)),
        out_shape=[jax.ShapeDtypeStruct((rows // pieces, width), dtype)] * pieces,
        in_specs=[VMEM] * (2 + len(extra)),
        out_specs=[VMEM] * pieces,
        compiler_params=params(2 * channels * width + 2 * rows * channels + 10 * rows * width),
        cost_estimate=pl.CostEstimate(
            flops=2 * rows * channels * width, bytes_accessed=2 * channels * width, transcendentals=0
        ),
    )(hidden, weight, *extra)


def start_projection(idx, gate_q, skip, weight, blocks, pieces):
    count = len(blocks)
    rows, channels = gate_q.shape
    width = channels // count
    if width % 128:
        conv = jnp.zeros((rows, channels), F32)
        for s in range(count):
            src = lax.rem(idx[0] + count - s, count)
            conv = lax.dynamic_update_slice_in_dim(conv, blocks[s].astype(F32), src * width, 1)
        hidden = (gate_q.astype(F32) * (conv + skip)).astype(BF16)
        return hidden, project(hidden, weight, pieces)
    columns = weight.shape[1]
    hidden, *parts = pl.pallas_call(
        functools.partial(hidden_kernel, count=count),
        out_shape=[jax.ShapeDtypeStruct((rows, channels), BF16)]
        + [jax.ShapeDtypeStruct((rows // pieces, columns), BF16)] * pieces,
        in_specs=[SMEM] + [VMEM] * (3 + count),
        out_specs=[VMEM] * (1 + pieces),
        compiler_params=params(2 * channels * columns + 10 * rows * channels + 2 * rows * columns),
        cost_estimate=pl.CostEstimate(
            flops=2 * rows * channels * columns, bytes_accessed=2 * channels * columns, transcendentals=0
        ),
    )(idx, gate_q, skip, weight, *blocks)
    return hidden, parts


def finish_kernel(*refs, at, terms):
    values, (out_ref, held, sem) = refs[:terms], refs[-3:]
    total = values[0][...]
    for value in values[1:]:
        total = total + value[...].astype(F32)
    held[...] = total.astype(BF16)
    rows = held.shape[0]
    copy = pltpu.make_async_copy(held, out_ref.at[pl.ds(at, rows), :], sem)
    copy.start()
    copy.wait()


def finish(values, at, rows, buffer):
    here, columns = values[0].shape
    aliased = [] if buffer is None else [buffer]
    return pl.pallas_call(
        functools.partial(finish_kernel, at=at, terms=len(values)),
        out_shape=jax.ShapeDtypeStruct((rows, columns), BF16),
        in_specs=[VMEM] * len(values) + [HBM] * len(aliased),
        out_specs=HBM,
        scratch_shapes=[pltpu.VMEM((here, columns), BF16), pltpu.SemaphoreType.DMA],
        input_output_aliases={len(values): 0} if aliased else {},
        compiler_params=params(2 * here * columns * (len(values) + 2)),
    )(*values, *aliased)


def local(gate_q, key_k, value_v, long_filter, skip_gain, out_weight):
    rows, channels = key_k.shape
    count = lax.axis_size("ctx")
    groups = lax.axis_size("ch")
    chips = groups // 2
    total = rows * count
    inner = next(n for n in range(128, 0, -16) if rows % n == 0)
    outer = total // inner
    width = channels // count
    lanes = -(-width // 128) * 128
    idx = lax.axis_index("ctx").astype(jnp.int32).reshape(1)
    first, mid, back, last = tables(total, inner)
    spot = pltpu.VMEM((outer, inner, width), BF16)
    mixed = pltpu.VMEM((outer, 2, inner, width), BF16)
    signal = 2 * total * lanes
    table = 2 * (first.size + mid.size)

    filter_in = exchange(send_slices(idx, [long_filter], count), "ctx", count)
    gated_in = exchange(send_slices(idx, [key_k, value_v], count), "ctx", count)
    here = lax.axis_index("ch").astype(jnp.int32)
    chip, core = here // 2, here % 2
    steps = list(range(1, chips)) + [0]
    order = [lax.rem(chip + step, chips) * 2 + which for step in steps for which in (1 - core, core)]
    skip, *weights = prepare(jnp.stack(order), key_k, value_v, skip_gain[None, :], out_weight)
    spectrum = pl.pallas_call(
        functools.partial(filter_kernel, count=count),
        out_shape=jax.ShapeDtypeStruct((outer, 2 * inner, width), BF16),
        in_specs=[SMEM] + [VMEM] * (2 + count),
        out_specs=VMEM,
        scratch_shapes=[spot, mixed],
        compiler_params=params(table + 6 * signal),
        cost_estimate=pl.CostEstimate(flops=3 * 10**9, bytes_accessed=8 * 10**6, transcendentals=0),
    )(idx, first, mid, *filter_in)
    spectrum, skip, *weights = lax.optimization_barrier((spectrum, skip, *weights))
    conv_out = pl.pallas_call(
        functools.partial(conv_kernel, count=count),
        out_shape=[jax.ShapeDtypeStruct((rows, width), BF16)] * count,
        in_specs=[SMEM] + [VMEM] * (5 + count),
        out_specs=[VMEM] * count,
        scratch_shapes=[spot, mixed],
        compiler_params=params(2 * table + 7 * signal),
        cost_estimate=pl.CostEstimate(flops=6 * 10**9, bytes_accessed=12 * 10**6, transcendentals=0),
    )(idx, first, mid, back, last, spectrum, *gated_in)
    conv_in = exchange(conv_out, "ctx", count)

    swap = [(i, i ^ 1) for i in range(groups)]
    pieces = 2

    def to_core(parts):
        return [lax.ppermute(part, "ch", swap) for part in parts]

    hidden, parts = start_projection(idx, gate_q, skip, weights[0], conv_in, pieces)
    arrived = []
    for at, step in enumerate(steps[:-1]):
        if at:
            parts = project(hidden, weights[2 * at], pieces)
        crossed = to_core(parts)
        own = project(hidden, weights[2 * at + 1], pieces, dtype=F32)
        perm = [(i, (i + 2 * step) % groups) for i in range(groups)]
        arrived.append(
            [
                lax.ppermute((a + b.astype(F32)).astype(BF16), "ch", perm)
                for a, b in zip(own, crossed)
            ]
        )
    crossed = to_core(project(hidden, weights[-2], pieces))
    own = project(hidden, weights[-1], pieces, crossed, F32)
    result = None
    for r in range(pieces):
        result = finish([own[r]] + [parts[r] for parts in arrived], r * (rows // pieces), rows, result)
    return result


def solution(mesh):
    placed = (
        P("ctx", "ch"),
        P("ctx", "ch"),
        P("ctx", "ch"),
        P("ctx", "ch"),
        P("ch"),
        P("ch", None),
    )
    return jax.shard_map(
        local, mesh=mesh, in_specs=placed, out_specs=P("ctx", "ch"), check_vma=False
    )
```

time: 126 us -> 92.9 us (0.74)
  Pallas kernels: 49.8 us -> 17.6 us
  starting transfers between devices: 41.2 us -> 47.7 us
  waiting for transfers between devices: 27.7 us -> 23.2 us
  other arithmetic: 2.54 us -> 0.24 us
    pallas_call x1, Pallas kernels: 17.9 us -> 3.05 us  [local(): pl.pallas_call(functools.partial(conv_kernel, count=count), out_shape=[ja...]
    pallas_call x7 -> x9, Pallas kernels: 22.2 us -> 13 us  [the longest x1 4.34 us: prepare(): pl.pallas_call(prepare_kernel, out_shape=[jax.ShapeDtypeStruct(key_k.shap...]
    pallas_call x1, Pallas kernels: 9.66 us -> 1.53 us  [local(): pl.pallas_call(functools.partial(filter_kernel, count=count), out_shape=j...]
    ppermute x21, waiting for transfers between devices: 13 us -> 7.73 us  [exchange(): lax.ppermute(blocks[s], axis, [(i, (i + s) % count) for i in range(count)])]
    ppermute x21, starting transfers between devices: 40.2 us -> 44.4 us  [exchange(): lax.ppermute(blocks[s], axis, [(i, (i + s) % count) for i in range(count)])]
    convert_element_type x1 -> x2, other arithmetic: 2.54 us -> 0.17 us  [local(): (a + b.astype(F32)).astype(BF16)]
    ppermute x3 -> x6, starting transfers between devices: 0.99 us -> 3.3 us  [the longest x2 2.16 us: local(): lax.ppermute((a + b.astype(F32)).astype(BF16), 'ch', perm)]
    ppermute x3 -> x6, waiting for transfers between devices: 14.6 us -> 15.5 us  [the longest x2 15.5 us: local(): lax.ppermute((a + b.astype(F32)).astype(BF16), 'ch', perm)]
  transfers between devices with their start and end apart: 24 -> 27, of which waited for: 4 -> 7; matrix products, arithmetic and copies ran while one was open for 0% -> 0% of each run, Pallas kernels for 18% -> 11%
where the time goes in v2:
time: 92.9 us; the launch traced here: 91.3 us
  starting transfers between devices  47.7 us (51%)
  waiting for transfers between devices  23.2 us (25%)
  Pallas kernels  17.6 us (19%)
  local copies, waits for them, and re-layouts  2.3 us (2%)
    ppermute x21, starting transfers between devices, exchange(): lax.ppermute(blocks[s], axis, [(i, (i + s) % count) for i in range(count)])  44.4 us
    ppermute x2, waiting for transfers between devices, local(): lax.ppermute((a + b.astype(F32)).astype(BF16), 'ch', perm)  15.5 us
    ppermute x21, waiting for transfers between devices, exchange(): lax.ppermute(blocks[s], axis, [(i, (i + s) % count) for i in range(count)])  7.73 us
    pallas_call x1, Pallas kernels, prepare(): pl.pallas_call(prepare_kernel, out_shape=[jax.ShapeDtypeStruct(key_k.shap...  4.34 us
    pallas_call x1, Pallas kernels, local(): pl.pallas_call(functools.partial(conv_kernel, count=count), out_shape=[ja...  3.05 us
    pallas_call x3, Pallas kernels, project(): pl.pallas_call(functools.partial(project_kernel, extra=len(extra)), out_s...  2.98 us
    pallas_call x2, Pallas kernels, send_slices(): pl.pallas_call(functools.partial(split_kernel if alone else gate_kernel,...  2.42 us
    unnamed x20, local copies, waits for them, and re-layouts  2.3 us
  transfers between devices with their start and end apart: 27, of which 7 were waited for; matrix products, arithmetic and copies ran while one was open for 0% of the time, Pallas kernels for 11%

profile of v2, /device:TPU:20, one launch (start us, length us, event | category | flops | bytes accessed | tf_op | source)
XLA Modules:
  0.0 91.3 jit_solution(13033887870202943031)
XLA Ops:
  0.0 2.0 %shard_map.100 = (bf16[384,128]{1,0:T(8,128)(2,1)S(1)}, bf16[384,128]{1,0:T(8,128)(2,1)}, bf16[384,128]{1,0:T(8,128)(2,1)S(1)}, bf16[384,128]{1,0:T(8,128)(2,1)S...) custom-call(s32[1]{0:T(128)} %bitcast.idx_ref, ...), custom_call_target="tpu_custom_call" | custom-call | flops 393216 | bytes 1572864 | tf_op jit(solution)/shard_map/pallas_call | solution.py:77
  2.0 1.5 %collective-permute-start = (bf16[384,128]{1,0:T(8,128)(2,1)}, bf16[384,128]{1,0:T(8,128)(2,1)S(1)}, u32[]{:S(2)}, u32[]{:S(2)}) collective-permute-start(bf16[384,128]{1,0:T(8,128)(2,1)} %get-tuple-element.50), channel_id=1, source_target_pairs={{0,4},{4,8},{8,12},{12,16},{16,20},{20,24},{24,28},{28,0},{1,5},{5... | collective-permute-start | bytes 294920 | tf_op jit(solution)/shard_map/ppermute | solution.py:91
  3.6 1.6 %collective-permute-start.1 = (bf16[384,128]{1,0:T(8,128)(2,1)S(1)}, bf16[384,128]{1,0:T(8,128)(2,1)S(1)}, u32[]{:S(2)}, u32[]{:S(2)}) collective-permute-start(bf16[384,128]{1,0:T(8,128)(2,1)S(1)} %get-tuple-element.51), channel_id=1, source_target_pairs={{0,8},{4,12},{8,16},{12,20},{16,24},{20,28},{24,0},{28,4},{1,9},{5... | collective-permute-start | bytes 294920 | tf_op jit(solution)/shard_map/ppermute | solution.py:91
  6.3 1.7 %collective-permute-start.3 = (bf16[384,128]{1,0:T(8,128)(2,1)S(1)}, bf16[384,128]{1,0:T(8,128)(2,1)S(1)}, u32[]{:S(2)}, u32[]{:S(2)}) collective-permute-start(bf16[384,128]{1,0:T(8,128)(2,1)S(1)} %get-tuple-element.53), channel_id=1, source_target_pairs={{0,16},{4,20},{8,24},{12,28},{16,0},{20,4},{24,8},{28,12},{1,17},{... | collective-permute-start | bytes 294920 | tf_op jit(solution)/shard_map/ppermute | solution.py:91
  12.0 1.4 %collective-permute-start.5 = (bf16[384,128]{1,0:T(8,128)(2,1)S(1)}, bf16[384,128]{1,0:T(8,128)(2,1)S(1)}, u32[]{:S(2)}, u32[]{:S(2)}) collective-permute-start(bf16[384,128]{1,0:T(8,128)(2,1)S(1)} %get-tuple-element.55), channel_id=1, source_target_pairs={{0,24},{4,28},{8,0},{12,4},{16,8},{20,12},{24,16},{28,20},{1,25},{... | collective-permute-start | bytes 294920 | tf_op jit(solution)/shard_map/ppermute | solution.py:91
  13.4 4.9 %collective-permute-start.6 = (bf16[384,128]{1,0:T(8,128)(2,1)S(1)}, bf16[384,128]{1,0:T(8,128)(2,1)S(1)}, u32[]{:S(2)}, u32[]{:S(2)}) collective-permute-start(bf16[384,128]{1,0:T(8,128)(2,1)S(1)} %get-tuple-element.56), channel_id=1, source_target_pairs={{0,28},{4,0},{8,4},{12,8},{16,12},{20,16},{24,20},{28,24},{1,29},{... | collective-permute-start | bytes 294920 | tf_op jit(solution)/shard_map/ppermute | solution.py:91
  19.6 3.4 %collective-permute-start.8 = (bf16[384,128]{1,0:T(8,128)(2,1)S(1)}, bf16[384,128]{1,0:T(8,128)(2,1)S(1)}, u32[]{:S(2)}, u32[]{:S(2)}) collective-permute-start(bf16[384,128]{1,0:T(8,128)(2,1)S(1)} %get-tuple-element.67), channel_id=1, source_target_pairs={{0,8},{4,12},{8,16},{12,20},{16,24},{20,28},{24,0},{28,4},{1,9},{5... | collective-permute-start | bytes 294920 | tf_op jit(solution)/shard_map/ppermute | solution.py:91
  23.1 4.3 %shard_map.102 = (f32[384,1024]{1,0:T(8,128)S(1)}, bf16[1024,1024]{1,0:T(8,128)(2,1)S(1)}, bf16[1024,1024]{1,0:T(8,128)(2,1)S(1)}, bf16[1024,1024]{1,0:T(8,128)(2,1)S(1)}, bf16[1024,1024]{1,0:T(8,128)(2,1)S(1)}) custom-call(s32[4]{0:T(128)S(1)} %pad_add_fusion.order_ref, bf16[384,1024]{1,0:T(8,128)(2,1)S(1)} %copy-done.1, bf16[384,1024]{1,0:T(8,128)(2,1)S(1)} %copy-done.3, ...), custom_call_target="tpu_custom_call" | custom-call | flops 393216 | bytes 8388608 | tf_op jit(solution)/shard_map/pallas_call | solution.py:196
  27.4 2.2 %collective-permute-start.9 = (bf16[384,128]{1,0:T(8,128)(2,1)S(1)}, bf16[384,128]{1,0:T(8,128)(2,1)S(1)}, u32[]{:S(2)}, u32[]{:S(2)}) collective-permute-start(bf16[384,128]{1,0:T(8,128)(2,1)S(1)} %get-tuple-element.68), channel_id=1, source_target_pairs={{0,12},{4,16},{8,20},{12,24},{16,28},{20,0},{24,4},{28,8},{1,13},{... | collective-permute-start | bytes 294920 | tf_op jit(solution)/shard_map/ppermute | solution.py:91
  29.6 2.3 %collective-permute-start.10 = (bf16[384,128]{1,0:T(8,128)(2,1)S(1)}, bf16[384,128]{1,0:T(8,128)(2,1)S(1)}, u32[]{:S(2)}, u32[]{:S(2)}) collective-permute-start(bf16[384,128]{1,0:T(8,128)(2,1)S(1)} %get-tuple-element.69), channel_id=1, source_target_pairs={{0,16},{4,20},{8,24},{12,28},{16,0},{20,4},{24,8},{28,12},{1,17},{... | collective-permute-start | bytes 294920 | tf_op jit(solution)/shard_map/ppermute | solution.py:91
  33.4 3.5 %collective-permute-start.13 = (bf16[384,128]{1,0:T(8,128)(2,1)S(1)}, bf16[384,128]{1,0:T(8,128)(2,1)S(1)}, u32[]{:S(2)}, u32[]{:S(2)}) collective-permute-start(bf16[384,128]{1,0:T(8,128)(2,1)S(1)} %get-tuple-element.72), channel_id=1, source_target_pairs={{0,28},{4,0},{8,4},{12,8},{16,12},{20,16},{24,20},{28,24},{1,29},{... | collective-permute-start | bytes 294920 | tf_op jit(solution)/shard_map/ppermute | solution.py:91
  36.9 1.5 %shard_map.101.filt_ref = bf16[24,256,128]{2,1,0:T(8,128)(2,1)S(1)} custom-call(s32[1]{0:T(128)} %bitcast.idx_ref, bf16[384,192]{1,0:T(8,128)(2,1)S(1)} %copy-done.8, bf16[24,256,256]{2,1,0:T(8,128)(2,1)S(1)} %copy-done.6, bf16[384,128]{1,0:T(8,128)(2,1)S(1)} %get-tuple-element.49.refs_0_, bf16[384,128]{1,0:T(8,128)(2,1)S(1)} %collective-permute-done.refs_1_, ...), custom_call_target="tpu_custom_call" | custom-call | flops 3000000000 | bytes 8000000 | tf_op jit(solution)/shard_map/pallas_call | solution.py:329
  39.5 2.0 %collective-permute-done.12.refs_6_ = bf16[384,128]{1,0:T(8,128)(2,1)S(1)} collective-permute-done((bf16[384,128]{1,0:T(8,128)(2,1)S(1)}, bf16[384,128]{1,0:T(8,128)(2,1)S(1)}, u32[]{:S(2)}, u32[]{:S(2)}) %collective-permute-start.12) | collective-permute-done | bytes 98336 | tf_op jit(solution)/shard_map/ppermute | solution.py:91
  42.6 3.1 %shard_map.104 = (bf16[384,128]{1,0:T(8,128)(2,1)S(1)}, bf16[384,128]{1,0:T(8,128)(2,1)S(1)}, bf16[384,128]{1,0:T(8,128)(2,1)S(1)}, bf16[384,128]{1,0:T(8,128)(2...) custom-call(s32[1]{0:T(128)} %bitcast.idx_ref, ...), custom_call_target="tpu_custom_call" | custom-call | flops 6000000000 | bytes 12000000 | tf_op jit(solution)/shard_map/pallas_call | solution.py:339
  46.0 4.4 %collective-permute-start.15 = (bf16[384,128]{1,0:T(8,128)(2,1)S(1)}, bf16[384,128]{1,0:T(8,128)(2,1)S(1)}, u32[]{:S(2)}, u32[]{:S(2)}) collective-permute-start(bf16[384,128]{1,0:T(8,128)(2,1)S(1)} %get-tuple-element.75), channel_id=1, source_target_pairs={{0,8},{4,12},{8,16},{12,20},{16,24},{20,28},{24,0},{28,4},{1,9},{5... | collective-permute-start | bytes 294920 | tf_op jit(solution)/shard_map/ppermute | solution.py:91
  51.0 1.3 %collective-permute-start.17 = (bf16[384,128]{1,0:T(8,128)(2,1)S(1)}, bf16[384,128]{1,0:T(8,128)(2,1)S(1)}, u32[]{:S(2)}, u32[]{:S(2)}) collective-permute-start(bf16[384,128]{1,0:T(8,128)(2,1)S(1)} %get-tuple-element.77), channel_id=1, source_target_pairs={{0,16},{4,20},{8,24},{12,28},{16,0},{20,4},{24,8},{28,12},{1,17},{... | collective-permute-start | bytes 294920 | tf_op jit(solution)/shard_map/ppermute | solution.py:91
  52.2 2.7 %collective-permute-start.18 = (bf16[384,128]{1,0:T(8,128)(2,1)S(1)}, bf16[384,128]{1,0:T(8,128)(2,1)S(1)}, u32[]{:S(2)}, u32[]{:S(2)}) collective-permute-start(bf16[384,128]{1,0:T(8,128)(2,1)S(1)} %get-tuple-element.78), channel_id=1, source_target_pairs={{0,20},{4,24},{8,28},{12,0},{16,4},{20,8},{24,12},{28,16},{1,21},{... | collective-permute-start | bytes 294920 | tf_op jit(solution)/shard_map/ppermute | solution.py:91
  55.7 6.7 %collective-permute-start.20 = (bf16[384,128]{1,0:T(8,128)(2,1)S(1)}, bf16[384,128]{1,0:T(8,128)(2,1)S(1)}, u32[]{:S(2)}, u32[]{:S(2)}) collective-permute-start(bf16[384,128]{1,0:T(8,128)(2,1)S(1)} %get-tuple-element.80), channel_id=1, source_target_pairs={{0,28},{4,0},{8,4},{12,8},{16,12},{20,16},{24,20},{28,24},{1,29},{... | collective-permute-start | bytes 294920 | tf_op jit(solution)/shard_map/ppermute | solution.py:91
  62.4 1.5 %collective-permute-done.19.refs_6_ = bf16[384,128]{1,0:T(8,128)(2,1)S(1)} collective-permute-done((bf16[384,128]{1,0:T(8,128)(2,1)S(1)}, bf16[384,128]{1,0:T(8,128)(2,1)S(1)}, u32[]{:S(2)}, u32[]{:S(2)}) %collective-permute-start.19) | collective-permute-done | bytes 98336 | tf_op jit(solution)/shard_map/ppermute | solution.py:91
  63.9 2.1 %collective-permute-done.20.refs_7_ = bf16[384,128]{1,0:T(8,128)(2,1)S(1)} collective-permute-done((bf16[384,128]{1,0:T(8,128)(2,1)S(1)}, bf16[384,128]{1,0:T(8,128)(2,1)S(1)}, u32[]{:S(2)}, u32[]{:S(2)}) %collective-permute-start.20) | collective-permute-done | bytes 98336 | tf_op jit(solution)/shard_map/ppermute | solution.py:91
  66.0 1.6 %shard_map.105 = (bf16[384,1024]{1,0:T(8,128)(2,1)S(1)}, bf16[192,1024]{1,0:T(8,128)(2,1)S(1)}, bf16[192,1024]{1,0:T(8,128)(2,1)S(1)}) custom-call(s32[1]{0:T(128)} %bitcast.idx_ref, bf16[384,1024]{1,0:T(8,128)(2,1)S(1)} %copy-done.4, f32[384,1024]{1,0:T(8,128)S(1)} %get-tuple-element.62.skip_ref, bf16[1024,1024]{1,0:T(8,128)(2,1)S(1)} %get-tuple-element.63.weight_ref, ...), custom_call_target="tpu_custom_call" | custom-call | flops 805306368 | bytes 2097152 | tf_op jit(solution)/shard_map/pallas_call | solution.py:265
  71.5 1.6 %collective-permute-start.24 = (bf16[192,1024]{1,0:T(8,128)(2,1)S(1)}, bf16[192,1024]{1,0:T(8,128)(2,1)S(1)}, u32[]{:S(2)}, u32[]{:S(2)}) collective-permute-start(bf16[192,1024]{1,0:T(8,128)(2,1)S(1)} %add_convert_fusion.1), channel_id=1, source_target_pairs={{0,2},{1,3},{2,0},{3,1},{4,6},{5,7},{6,4},{7,5},{8,10},{9,11},{10,... | collective-permute-start | bytes 1179656 | tf_op jit(solution)/shard_map/ppermute | solution.py:366
  74.1 8.8 %collective-permute-done.26.refs_1_ = bf16[192,1024]{1,0:T(8,128)(2,1)S(1)} collective-permute-done((bf16[192,1024]{1,0:T(8,128)(2,1)S(1)}, bf16[192,1024]{1,0:T(8,128)(2,1)S(1)}, u32[]{:S(2)}, u32[]{:S(2)}) %collective-permute-start.26) | collective-permute-done | bytes 393248 | tf_op jit(solution)/shard_map/ppermute | solution.py:366
  83.7 6.7 %collective-permute-done.24.refs_1_ = bf16[192,1024]{1,0:T(8,128)(2,1)S(1)} collective-permute-done((bf16[192,1024]{1,0:T(8,128)(2,1)S(1)}, bf16[192,1024]{1,0:T(8,128)(2,1)S(1)}, u32[]{:S(2)}, u32[]{:S(2)}) %collective-permute-start.24) | collective-permute-done | bytes 393248 | tf_op jit(solution)/shard_map/ppermute | solution.py:366
  (64 shorter events, 18.4 us)
Async XLA Ops:
  2.0 10.0 %collective-permute-start = (bf16[384,128]{1,0:T(8,128)(2,1)}, bf16[384,128]{1,0:T(8,128)(2,1)S(1)}, u32[]{:S(2)}, u32[]{:S(2)}) collective-permute-start(bf16[384,128]{1,0:T(8,128)(2,1)} %get-tuple-element.50), channel_id=1, source_target_pairs={{0,4},{4,8},{8,12},{12,16},{16,20},{20,24},{24,28},{28,0},{1,5},{5... | collective-permute-start | bytes 294920 | tf_op jit(solution)/shard_map/ppermute | solution.py:91
  3.6 9.9 %collective-permute-start.1 = (bf16[384,128]{1,0:T(8,128)(2,1)S(1)}, bf16[384,128]{1,0:T(8,128)(2,1)S(1)}, u32[]{:S(2)}, u32[]{:S(2)}) collective-permute-start(bf16[384,128]{1,0:T(8,128)(2,1)S(1)} %get-tuple-element.51), channel_id=1, source_target_pairs={{0,8},{4,12},{8,16},{12,20},{16,24},{20,28},{24,0},{28,4},{1,9},{5... | collective-permute-start | bytes 294920 | tf_op jit(solution)/shard_map/ppermute | solution.py:91
  5.1 13.2 %collective-permute-start.2 = (bf16[384,128]{1,0:T(8,128)(2,1)S(1)}, bf16[384,128]{1,0:T(8,128)(2,1)S(1)}, u32[]{:S(2)}, u32[]{:S(2)}) collective-permute-start(bf16[384,128]{1,0:T(8,128)(2,1)S(1)} %get-tuple-element.52), channel_id=1, source_target_pairs={{0,12},{4,16},{8,20},{12,24},{16,28},{20,0},{24,4},{28,8},{1,13},{... | collective-permute-start | bytes 294920 | tf_op jit(solution)/shard_map/ppermute | solution.py:91
  6.3 13.2 %collective-permute-start.3 = (bf16[384,128]{1,0:T(8,128)(2,1)S(1)}, bf16[384,128]{1,0:T(8,128)(2,1)S(1)}, u32[]{:S(2)}, u32[]{:S(2)}) collective-permute-start(bf16[384,128]{1,0:T(8,128)(2,1)S(1)} %get-tuple-element.53), channel_id=1, source_target_pairs={{0,16},{4,20},{8,24},{12,28},{16,0},{20,4},{24,8},{28,12},{1,17},{... | collective-permute-start | bytes 294920 | tf_op jit(solution)/shard_map/ppermute | solution.py:91
  8.0 19.4 %collective-permute-start.4 = (bf16[384,128]{1,0:T(8,128)(2,1)S(1)}, bf16[384,128]{1,0:T(8,128)(2,1)S(1)}, u32[]{:S(2)}, u32[]{:S(2)}) collective-permute-start(bf16[384,128]{1,0:T(8,128)(2,1)S(1)} %get-tuple-element.54), channel_id=1, source_target_pairs={{0,20},{4,24},{8,28},{12,0},{16,4},{20,8},{24,12},{28,16},{1,21},{... | collective-permute-start | bytes 294920 | tf_op jit(solution)/shard_map/ppermute | solution.py:91
  12.0 17.6 %collective-permute-start.5 = (bf16[384,128]{1,0:T(8,128)(2,1)S(1)}, bf16[384,128]{1,0:T(8,128)(2,1)S(1)}, u32[]{:S(2)}, u32[]{:S(2)}) collective-permute-start(bf16[384,128]{1,0:T(8,128)(2,1)S(1)} %get-tuple-element.55), channel_id=1, source_target_pairs={{0,24},{4,28},{8,0},{12,4},{16,8},{20,12},{24,16},{28,20},{1,25},{... | collective-permute-start | bytes 294920 | tf_op jit(solution)/shard_map/ppermute | solution.py:91
  13.4 18.4 %collective-permute-start.6 = (bf16[384,128]{1,0:T(8,128)(2,1)S(1)}, bf16[384,128]{1,0:T(8,128)(2,1)S(1)}, u32[]{:S(2)}, u32[]{:S(2)}) collective-permute-start(bf16[384,128]{1,0:T(8,128)(2,1)S(1)} %get-tuple-element.56), channel_id=1, source_target_pairs={{0,28},{4,0},{8,4},{12,8},{16,12},{20,16},{24,20},{28,24},{1,29},{... | collective-permute-start | bytes 294920 | tf_op jit(solution)/shard_map/ppermute | solution.py:91
  18.3 14.3 %collective-permute-start.7 = (bf16[384,128]{1,0:T(8,128)(2,1)S(1)}, bf16[384,128]{1,0:T(8,128)(2,1)S(1)}, u32[]{:S(2)}, u32[]{:S(2)}) collective-permute-start(bf16[384,128]{1,0:T(8,128)(2,1)S(1)} %get-tuple-element.66), channel_id=1, source_target_pairs={{0,4},{4,8},{8,12},{12,16},{16,20},{20,24},{24,28},{28,0},{1,5},{5... | collective-permute-start | bytes 294920 | tf_op jit(solution)/shard_map/ppermute | solution.py:91
  19.6 13.8 %collective-permute-start.8 = (bf16[384,128]{1,0:T(8,128)(2,1)S(1)}, bf16[384,128]{1,0:T(8,128)(2,1)S(1)}, u32[]{:S(2)}, u32[]{:S(2)}) collective-permute-start(bf16[384,128]{1,0:T(8,128)(2,1)S(1)} %get-tuple-element.67), channel_id=1, source_target_pairs={{0,8},{4,12},{8,16},{12,20},{16,24},{20,28},{24,0},{28,4},{1,9},{5... | collective-permute-start | bytes 294920 | tf_op jit(solution)/shard_map/ppermute | solution.py:91
  27.4 11.0 %collective-permute-start.9 = (bf16[384,128]{1,0:T(8,128)(2,1)S(1)}, bf16[384,128]{1,0:T(8,128)(2,1)S(1)}, u32[]{:S(2)}, u32[]{:S(2)}) collective-permute-start(bf16[384,128]{1,0:T(8,128)(2,1)S(1)} %get-tuple-element.68), channel_id=1, source_target_pairs={{0,12},{4,16},{8,20},{12,24},{16,28},{20,0},{24,4},{28,8},{1,13},{... | collective-permute-start | bytes 294920 | tf_op jit(solution)/shard_map/ppermute | solution.py:91
  29.6 8.9 %collective-permute-start.10 = (bf16[384,128]{1,0:T(8,128)(2,1)S(1)}, bf16[384,128]{1,0:T(8,128)(2,1)S(1)}, u32[]{:S(2)}, u32[]{:S(2)}) collective-permute-start(bf16[384,128]{1,0:T(8,128)(2,1)S(1)} %get-tuple-element.69), channel_id=1, source_target_pairs={{0,16},{4,20},{8,24},{12,28},{16,0},{20,4},{24,8},{28,12},{1,17},{... | collective-permute-start | bytes 294920 | tf_op jit(solution)/shard_map/ppermute | solution.py:91
  31.9 7.7 %collective-permute-start.11 = (bf16[384,128]{1,0:T(8,128)(2,1)S(1)}, bf16[384,128]{1,0:T(8,128)(2,1)S(1)}, u32[]{:S(2)}, u32[]{:S(2)}) collective-permute-start(bf16[384,128]{1,0:T(8,128)(2,1)S(1)} %get-tuple-element.70), channel_id=1, source_target_pairs={{0,20},{4,24},{8,28},{12,0},{16,4},{20,8},{24,12},{28,16},{1,21},{... | collective-permute-start | bytes 294920 | tf_op jit(solution)/shard_map/ppermute | solution.py:91
  32.6 8.9 %collective-permute-start.12 = (bf16[384,128]{1,0:T(8,128)(2,1)S(1)}, bf16[384,128]{1,0:T(8,128)(2,1)S(1)}, u32[]{:S(2)}, u32[]{:S(2)}) collective-permute-start(bf16[384,128]{1,0:T(8,128)(2,1)S(1)} %get-tuple-element.71), channel_id=1, source_target_pairs={{0,24},{4,28},{8,0},{12,4},{16,8},{20,12},{24,16},{28,20},{1,25},{... | collective-permute-start | bytes 294920 | tf_op jit(solution)/shard_map/ppermute | solution.py:91
  33.4 9.1 %collective-permute-start.13 = (bf16[384,128]{1,0:T(8,128)(2,1)S(1)}, bf16[384,128]{1,0:T(8,128)(2,1)S(1)}, u32[]{:S(2)}, u32[]{:S(2)}) collective-permute-start(bf16[384,128]{1,0:T(8,128)(2,1)S(1)} %get-tuple-element.72), channel_id=1, source_target_pairs={{0,28},{4,0},{8,4},{12,8},{16,12},{20,16},{24,20},{28,24},{1,29},{... | collective-permute-start | bytes 294920 | tf_op jit(solution)/shard_map/ppermute | solution.py:91
  45.6 9.3 %collective-permute-start.14 = (bf16[384,128]{1,0:T(8,128)(2,1)S(1)}, bf16[384,128]{1,0:T(8,128)(2,1)S(1)}, u32[]{:S(2)}, u32[]{:S(2)}) collective-permute-start(bf16[384,128]{1,0:T(8,128)(2,1)S(1)} %get-tuple-element.74), channel_id=1, source_target_pairs={{0,4},{4,8},{8,12},{12,16},{16,20},{20,24},{24,28},{28,0},{1,5},{5... | collective-permute-start | bytes 294920 | tf_op jit(solution)/shard_map/ppermute | solution.py:91
  46.0 9.7 %collective-permute-start.15 = (bf16[384,128]{1,0:T(8,128)(2,1)S(1)}, bf16[384,128]{1,0:T(8,128)(2,1)S(1)}, u32[]{:S(2)}, u32[]{:S(2)}) collective-permute-start(bf16[384,128]{1,0:T(8,128)(2,1)S(1)} %get-tuple-element.75), channel_id=1, source_target_pairs={{0,8},{4,12},{8,16},{12,20},{16,24},{20,28},{24,0},{28,4},{1,9},{5... | collective-permute-start | bytes 294920 | tf_op jit(solution)/shard_map/ppermute | solution.py:91
  50.4 12.0 %collective-permute-start.16 = (bf16[384,128]{1,0:T(8,128)(2,1)S(1)}, bf16[384,128]{1,0:T(8,128)(2,1)S(1)}, u32[]{:S(2)}, u32[]{:S(2)}) collective-permute-start(bf16[384,128]{1,0:T(8,128)(2,1)S(1)} %get-tuple-element.76), channel_id=1, source_target_pairs={{0,12},{4,16},{8,20},{12,24},{16,28},{20,0},{24,4},{28,8},{1,13},{... | collective-permute-start | bytes 294920 | tf_op jit(solution)/shard_map/ppermute | solution.py:91
  51.0 11.4 %collective-permute-start.17 = (bf16[384,128]{1,0:T(8,128)(2,1)S(1)}, bf16[384,128]{1,0:T(8,128)(2,1)S(1)}, u32[]{:S(2)}, u32[]{:S(2)}) collective-permute-start(bf16[384,128]{1,0:T(8,128)(2,1)S(1)} %get-tuple-element.77), channel_id=1, source_target_pairs={{0,16},{4,20},{8,24},{12,28},{16,0},{20,4},{24,8},{28,12},{1,17},{... | collective-permute-start | bytes 294920 | tf_op jit(solution)/shard_map/ppermute | solution.py:91
  52.2 10.1 %collective-permute-start.18 = (bf16[384,128]{1,0:T(8,128)(2,1)S(1)}, bf16[384,128]{1,0:T(8,128)(2,1)S(1)}, u32[]{:S(2)}, u32[]{:S(2)}) collective-permute-start(bf16[384,128]{1,0:T(8,128)(2,1)S(1)} %get-tuple-element.78), channel_id=1, source_target_pairs={{0,20},{4,24},{8,28},{12,0},{16,4},{20,8},{24,12},{28,16},{1,21},{... | collective-permute-start | bytes 294920 | tf_op jit(solution)/shard_map/ppermute | solution.py:91
  54.9 8.9 %collective-permute-start.19 = (bf16[384,128]{1,0:T(8,128)(2,1)S(1)}, bf16[384,128]{1,0:T(8,128)(2,1)S(1)}, u32[]{:S(2)}, u32[]{:S(2)}) collective-permute-start(bf16[384,128]{1,0:T(8,128)(2,1)S(1)} %get-tuple-element.79), channel_id=1, source_target_pairs={{0,24},{4,28},{8,0},{12,4},{16,8},{20,12},{24,16},{28,20},{1,25},{... | collective-permute-start | bytes 294920 | tf_op jit(solution)/shard_map/ppermute | solution.py:91
  55.7 10.3 %collective-permute-start.20 = (bf16[384,128]{1,0:T(8,128)(2,1)S(1)}, bf16[384,128]{1,0:T(8,128)(2,1)S(1)}, u32[]{:S(2)}, u32[]{:S(2)}) collective-permute-start(bf16[384,128]{1,0:T(8,128)(2,1)S(1)} %get-tuple-element.80), channel_id=1, source_target_pairs={{0,28},{4,0},{8,4},{12,8},{16,12},{20,16},{24,20},{28,24},{1,29},{... | collective-permute-start | bytes 294920 | tf_op jit(solution)/shard_map/ppermute | solution.py:91
  69.2 3.9 %collective-permute-start.21 = (bf16[192,1024]{1,0:T(8,128)(2,1)S(1)}, bf16[192,1024]{1,0:T(8,128)(2,1)S(1)}, u32[]{:S(2)}, u32[]{:S(2)}) collective-permute-start(bf16[192,1024]{1,0:T(8,128)(2,1)S(1)} %get-tuple-element.84), channel_id=1, source_target_pairs={{0,1},{1,0},{2,3},{3,2},{4,5},{5,4},{6,7},{7,6},{8,9},{9,8},{10,11... | collective-permute-start | bytes 1179656 | tf_op jit(solution)/shard_map/ppermute | solution.py:354
  70.8 12.0 %collective-permute-start.26 = (bf16[192,1024]{1,0:T(8,128)(2,1)S(1)}, bf16[192,1024]{1,0:T(8,128)(2,1)S(1)}, u32[]{:S(2)}, u32[]{:S(2)}) collective-permute-start(bf16[192,1024]{1,0:T(8,128)(2,1)S(1)} %add_convert_fusion), channel_id=1, source_target_pairs={{0,2},{1,3},{2,0},{3,1},{4,6},{5,7},{6,4},{7,5},{8,10},{9,11},{10,... | collective-permute-start | bytes 1179656 | tf_op jit(solution)/shard_map/ppermute | solution.py:366
  71.5 18.9 %collective-permute-start.24 = (bf16[192,1024]{1,0:T(8,128)(2,1)S(1)}, bf16[192,1024]{1,0:T(8,128)(2,1)S(1)}, u32[]{:S(2)}, u32[]{:S(2)}) collective-permute-start(bf16[192,1024]{1,0:T(8,128)(2,1)S(1)} %add_convert_fusion.1), channel_id=1, source_target_pairs={{0,2},{1,3},{2,0},{3,1},{4,6},{5,7},{6,4},{7,5},{8,10},{9,11},{10,... | collective-permute-start | bytes 1179656 | tf_op jit(solution)/shard_map/ppermute | solution.py:366
  (13 other events, 132.9 us)

commit v3 on v2

v3 whole, which is shorter than its diff:
```python
import functools
import math

import jax
import jax.numpy as jnp
import numpy as np
from jax import lax
from jax.experimental import pallas as pl
from jax.experimental.pallas import tpu as pltpu
from jax.sharding import PartitionSpec as P

F32 = jnp.float32
BF16 = jnp.bfloat16
VMEM = pl.BlockSpec(memory_space=pltpu.VMEM)
SMEM = pl.BlockSpec(memory_space=pltpu.SMEM)
HBM = pl.BlockSpec(memory_space=pltpu.HBM)
SUB = 8


def params(nbytes):
    return pltpu.CompilerParams(vmem_limit_bytes=int(min(nbytes + 4 * 2**20, 58 * 2**20)))


def tables(total, inner):
    outer = total // inner
    n1 = np.arange(outer)
    eye = np.eye(SUB)
    ang = 2.0 * np.pi * np.outer(n1 + 0.25, n1) / outer
    first = np.stack([np.cos(ang), -np.sin(ang)], axis=1)
    first = np.einsum("kcn,ij->kcinj", first, eye).reshape(2 * outer * SUB, outer * SUB)
    last = np.stack([np.cos(ang), -np.sin(ang)], axis=1) / total
    last = np.einsum("kcn,ij->nikcj", last, eye).reshape(outer * SUB, 2 * outer * SUB)
    n2 = np.arange(inner)
    freq = n1[:, None] + outer * n2[None, :] + 0.25
    ang = 2.0 * np.pi * freq[:, :, None] * n2[None, None, :] / total
    cos, sin = np.cos(ang), np.sin(ang)
    mid = np.concatenate(
        [np.concatenate([cos, sin], axis=2), np.concatenate([-sin, cos], axis=2)], axis=1
    )
    back = np.swapaxes(mid, 1, 2)
    return tuple(jnp.asarray(np.ascontiguousarray(a).astype(jnp.bfloat16)) for a in (first, mid, back, last))


def split_kernel(idx_ref, array_ref, *outs, count):
    width = outs[0].shape[1]
    for s in range(count):
        at = pl.ds(pl.multiple_of(lax.rem(idx_ref[0] + s, count) * width, width), width)
        outs[s][...] = array_ref[:, at]


def filter_slices(idx, value, count):
    rows, channels = value.shape
    width = channels // count
    if width % 128:
        return [
            lax.dynamic_slice_in_dim(value, lax.rem(idx[0] + s, count) * width, width, 1)
            for s in range(count)
        ]
    return pl.pallas_call(
        functools.partial(split_kernel, count=count),
        out_shape=[jax.ShapeDtypeStruct((rows, width), BF16)] * count,
        in_specs=[SMEM, VMEM],
        out_specs=[VMEM] * count,
        compiler_params=params(4 * rows * channels),
        cost_estimate=pl.CostEstimate(flops=0, bytes_accessed=4 * rows * channels, transcendentals=0),
    )(idx, value)


def gate_kernel(idx_ref, order_ref, key_hbm, value_hbm, weight_ref, *refs, count):
    outs, columns = refs[:count], refs[count:-4]
    key_ref, value_ref, own_sems, sems = refs[-4:]
    width, cols = outs[0].shape[1], columns[0].shape[1]
    copies = [
        pltpu.make_async_copy(key_hbm, key_ref, own_sems.at[0]),
        pltpu.make_async_copy(value_hbm, value_ref, own_sems.at[1]),
    ]
    for j, column_ref in enumerate(columns):
        at = pl.ds(pl.multiple_of(order_ref[j] * cols, cols), cols)
        copies.append(pltpu.make_async_copy(weight_ref.at[:, at], column_ref, sems.at[j]))
    for copy in copies:
        copy.start()
    for copy in copies[:2]:
        copy.wait()
    for s in range(count):
        at = pl.ds(pl.multiple_of(lax.rem(idx_ref[0] + s, count) * width, width), width)
        outs[s][...] = (key_ref[:, at].astype(F32) * value_ref[:, at].astype(F32)).astype(BF16)
    for copy in copies[2:]:
        copy.wait()


def plain_kernel(order_ref, weight_ref, *refs):
    *columns, sems = refs
    cols = columns[0].shape[1]
    copies = []
    for j, column_ref in enumerate(columns):
        at = pl.ds(pl.multiple_of(order_ref[j] * cols, cols), cols)
        copies.append(pltpu.make_async_copy(weight_ref.at[:, at], column_ref, sems.at[j]))
        copies[-1].start()
    for copy in copies:
        copy.wait()


def gated_slices(idx, key_k, value_v, count, order, weight, groups):
    rows, channels = key_k.shape
    width, cols = channels // count, weight.shape[1] // groups
    picked = order.shape[0]
    weight = pltpu.with_memory_space_constraint(weight, pltpu.HBM)
    columns = [pltpu.VMEM((weight.shape[0], cols), BF16)] * picked
    limit = 8 * rows * channels + 2 * picked * weight.shape[0] * cols
    cost = pl.CostEstimate(flops=rows * channels, bytes_accessed=limit, transcendentals=0)
    if width % 128:
        gated = (key_k.astype(F32) * value_v.astype(F32)).astype(BF16)
        return filter_slices(idx, gated, count), pl.pallas_call(
            plain_kernel,
            out_shape=columns,
            in_specs=[SMEM, HBM],
            out_specs=[VMEM] * picked,
            scratch_shapes=[pltpu.SemaphoreType.DMA((picked,))],
            compiler_params=params(limit),
            cost_estimate=cost,
        )(order, weight)
    outs = pl.pallas_call(
        functools.partial(gate_kernel, count=count),
        out_shape=[jax.ShapeDtypeStruct((rows, width), BF16)] * count + columns,
        in_specs=[SMEM, SMEM] + [HBM] * 3,
        out_specs=[VMEM] * (count + picked),
        scratch_shapes=[pltpu.VMEM((rows, channels), BF16)] * 2
        + [pltpu.SemaphoreType.DMA((2,)), pltpu.SemaphoreType.DMA((picked,))],
        compiler_params=params(limit),
        cost_estimate=cost,
    )(
        idx,
        order,
        pltpu.with_memory_space_constraint(key_k, pltpu.HBM),
        pltpu.with_memory_space_constraint(value_v, pltpu.HBM),
        weight,
    )
    return outs[:count], outs[count:]


def exchange(blocks, axis, count):
    out = [blocks[0]]
    for s in range(1, count):
        out.append(lax.ppermute(blocks[s], axis, [(i, (i + s) % count) for i in range(count)]))
    return out


def gather_positions(me, blocks, spot, count):
    outer_here = blocks[0].shape[0] // spot.shape[1]
    for s in range(count):
        src = lax.rem(me + count - s, count)
        spot[pl.ds(src * outer_here, outer_here)] = blocks[s][...].reshape(outer_here, *spot.shape[1:])


def halves(tile):
    tile = tile.astype(F32)
    width = tile.shape[-1]
    return jnp.concatenate(
        [tile[..., at : at + SUB, :].reshape(-1, width).astype(BF16) for at in (0, SUB)], axis=1
    )


def joined(value, lead):
    width = value.shape[1] // 2
    parts = [value[:, at : at + width].reshape(*lead, SUB, width) for at in (0, width)]
    return jnp.concatenate(parts, axis=len(lead)).astype(BF16)


def for_each(count, body):
    if count <= 32:
        for i in range(count):
            body(i)
    else:
        lax.fori_loop(0, count, lambda i, c: (body(i), c)[1], 0, unroll=4 if count % 4 == 0 else 1)


def forward_first(first_ref, spot, mixed):
    outer, inner, _ = spot.shape

    def body(i):
        rows = pl.ds(i * 2 * SUB, 2 * SUB)
        value = jnp.dot(first_ref[...], halves(spot[:, rows, :]), preferred_element_type=F32)
        mixed[:, :, rows, :] = joined(value, (outer, 2))

    for_each(inner // (2 * SUB), body)


def filter_kernel(idx_ref, first_ref, mid_hbm, back_hbm, *refs, count):
    blocks, (out_ref, mid_ref, back_ref, spot, mixed, sems) = refs[:count], refs[count:]
    outer, _, inner, width = mixed.shape
    parts = sems.shape[0] - 1
    cuts = [outer * p // parts for p in range(parts + 1)]
    spans = [pl.ds(lo, hi - lo) for lo, hi in zip(cuts, cuts[1:])]
    copies = [pltpu.make_async_copy(mid_hbm.at[at], mid_ref.at[at], sems.at[p]) for p, at in enumerate(spans)]
    copies.append(pltpu.make_async_copy(back_hbm, back_ref, sems.at[parts]))
    for copy in copies:
        copy.start()
    gather_positions(idx_ref[0], blocks, spot, count)
    forward_first(first_ref, spot, mixed)

    for p in range(parts):
        copies[p].wait()

        def body(k):
            k = k + cuts[p]
            out_ref[k] = jnp.dot(
                mid_ref[k], mixed[k].reshape(2 * inner, width), preferred_element_type=F32
            ).astype(BF16)

        for_each(cuts[p + 1] - cuts[p], body)
    copies[parts].wait()


def conv_kernel(idx_ref, first_ref, mid_ref, back_ref, last_ref, filt_ref, *refs, count):
    blocks, outs, (spot, mixed) = refs[:count], refs[count : 2 * count], refs[2 * count :]
    me = idx_ref[0]
    gather_positions(me, blocks, spot, count)
    forward_first(first_ref, spot, mixed)
    outer, _, inner, width = mixed.shape

    def middle(k):
        spec = jnp.dot(mid_ref[k], mixed[k].reshape(2 * inner, width), preferred_element_type=F32)
        filt = filt_ref[k].astype(F32)
        re, im = spec[:inner], spec[inner:]
        fre, fim = filt[:inner], filt[inner:]
        prod = jnp.concatenate([re * fre - im * fim, re * fim + im * fre], axis=0).astype(BF16)
        turned = jnp.dot(back_ref[k], prod, preferred_element_type=F32)
        mixed[k] = turned.astype(BF16).reshape(2, inner, width)

    for_each(outer, middle)

    def ending(i):
        rows = pl.ds(i * 2 * SUB, 2 * SUB)
        value = jnp.dot(last_ref[...], halves(mixed[:, :, rows, :]), preferred_element_type=F32)
        spot[:, rows, :] = joined(value, (outer,))

    for_each(inner // (2 * SUB), ending)
    here = outer // count
    for s in range(count):
        dst = lax.rem(me + s, count)
        outs[s][...] = spot[pl.ds(dst * here, here)].reshape(here * inner, width)


def hidden_rows(idx_ref, gain_ref, gate_ref, key_ref, value_ref, blocks, out_ref, at):
    me, count = idx_ref[0], len(blocks)
    width = blocks[0].shape[1]
    rows = slice(at, at + out_ref.shape[0])
    for s in range(count):
        src = lax.rem(me + count - s, count)
        cols = pl.ds(pl.multiple_of(src * width, width), width)
        gated = (key_ref[rows, cols].astype(F32) * value_ref[rows, cols].astype(F32)).astype(BF16).astype(F32)
        total = blocks[s][rows, :].astype(F32) + gain_ref[:, cols] * gated
        out_ref[:, cols] = (gate_ref[rows, cols].astype(F32) * total).astype(BF16)


def times_columns(hid_ref, weight_ref, part_ref, extra_ref=None):
    width = part_ref.shape[1]
    tile = min(256, width)
    for j in range(width // tile):
        cols = slice(j * tile, (j + 1) * tile)
        value = jnp.dot(hid_ref[...], weight_ref[:, cols], preferred_element_type=F32)
        if extra_ref is not None:
            value = value + extra_ref[:, cols].astype(F32)
        part_ref[:, cols] = value.astype(part_ref.dtype)


def rows_kernel(idx_ref, gain_ref, gate_ref, key_ref, value_ref, *refs, at, others, more):
    weights, refs = refs[:others], refs[others:]
    if more:
        own_ref, first_ref, *refs = refs
        *refs, own_first = refs
    *blocks, hid_ref, part_ref = refs
    if more:
        times_columns(first_ref, own_ref, own_first)
    hidden_rows(idx_ref, gain_ref, gate_ref, key_ref, value_ref, blocks, hid_ref, at)
    for j, weight_ref in enumerate(weights):
        cols = weight_ref.shape[1]
        times_columns(hid_ref, weight_ref, part_ref.at[:, j * cols : (j + 1) * cols])


def hidden_products(arrays, weights, blocks, at, rows, more=()):
    total, channels = arrays[2].shape
    columns = weights[0].shape[1]
    pinned = [pltpu.with_memory_space_constraint(w, pltpu.VMEM) for w in (*weights, *more)]
    limit = 2 * (len(pinned) + 1) * channels * columns + 12 * total * channels + 8 * total * columns
    outs = [pltpu.VMEM((rows, channels), BF16), pltpu.VMEM((rows, len(weights) * columns), BF16)]
    if more:
        outs.append(pltpu.VMEM((more[1].shape[0], columns), BF16))
    return pl.pallas_call(
        functools.partial(rows_kernel, at=at, others=len(weights), more=bool(more)),
        out_shape=outs,
        in_specs=[SMEM] + [VMEM] * (4 + len(pinned) + len(blocks)),
        out_specs=[VMEM] * len(outs),
        compiler_params=params(limit),
        cost_estimate=pl.CostEstimate(flops=4 * rows * channels * columns, bytes_accessed=limit, transcendentals=0),
    )(*arrays, *pinned, *blocks)


def own_kernel(hid_ref, weight_ref, crossed_ref, out_ref):
    times_columns(hid_ref, weight_ref, out_ref, crossed_ref.at[:, : out_ref.shape[1]])


def own_product(hidden, weight, crossed):
    rows, channels = hidden.shape
    columns = weight.shape[1]
    return pl.pallas_call(
        own_kernel,
        out_shape=pltpu.VMEM((rows, columns), BF16),
        in_specs=[VMEM] * 3,
        out_specs=VMEM,
        compiler_params=params(2 * channels * columns + 4 * rows * channels + 8 * rows * columns),
        cost_estimate=pl.CostEstimate(
            flops=2 * rows * channels * columns, bytes_accessed=2 * channels * columns, transcendentals=0
        ),
    )(*(pltpu.with_memory_space_constraint(a, pltpu.VMEM) for a in (hidden, weight, crossed)))


def late_kernel(group_ref, weight_ref, *refs, pieces, at):
    hids, extras = refs[:pieces], refs[pieces : 2 * pieces]
    parts, (held, sem) = refs[2 * pieces : -2], refs[-2:]
    width = held.shape[1]
    cols = pl.ds(pl.multiple_of(group_ref[0] * width, width), width)
    copy = pltpu.make_async_copy(weight_ref.at[:, cols], held, sem)
    copy.start()
    copy.wait()
    for r in range(pieces):
        times_columns(hids[r], held, parts[r], extras[r].at[:, at : at + width])


def late_product(group, hidden, weight, groups, extra, at, dtype):
    pieces = len(hidden)
    channels, width = weight.shape[0], weight.shape[1] // groups
    rows = sum(h.shape[0] for h in hidden)
    return pl.pallas_call(
        functools.partial(late_kernel, pieces=pieces, at=at),
        out_shape=[pltpu.VMEM((h.shape[0], width), dtype) for h in hidden],
        in_specs=[SMEM, HBM] + [VMEM] * (2 * pieces),
        out_specs=[VMEM] * pieces,
        scratch_shapes=[pltpu.VMEM((channels, width), BF16), pltpu.SemaphoreType.DMA],
        compiler_params=params(2 * channels * width + 2 * rows * channels + 2 * rows * weight.shape[1] + 6 * rows * width),
        cost_estimate=pl.CostEstimate(flops=0, bytes_accessed=channels, transcendentals=0),
    )(group, pltpu.with_memory_space_constraint(weight, pltpu.HBM), *hidden, *extra)


def add_kernel(own_ref, other_ref, out_ref):
    other = other_ref[:, : own_ref.shape[1]].astype(F32)
    out_ref[...] = (own_ref[...].astype(F32) + other).astype(BF16)


def add(own, other):
    return pl.pallas_call(
        add_kernel,
        out_shape=pltpu.VMEM(own.shape, BF16),
        in_specs=[VMEM] * 2,
        out_specs=VMEM,
        compiler_params=params(4 * own.size + 2 * other.size),
        cost_estimate=pl.CostEstimate(flops=own.size, bytes_accessed=6 * own.size, transcendentals=0),
    )(own, pltpu.with_memory_space_constraint(other, pltpu.VMEM))


def finish_kernel(*refs, at, terms):
    values, (out_ref, held, sem) = refs[:terms], refs[-3:]
    total = values[0][...]
    for value in values[1:]:
        total = total + value[...].astype(F32)
    held[...] = total.astype(BF16)
    rows = held.shape[0]
    copy = pltpu.make_async_copy(held, out_ref.at[pl.ds(at, rows), :], sem)
    copy.start()
    copy.wait()


def finish(values, at, rows, buffer):
    here, columns = values[0].shape
    aliased = [] if buffer is None else [buffer]
    return pl.pallas_call(
        functools.partial(finish_kernel, at=at, terms=len(values)),
        out_shape=jax.ShapeDtypeStruct((rows, columns), BF16),
        in_specs=[VMEM] * len(values) + [HBM] * len(aliased),
        out_specs=HBM,
        scratch_shapes=[pltpu.VMEM((here, columns), BF16), pltpu.SemaphoreType.DMA],
        input_output_aliases={len(values): 0} if aliased else {},
        compiler_params=params(4 * here * columns * (len(values) + 2)),
        cost_estimate=pl.CostEstimate(flops=0, bytes_accessed=columns, transcendentals=0),
    )(*(pltpu.with_memory_space_constraint(v, pltpu.VMEM) for v in values), *aliased)


def local(gate_q, key_k, value_v, long_filter, skip_gain, out_weight):
    rows, channels = key_k.shape
    count = lax.axis_size("ctx")
    groups = lax.axis_size("ch")
    chips = groups // 2
    total = rows * count
    inner = next(n for n in range(128, 0, -16) if rows % n == 0)
    outer = total // inner
    width = channels // count
    lanes = -(-width // 128) * 128
    idx = lax.axis_index("ctx").astype(jnp.int32).reshape(1)
    first, mid, back, last = tables(total, inner)
    spot = pltpu.VMEM((outer, inner, width), BF16)
    mixed = pltpu.VMEM((outer, 2, inner, width), BF16)
    signal = 2 * total * lanes
    table = 2 * (first.size + mid.size)

    here = lax.axis_index("ch").astype(jnp.int32)
    chip, core = here // 2, here % 2

    def group_of(step, which):
        return lax.rem(chip + step, chips) * 2 + which

    filter_in = exchange(filter_slices(idx, long_filter, count), "ctx", count)
    steps = list(range(1, chips)) + [0]
    order = jnp.stack([group_of(step, 1 - core) for step in steps] + [group_of(1, core)])
    slices, weights = gated_slices(idx, key_k, value_v, count, order, out_weight, groups)
    gated_in = exchange(slices, "ctx", count)
    spectrum, mid, back = pl.pallas_call(
        functools.partial(filter_kernel, count=count),
        out_shape=[
            jax.ShapeDtypeStruct((outer, 2 * inner, width), BF16),
            jax.ShapeDtypeStruct(mid.shape, BF16),
            jax.ShapeDtypeStruct(back.shape, BF16),
        ],
        in_specs=[SMEM, VMEM, HBM, HBM] + [VMEM] * count,
        out_specs=[VMEM] * 3,
        scratch_shapes=[spot, mixed, pltpu.SemaphoreType.DMA((5,))],
        compiler_params=params(2 * table + 6 * signal),
        cost_estimate=pl.CostEstimate(flops=3 * 10**9, bytes_accessed=8 * 10**6, transcendentals=0),
    )(
        idx,
        first,
        pltpu.with_memory_space_constraint(mid, pltpu.HBM),
        pltpu.with_memory_space_constraint(back, pltpu.HBM),
        *filter_in,
    )
    conv_out = pl.pallas_call(
        functools.partial(conv_kernel, count=count),
        out_shape=[jax.ShapeDtypeStruct((rows, width), BF16)] * count,
        in_specs=[SMEM] + [VMEM] * (5 + count),
        out_specs=[VMEM] * count,
        scratch_shapes=[spot, mixed],
        compiler_params=params(2 * table + 7 * signal),
        cost_estimate=pl.CostEstimate(flops=6 * 10**9, bytes_accessed=12 * 10**6, transcendentals=0),
    )(idx, first, mid, back, last, spectrum, *gated_in)
    conv_in = exchange(conv_out, "ctx", count)

    swap = [(i, i ^ 1) for i in range(groups)]
    lead = rows // 32 * 16

    def to_chip(part, step):
        return lax.ppermute(part, "ch", [(i, (i + 2 * step) % groups) for i in range(groups)])

    gain = skip_gain[None, :]
    if width % 128:
        conv = jnp.zeros((rows, channels), BF16)
        for s in range(count):
            src = lax.rem(idx[0] + count - s, count)
            conv = lax.dynamic_update_slice_in_dim(conv, conv_in[s], src * width, 1)
        idx, conv_in = jnp.zeros_like(idx), [conv]
    arrays = [idx, gain, gate_q, key_k, value_v]
    *others, own = weights
    hid_first, part_first = hidden_products(arrays, others, conv_in, 0, lead)
    crossed = [lax.ppermute(part_first, "ch", swap)]
    hid_rest, part_rest, sums = hidden_products(arrays, others, conv_in, lead, rows - lead, (own, hid_first))
    crossed.append(lax.ppermute(part_rest, "ch", swap))
    hidden = [hid_first, hid_rest]
    first_total = add(sums, crossed[0])
    arrived = [[to_chip(first_total, 1)], [to_chip(own_product(hid_rest, own, crossed[1]), 1)]]
    later = list(lax.optimization_barrier((*hidden, first_total))[:2])
    for j, step in enumerate(steps[1:-1]):
        totals = late_product(
            group_of(step, core).reshape(1), later, out_weight, groups, crossed, (j + 1) * own.shape[1], BF16
        )
        for got, total in zip(arrived, totals):
            got.append(to_chip(total, step))
    last_sums = late_product(
        group_of(0, core).reshape(1), later, out_weight, groups, crossed, (chips - 1) * own.shape[1], F32
    )
    first_rows = finish([last_sums[0]] + arrived[0], 0, rows, None)
    return finish([last_sums[1]] + arrived[1], lead, rows, first_rows)


def solution(mesh):
    placed = (
        P("ctx", "ch"),
        P("ctx", "ch"),
        P("ctx", "ch"),
        P("ctx", "ch"),
        P("ch"),
        P("ch", None),
    )
    return jax.shard_map(
        local, mesh=mesh, in_specs=placed, out_specs=P("ctx", "ch"), check_vma=False
    )
```

time: 92.9 us -> 89.8 us (0.967)
  waiting for transfers between devices: 23.2 us -> 20.6 us
  Pallas kernels: 17.6 us -> 19.5 us
  starting transfers between devices: 47.7 us -> 46.5 us
  local copies, waits for them, and re-layouts: 2.3 us -> 1.16 us
    ppermute x21, waiting for transfers between devices: 7.73 us -> 6.16 us  [exchange(): lax.ppermute(blocks[s], axis, [(i, (i + s) % count) for i in range(count)])]
    ppermute x6 -> x4, starting transfers between devices: 3.3 us -> 1.78 us  [the longest x2 1.16 us: to_chip(): lax.ppermute(part, 'ch', [(i, (i + 2 * step) % groups) for i in range(gro...]
    unnamed x20 -> x14, local copies, waits for them, and re-layouts: 2.3 us -> 1.16 us
    ppermute x6 -> x4, waiting for transfers between devices: 15.5 us -> 14.4 us  [the longest x2 13.2 us: to_chip(): lax.ppermute(part, 'ch', [(i, (i + 2 * step) % groups) for i in range(gro...]
    pallas_call x2, Pallas kernels: 1.64 us -> 2.65 us  [finish(): pl.pallas_call(functools.partial(finish_kernel, at=at, terms=len(values))...]
  transfers between devices with their start and end apart: 27 -> 25, of which waited for: 7 -> 8; matrix products, arithmetic and copies ran while one was open for 0% -> 0% of each run, Pallas kernels for 11% -> 15%
where the time goes in v3:
time: 89.8 us; the launch traced here: 88.1 us
  starting transfers between devices  46.5 us (52%)
  waiting for transfers between devices  20.6 us (23%)
  Pallas kernels  19.5 us (22%)
  local copies, waits for them, and re-layouts  1.16 us (1%)
    ppermute x21, starting transfers between devices, exchange(): lax.ppermute(blocks[s], axis, [(i, (i + s) % count) for i in range(count)])  44.7 us
    ppermute x2, waiting for transfers between devices, to_chip(): lax.ppermute(part, 'ch', [(i, (i + 2 * step) % groups) for i in range(gro...  13.2 us
    ppermute x21, waiting for transfers between devices, exchange(): lax.ppermute(blocks[s], axis, [(i, (i + s) % count) for i in range(count)])  6.16 us
    pallas_call x1, Pallas kernels, gated_slices(): pl.pallas_call(functools.partial(gate_kernel, count=count), out_shape=[ja...  3.93 us
    pallas_call x2, Pallas kernels, hidden_products(): pl.pallas_call(functools.partial(rows_kernel, at=at, others=len(weights),...  3.35 us
    pallas_call x1, Pallas kernels, local(): pl.pallas_call(functools.partial(conv_kernel, count=count), out_shape=[ja...  3.05 us
    pallas_call x1, Pallas kernels, local(): pl.pallas_call(functools.partial(filter_kernel, count=count), out_shape=[...  2.98 us
    pallas_call x2, Pallas kernels, finish(): pl.pallas_call(functools.partial(finish_kernel, at=at, terms=len(values))...  2.65 us
  transfers between devices with their start and end apart: 25, of which 8 were waited for; matrix products, arithmetic and copies ran while one was open for 0% of the time, Pallas kernels for 15%

profile of v3, /device:TPU:20, one launch (start us, length us, event | category | flops | bytes accessed | tf_op | source)
XLA Modules:
  0.0 88.1 jit_solution(7986532473688789882)
XLA Ops:
  1.3 1.5 %collective-permute-start = (bf16[384,128]{1,0:T(8,128)(2,1)S(1)}, bf16[384,128]{1,0:T(8,128)(2,1)S(1)}, u32[]{:S(2)}, u32[]{:S(2)}) collective-permute-start(bf16[384,128]{1,0:T(8,128)(2,1)S(1)} %get-tuple-element.47), channel_id=1, source_target_pairs={{0,4},{4,8},{8,12},{12,16},{16,20},{20,24},{24,28},{28,0},{1,5},{5... | collective-permute-start | bytes 294920 | tf_op jit(solution)/shard_map/ppermute | solution.py:144
  2.9 1.6 %collective-permute-start.1 = (bf16[384,128]{1,0:T(8,128)(2,1)S(1)}, bf16[384,128]{1,0:T(8,128)(2,1)S(1)}, u32[]{:S(2)}, u32[]{:S(2)}) collective-permute-start(bf16[384,128]{1,0:T(8,128)(2,1)S(1)} %get-tuple-element.48), channel_id=1, source_target_pairs={{0,8},{4,12},{8,16},{12,20},{16,24},{20,28},{24,0},{28,4},{1,9},{5... | collective-permute-start | bytes 294920 | tf_op jit(solution)/shard_map/ppermute | solution.py:144
  5.7 1.7 %collective-permute-start.3 = (bf16[384,128]{1,0:T(8,128)(2,1)S(1)}, bf16[384,128]{1,0:T(8,128)(2,1)S(1)}, u32[]{:S(2)}, u32[]{:S(2)}) collective-permute-start(bf16[384,128]{1,0:T(8,128)(2,1)S(1)} %get-tuple-element.50), channel_id=1, source_target_pairs={{0,16},{4,20},{8,24},{12,28},{16,0},{20,4},{24,8},{28,12},{1,17},{... | collective-permute-start | bytes 294920 | tf_op jit(solution)/shard_map/ppermute | solution.py:144
  8.7 3.9 %shard_map.100 = (bf16[384,128]{1,0:T(8,128)(2,1)S(1)}, bf16[384,128]{1,0:T(8,128)(2,1)S(1)}, bf16[384,128]{1,0:T(8,128)(2,1)S(1)}, bf16[384,128]{1,0:T(8,128)(2...) custom-call(s32[1]{0:T(128)} %bitcast.1.idx_ref, ...), custom_call_target="tpu_custom_call" | custom-call | flops 393216 | bytes 9437184 | tf_op jit(solution)/shard_map/pallas_call | solution.py:122
  12.7 1.4 %collective-permute-start.5 = (bf16[384,128]{1,0:T(8,128)(2,1)S(1)}, bf16[384,128]{1,0:T(8,128)(2,1)S(1)}, u32[]{:S(2)}, u32[]{:S(2)}) collective-permute-start(bf16[384,128]{1,0:T(8,128)(2,1)S(1)} %get-tuple-element.52), channel_id=1, source_target_pairs={{0,24},{4,28},{8,0},{12,4},{16,8},{20,12},{24,16},{28,20},{1,25},{... | collective-permute-start | bytes 294920 | tf_op jit(solution)/shard_map/ppermute | solution.py:144
  14.1 2.6 %collective-permute-start.6 = (bf16[384,128]{1,0:T(8,128)(2,1)S(1)}, bf16[384,128]{1,0:T(8,128)(2,1)S(1)}, u32[]{:S(2)}, u32[]{:S(2)}) collective-permute-start(bf16[384,128]{1,0:T(8,128)(2,1)S(1)} %get-tuple-element.53), channel_id=1, source_target_pairs={{0,28},{4,0},{8,4},{12,8},{16,12},{20,16},{24,20},{28,24},{1,29},{... | collective-permute-start | bytes 294920 | tf_op jit(solution)/shard_map/ppermute | solution.py:144
  17.9 4.1 %collective-permute-start.8 = (bf16[384,128]{1,0:T(8,128)(2,1)S(1)}, bf16[384,128]{1,0:T(8,128)(2,1)S(1)}, u32[]{:S(2)}, u32[]{:S(2)}) collective-permute-start(bf16[384,128]{1,0:T(8,128)(2,1)S(1)} %get-tuple-element.59), channel_id=1, source_target_pairs={{0,8},{4,12},{8,16},{12,20},{16,24},{20,28},{24,0},{28,4},{1,9},{5... | collective-permute-start | bytes 294920 | tf_op jit(solution)/shard_map/ppermute | solution.py:144
  21.9 3.3 %collective-permute-start.9 = (bf16[384,128]{1,0:T(8,128)(2,1)S(1)}, bf16[384,128]{1,0:T(8,128)(2,1)S(1)}, u32[]{:S(2)}, u32[]{:S(2)}) collective-permute-start(bf16[384,128]{1,0:T(8,128)(2,1)S(1)} %get-tuple-element.60), channel_id=1, source_target_pairs={{0,12},{4,16},{8,20},{12,24},{16,28},{20,0},{24,4},{28,8},{1,13},{... | collective-permute-start | bytes 294920 | tf_op jit(solution)/shard_map/ppermute | solution.py:144
  26.3 4.1 %collective-permute-start.11 = (bf16[384,128]{1,0:T(8,128)(2,1)S(1)}, bf16[384,128]{1,0:T(8,128)(2,1)S(1)}, u32[]{:S(2)}, u32[]{:S(2)}) collective-permute-start(bf16[384,128]{1,0:T(8,128)(2,1)S(1)} %get-tuple-element.62), channel_id=1, source_target_pairs={{0,20},{4,24},{8,28},{12,0},{16,4},{20,8},{24,12},{28,16},{1,21},{... | collective-permute-start | bytes 294920 | tf_op jit(solution)/shard_map/ppermute | solution.py:144
  30.4 2.5 %collective-permute-start.12 = (bf16[384,128]{1,0:T(8,128)(2,1)S(1)}, bf16[384,128]{1,0:T(8,128)(2,1)S(1)}, u32[]{:S(2)}, u32[]{:S(2)}) collective-permute-start(bf16[384,128]{1,0:T(8,128)(2,1)S(1)} %get-tuple-element.63), channel_id=1, source_target_pairs={{0,24},{4,28},{8,0},{12,4},{16,8},{20,12},{24,16},{28,20},{1,25},{... | collective-permute-start | bytes 294920 | tf_op jit(solution)/shard_map/ppermute | solution.py:144
  32.9 3.0 %shard_map.102 = (bf16[24,256,128]{2,1,0:T(8,128)(2,1)S(1)}, bf16[24,256,256]{2,1,0:T(8,128)(2,1)S(1)}, bf16[24,256,256]{2,1,0:T(8,128)(2,1)S(1)}) custom-call(s32[1]{0:T(128)} %bitcast.1.idx_ref, bf16[384,192]{1,0:T(8,128)(2,1)S(1)} %copy-done.5, bf16[24,256,256]{2,1,0:T(8,128)(2,1)} %constant.47.clone.mid_hbm, ...), custom_call_target="tpu_custom_call" | custom-call | flops 3000000000 | bytes 8000000 | tf_op jit(solution)/shard_map/pallas_call | solution.py:416
  38.5 3.0 %shard_map.103 = (bf16[384,128]{1,0:T(8,128)(2,1)S(1)}, bf16[384,128]{1,0:T(8,128)(2,1)S(1)}, bf16[384,128]{1,0:T(8,128)(2,1)S(1)}, bf16[384,128]{1,0:T(8,128)(2...) custom-call(s32[1]{0:T(128)} %bitcast.1.idx_ref, ...), custom_call_target="tpu_custom_call" | custom-call | flops 6000000000 | bytes 12000000 | tf_op jit(solution)/shard_map/pallas_call | solution.py:435
  41.6 1.4 %collective-permute-start.14 = (bf16[384,128]{1,0:T(8,128)(2,1)S(1)}, bf16[384,128]{1,0:T(8,128)(2,1)S(1)}, u32[]{:S(2)}, u32[]{:S(2)}) collective-permute-start(bf16[384,128]{1,0:T(8,128)(2,1)S(1)} %get-tuple-element.66), channel_id=1, source_target_pairs={{0,4},{4,8},{8,12},{12,16},{16,20},{20,24},{24,28},{28,0},{1,5},{5... | collective-permute-start | bytes 294920 | tf_op jit(solution)/shard_map/ppermute | solution.py:144
  42.9 2.6 %collective-permute-start.15 = (bf16[384,128]{1,0:T(8,128)(2,1)S(1)}, bf16[384,128]{1,0:T(8,128)(2,1)S(1)}, u32[]{:S(2)}, u32[]{:S(2)}) collective-permute-start(bf16[384,128]{1,0:T(8,128)(2,1)S(1)} %get-tuple-element.67), channel_id=1, source_target_pairs={{0,8},{4,12},{8,16},{12,20},{16,24},{20,28},{24,0},{28,4},{1,9},{5... | collective-permute-start | bytes 294920 | tf_op jit(solution)/shard_map/ppermute | solution.py:144
  47.0 3.8 %collective-permute-start.18 = (bf16[384,128]{1,0:T(8,128)(2,1)S(1)}, bf16[384,128]{1,0:T(8,128)(2,1)S(1)}, u32[]{:S(2)}, u32[]{:S(2)}) collective-permute-start(bf16[384,128]{1,0:T(8,128)(2,1)S(1)} %get-tuple-element.70), channel_id=1, source_target_pairs={{0,20},{4,24},{8,28},{12,0},{16,4},{20,8},{24,12},{28,16},{1,21},{... | collective-permute-start | bytes 294920 | tf_op jit(solution)/shard_map/ppermute | solution.py:144
  51.4 7.4 %collective-permute-start.20 = (bf16[384,128]{1,0:T(8,128)(2,1)S(1)}, bf16[384,128]{1,0:T(8,128)(2,1)S(1)}, u32[]{:S(2)}, u32[]{:S(2)}) collective-permute-start(bf16[384,128]{1,0:T(8,128)(2,1)S(1)} %get-tuple-element.72), channel_id=1, source_target_pairs={{0,28},{4,0},{8,4},{12,8},{16,12},{20,16},{24,20},{28,24},{1,29},{... | collective-permute-start | bytes 294920 | tf_op jit(solution)/shard_map/ppermute | solution.py:144
  58.8 1.5 %collective-permute-done.19.refs_8_.refs_10_ = bf16[384,128]{1,0:T(8,128)(2,1)S(1)} collective-permute-done((bf16[384,128]{1,0:T(8,128)(2,1)S(1)}, bf16[384,128]{1,0:T(8,128)(2,1)S(1)}, u32[]{:S(2)}, u32[]{:S(2)}) %collective-permute-start.19) | collective-permute-done | bytes 98336 | tf_op jit(solution)/shard_map/ppermute | solution.py:144
  60.2 2.1 %collective-permute-done.20.refs_9_.refs_11_ = bf16[384,128]{1,0:T(8,128)(2,1)S(1)} collective-permute-done((bf16[384,128]{1,0:T(8,128)(2,1)S(1)}, bf16[384,128]{1,0:T(8,128)(2,1)S(1)}, u32[]{:S(2)}, u32[]{:S(2)}) %collective-permute-start.20) | collective-permute-done | bytes 98336 | tf_op jit(solution)/shard_map/ppermute | solution.py:144
  62.4 1.5 %shard_map.104 = (bf16[192,1024]{1,0:T(8,128)(2,1)S(1)}, bf16[192,2048]{1,0:T(8,128)(2,1)S(1)}) custom-call(s32[1]{0:T(128)} %bitcast.1.idx_ref, f32[1,1024]{1,0:T(1,128)S(1)} %bitcast.6, bf16[384,1024]{1,0:T(8,128)(2,1)S(1)} %copy-done.2, bf16[384,1024]{1,0:T(8,128)(2,1)S(1)} %copy-done, bf16[384,1024]{1,0:T(8,128)(2,1)S(1)} %copy-done.1, ...), custom_call_target="tpu_custom_call" | custom-call | flops 805306368 | bytes 14155776 | tf_op jit(solution)/shard_map/pallas_call | solution.py:289
  64.0 1.9 %shard_map.105 = (bf16[192,1024]{1,0:T(8,128)(2,1)S(1)}, bf16[192,2048]{1,0:T(8,128)(2,1)S(1)}, bf16[192,1024]{1,0:T(8,128)(2,1)S(1)}) custom-call(s32[1]{0:T(128)} %bitcast.1.idx_ref, f32[1,1024]{1,0:T(1,128)S(1)} %bitcast.7, bf16[384,1024]{1,0:T(8,128)(2,1)S(1)} %copy-done.2, bf16[384,1024]{1,0:T(8,128)(2,1)S(1)} %copy-done, ...), custom_call_target="tpu_custom_call" | custom-call | flops 805306368 | bytes 18350080 | tf_op jit(solution)/shard_map/pallas_call | solution.py:289
  69.5 2.6 %shard_map.107 = (f32[192,1024]{1,0:T(8,128)S(1)}, f32[192,1024]{1,0:T(8,128)S(1)}) custom-call(s32[1]{0:T(128)} %bitcast.group_ref, bf16[1024,4096]{1,0:T(8,128)(2,1)} %weight_ref.3, bf16[192,1024]{1,0:T(8,128)(2,1)S(1)} %get-tuple-element.78.refs_3_.refs_0_, bf16[192,1024]{1,0:T(8,128)(2,1)S(1)} %get-tuple-element.79.refs_1_.hid_ref, ...), custom_call_target="tpu_custom_call" | custom-call | bytes 1024 | tf_op jit(solution)/shard_map/pallas_call | solution.py:334
  72.1 6.4 %collective-permute-done.24.refs_1_ = bf16[192,1024]{1,0:T(8,128)(2,1)S(1)} collective-permute-done((bf16[192,1024]{1,0:T(8,128)(2,1)S(1)}, bf16[192,1024]{1,0:T(8,128)(2,1)S(1)}, u32[]{:S(2)}, u32[]{:S(2)}) %collective-permute-start.24) | collective-permute-done | bytes 393248 | tf_op jit(solution)/shard_map/ppermute | solution.py:450
  79.4 6.8 %collective-permute-done.23.refs_1_ = bf16[192,1024]{1,0:T(8,128)(2,1)} collective-permute-done((bf16[192,1024]{1,0:T(8,128)(2,1)S(1)}, bf16[192,1024]{1,0:T(8,128)(2,1)}, u32[]{:S(2)}, u32[]{:S(2)}) %collective-permute-start.23) | collective-permute-done | bytes 393248 | tf_op jit(solution)/shard_map/ppermute | solution.py:450
  86.1 1.8 %shard_map.110 = bf16[384,1024]{1,0:T(8,128)(2,1)} custom-call(f32[192,1024]{1,0:T(8,128)S(1)} %get-tuple-element.81.refs_0_, bf16[192,1024]{1,0:T(8,128)(2,1)} %collective-permute-done.23.refs_1_, bf16[384,1024]{1,0:T(8,128)(2,1)} %shard_map.109.refs_2_), custom_call_target="tpu_custom_call", output_to_operand_aliasing={{}: (2, {})} | custom-call | bytes 1024 | tf_op jit(solution)/shard_map/pallas_call | solution.py:376
  (52 shorter events, 15.3 us)
Async XLA Ops:
  1.3 11.3 %collective-permute-start = (bf16[384,128]{1,0:T(8,128)(2,1)S(1)}, bf16[384,128]{1,0:T(8,128)(2,1)S(1)}, u32[]{:S(2)}, u32[]{:S(2)}) collective-permute-start(bf16[384,128]{1,0:T(8,128)(2,1)S(1)} %get-tuple-element.47), channel_id=1, source_target_pairs={{0,4},{4,8},{8,12},{12,16},{16,20},{20,24},{24,28},{28,0},{1,5},{5... | collective-permute-start | bytes 294920 | tf_op jit(solution)/shard_map/ppermute | solution.py:144
  2.9 11.2 %collective-permute-start.1 = (bf16[384,128]{1,0:T(8,128)(2,1)S(1)}, bf16[384,128]{1,0:T(8,128)(2,1)S(1)}, u32[]{:S(2)}, u32[]{:S(2)}) collective-permute-start(bf16[384,128]{1,0:T(8,128)(2,1)S(1)} %get-tuple-element.48), channel_id=1, source_target_pairs={{0,8},{4,12},{8,16},{12,20},{16,24},{20,28},{24,0},{28,4},{1,9},{5... | collective-permute-start | bytes 294920 | tf_op jit(solution)/shard_map/ppermute | solution.py:144
  4.5 12.2 %collective-permute-start.2 = (bf16[384,128]{1,0:T(8,128)(2,1)S(1)}, bf16[384,128]{1,0:T(8,128)(2,1)S(1)}, u32[]{:S(2)}, u32[]{:S(2)}) collective-permute-start(bf16[384,128]{1,0:T(8,128)(2,1)S(1)} %get-tuple-element.49), channel_id=1, source_target_pairs={{0,12},{4,16},{8,20},{12,24},{16,28},{20,0},{24,4},{28,8},{1,13},{... | collective-permute-start | bytes 294920 | tf_op jit(solution)/shard_map/ppermute | solution.py:144
  5.7 12.2 %collective-permute-start.3 = (bf16[384,128]{1,0:T(8,128)(2,1)S(1)}, bf16[384,128]{1,0:T(8,128)(2,1)S(1)}, u32[]{:S(2)}, u32[]{:S(2)}) collective-permute-start(bf16[384,128]{1,0:T(8,128)(2,1)S(1)} %get-tuple-element.50), channel_id=1, source_target_pairs={{0,16},{4,20},{8,24},{12,28},{16,0},{20,4},{24,8},{28,12},{1,17},{... | collective-permute-start | bytes 294920 | tf_op jit(solution)/shard_map/ppermute | solution.py:144
  7.4 14.6 %collective-permute-start.4 = (bf16[384,128]{1,0:T(8,128)(2,1)S(1)}, bf16[384,128]{1,0:T(8,128)(2,1)S(1)}, u32[]{:S(2)}, u32[]{:S(2)}) collective-permute-start(bf16[384,128]{1,0:T(8,128)(2,1)S(1)} %get-tuple-element.51), channel_id=1, source_target_pairs={{0,20},{4,24},{8,28},{12,0},{16,4},{20,8},{24,12},{28,16},{1,21},{... | collective-permute-start | bytes 294920 | tf_op jit(solution)/shard_map/ppermute | solution.py:144
  12.7 12.6 %collective-permute-start.5 = (bf16[384,128]{1,0:T(8,128)(2,1)S(1)}, bf16[384,128]{1,0:T(8,128)(2,1)S(1)}, u32[]{:S(2)}, u32[]{:S(2)}) collective-permute-start(bf16[384,128]{1,0:T(8,128)(2,1)S(1)} %get-tuple-element.52), channel_id=1, source_target_pairs={{0,24},{4,28},{8,0},{12,4},{16,8},{20,12},{24,16},{28,20},{1,25},{... | collective-permute-start | bytes 294920 | tf_op jit(solution)/shard_map/ppermute | solution.py:144
  14.1 12.3 %collective-permute-start.6 = (bf16[384,128]{1,0:T(8,128)(2,1)S(1)}, bf16[384,128]{1,0:T(8,128)(2,1)S(1)}, u32[]{:S(2)}, u32[]{:S(2)}) collective-permute-start(bf16[384,128]{1,0:T(8,128)(2,1)S(1)} %get-tuple-element.53), channel_id=1, source_target_pairs={{0,28},{4,0},{8,4},{12,8},{16,12},{20,16},{24,20},{28,24},{1,29},{... | collective-permute-start | bytes 294920 | tf_op jit(solution)/shard_map/ppermute | solution.py:144
  16.7 13.7 %collective-permute-start.7 = (bf16[384,128]{1,0:T(8,128)(2,1)S(1)}, bf16[384,128]{1,0:T(8,128)(2,1)S(1)}, u32[]{:S(2)}, u32[]{:S(2)}) collective-permute-start(bf16[384,128]{1,0:T(8,128)(2,1)S(1)} %get-tuple-element.58), channel_id=1, source_target_pairs={{0,4},{4,8},{8,12},{12,16},{16,20},{20,24},{24,28},{28,0},{1,5},{5... | collective-permute-start | bytes 294920 | tf_op jit(solution)/shard_map/ppermute | solution.py:144
  17.9 15.1 %collective-permute-start.8 = (bf16[384,128]{1,0:T(8,128)(2,1)S(1)}, bf16[384,128]{1,0:T(8,128)(2,1)S(1)}, u32[]{:S(2)}, u32[]{:S(2)}) collective-permute-start(bf16[384,128]{1,0:T(8,128)(2,1)S(1)} %get-tuple-element.59), channel_id=1, source_target_pairs={{0,8},{4,12},{8,16},{12,20},{16,24},{20,28},{24,0},{28,4},{1,9},{5... | collective-permute-start | bytes 294920 | tf_op jit(solution)/shard_map/ppermute | solution.py:144
  21.9 14.0 %collective-permute-start.9 = (bf16[384,128]{1,0:T(8,128)(2,1)S(1)}, bf16[384,128]{1,0:T(8,128)(2,1)S(1)}, u32[]{:S(2)}, u32[]{:S(2)}) collective-permute-start(bf16[384,128]{1,0:T(8,128)(2,1)S(1)} %get-tuple-element.60), channel_id=1, source_target_pairs={{0,12},{4,16},{8,20},{12,24},{16,28},{20,0},{24,4},{28,8},{1,13},{... | collective-permute-start | bytes 294920 | tf_op jit(solution)/shard_map/ppermute | solution.py:144
  25.2 10.7 %collective-permute-start.10 = (bf16[384,128]{1,0:T(8,128)(2,1)S(1)}, bf16[384,128]{1,0:T(8,128)(2,1)S(1)}, u32[]{:S(2)}, u32[]{:S(2)}) collective-permute-start(bf16[384,128]{1,0:T(8,128)(2,1)S(1)} %get-tuple-element.61), channel_id=1, source_target_pairs={{0,16},{4,20},{8,24},{12,28},{16,0},{20,4},{24,8},{28,12},{1,17},{... | collective-permute-start | bytes 294920 | tf_op jit(solution)/shard_map/ppermute | solution.py:144
  26.3 10.9 %collective-permute-start.11 = (bf16[384,128]{1,0:T(8,128)(2,1)S(1)}, bf16[384,128]{1,0:T(8,128)(2,1)S(1)}, u32[]{:S(2)}, u32[]{:S(2)}) collective-permute-start(bf16[384,128]{1,0:T(8,128)(2,1)S(1)} %get-tuple-element.62), channel_id=1, source_target_pairs={{0,20},{4,24},{8,28},{12,0},{16,4},{20,8},{24,12},{28,16},{1,21},{... | collective-permute-start | bytes 294920 | tf_op jit(solution)/shard_map/ppermute | solution.py:144
  30.4 7.0 %collective-permute-start.12 = (bf16[384,128]{1,0:T(8,128)(2,1)S(1)}, bf16[384,128]{1,0:T(8,128)(2,1)S(1)}, u32[]{:S(2)}, u32[]{:S(2)}) collective-permute-start(bf16[384,128]{1,0:T(8,128)(2,1)S(1)} %get-tuple-element.63), channel_id=1, source_target_pairs={{0,24},{4,28},{8,0},{12,4},{16,8},{20,12},{24,16},{28,20},{1,25},{... | collective-permute-start | bytes 294920 | tf_op jit(solution)/shard_map/ppermute | solution.py:144
  32.9 5.6 %collective-permute-start.13 = (bf16[384,128]{1,0:T(8,128)(2,1)S(1)}, bf16[384,128]{1,0:T(8,128)(2,1)S(1)}, u32[]{:S(2)}, u32[]{:S(2)}) collective-permute-start(bf16[384,128]{1,0:T(8,128)(2,1)S(1)} %get-tuple-element.64), channel_id=1, source_target_pairs={{0,28},{4,0},{8,4},{12,8},{16,12},{20,16},{24,20},{28,24},{1,29},{... | collective-permute-start | bytes 294920 | tf_op jit(solution)/shard_map/ppermute | solution.py:144
  41.6 9.3 %collective-permute-start.14 = (bf16[384,128]{1,0:T(8,128)(2,1)S(1)}, bf16[384,128]{1,0:T(8,128)(2,1)S(1)}, u32[]{:S(2)}, u32[]{:S(2)}) collective-permute-start(bf16[384,128]{1,0:T(8,128)(2,1)S(1)} %get-tuple-element.66), channel_id=1, source_target_pairs={{0,4},{4,8},{8,12},{12,16},{16,20},{20,24},{24,28},{28,0},{1,5},{5... | collective-permute-start | bytes 294920 | tf_op jit(solution)/shard_map/ppermute | solution.py:144
  42.9 8.5 %collective-permute-start.15 = (bf16[384,128]{1,0:T(8,128)(2,1)S(1)}, bf16[384,128]{1,0:T(8,128)(2,1)S(1)}, u32[]{:S(2)}, u32[]{:S(2)}) collective-permute-start(bf16[384,128]{1,0:T(8,128)(2,1)S(1)} %get-tuple-element.67), channel_id=1, source_target_pairs={{0,8},{4,12},{8,16},{12,20},{16,24},{20,28},{24,0},{28,4},{1,9},{5... | collective-permute-start | bytes 294920 | tf_op jit(solution)/shard_map/ppermute | solution.py:144
  45.5 13.2 %collective-permute-start.16 = (bf16[384,128]{1,0:T(8,128)(2,1)S(1)}, bf16[384,128]{1,0:T(8,128)(2,1)S(1)}, u32[]{:S(2)}, u32[]{:S(2)}) collective-permute-start(bf16[384,128]{1,0:T(8,128)(2,1)S(1)} %get-tuple-element.68), channel_id=1, source_target_pairs={{0,12},{4,16},{8,20},{12,24},{16,28},{20,0},{24,4},{28,8},{1,13},{... | collective-permute-start | bytes 294920 | tf_op jit(solution)/shard_map/ppermute | solution.py:144
  46.8 11.9 %collective-permute-start.17 = (bf16[384,128]{1,0:T(8,128)(2,1)S(1)}, bf16[384,128]{1,0:T(8,128)(2,1)S(1)}, u32[]{:S(2)}, u32[]{:S(2)}) collective-permute-start(bf16[384,128]{1,0:T(8,128)(2,1)S(1)} %get-tuple-element.69), channel_id=1, source_target_pairs={{0,16},{4,20},{8,24},{12,28},{16,0},{20,4},{24,8},{28,12},{1,17},{... | collective-permute-start | bytes 294920 | tf_op jit(solution)/shard_map/ppermute | solution.py:144
  47.0 11.8 %collective-permute-start.18 = (bf16[384,128]{1,0:T(8,128)(2,1)S(1)}, bf16[384,128]{1,0:T(8,128)(2,1)S(1)}, u32[]{:S(2)}, u32[]{:S(2)}) collective-permute-start(bf16[384,128]{1,0:T(8,128)(2,1)S(1)} %get-tuple-element.70), channel_id=1, source_target_pairs={{0,20},{4,24},{8,28},{12,0},{16,4},{20,8},{24,12},{28,16},{1,21},{... | collective-permute-start | bytes 294920 | tf_op jit(solution)/shard_map/ppermute | solution.py:144
  50.8 9.4 %collective-permute-start.19 = (bf16[384,128]{1,0:T(8,128)(2,1)S(1)}, bf16[384,128]{1,0:T(8,128)(2,1)S(1)}, u32[]{:S(2)}, u32[]{:S(2)}) collective-permute-start(bf16[384,128]{1,0:T(8,128)(2,1)S(1)} %get-tuple-element.71), channel_id=1, source_target_pairs={{0,24},{4,28},{8,0},{12,4},{16,8},{20,12},{24,16},{28,20},{1,25},{... | collective-permute-start | bytes 294920 | tf_op jit(solution)/shard_map/ppermute | solution.py:144
  51.4 11.0 %collective-permute-start.20 = (bf16[384,128]{1,0:T(8,128)(2,1)S(1)}, bf16[384,128]{1,0:T(8,128)(2,1)S(1)}, u32[]{:S(2)}, u32[]{:S(2)}) collective-permute-start(bf16[384,128]{1,0:T(8,128)(2,1)S(1)} %get-tuple-element.72), channel_id=1, source_target_pairs={{0,28},{4,0},{8,4},{12,8},{16,12},{20,16},{24,20},{28,24},{1,29},{... | collective-permute-start | bytes 294920 | tf_op jit(solution)/shard_map/ppermute | solution.py:144
  63.9 2.5 %collective-permute-start.21 = (bf16[192,2048]{1,0:T(8,128)(2,1)S(1)}, bf16[192,2048]{1,0:T(8,128)(2,1)S(1)}, u32[]{:S(2)}, u32[]{:S(2)}) collective-permute-start(bf16[192,2048]{1,0:T(8,128)(2,1)S(1)} %get-tuple-element.77), channel_id=1, source_target_pairs={{0,1},{1,0},{2,3},{3,2},{4,5},{5,4},{6,7},{7,6},{8,9},{9,8},{10,11... | collective-permute-start | bytes 2359304 | tf_op jit(solution)/shard_map/ppermute | solution.py:462
  66.5 12.0 %collective-permute-start.24 = (bf16[192,1024]{1,0:T(8,128)(2,1)S(1)}, bf16[192,1024]{1,0:T(8,128)(2,1)S(1)}, u32[]{:S(2)}, u32[]{:S(2)}) collective-permute-start(bf16[192,1024]{1,0:T(8,128)(2,1)S(1)} %shard_map.106), channel_id=1, source_target_pairs={{0,2},{1,3},{2,0},{3,1},{4,6},{5,7},{6,4},{7,5},{8,10},{9,11},{10,... | collective-permute-start | bytes 1179656 | tf_op jit(solution)/shard_map/ppermute | solution.py:450
  68.9 17.2 %collective-permute-start.23 = (bf16[192,1024]{1,0:T(8,128)(2,1)S(1)}, bf16[192,1024]{1,0:T(8,128)(2,1)}, u32[]{:S(2)}, u32[]{:S(2)}) collective-permute-start(bf16[192,1024]{1,0:T(8,128)(2,1)S(1)} %shard_map.108), channel_id=1, source_target_pairs={{0,2},{1,3},{2,0},{3,1},{4,6},{5,7},{6,4},{7,5},{8,10},{9,11},{10,... | collective-permute-start | bytes 1179656 | tf_op jit(solution)/shard_map/ppermute | solution.py:450
  (8 other events, 129.0 us)

commit v4 on v3

--- a/solution.py
+++ b/solution.py
@@ -296,15 +296,15 @@
     )(*arrays, *pinned, *blocks)
 
 
-def own_kernel(hid_ref, weight_ref, crossed_ref, out_ref):
-    times_columns(hid_ref, weight_ref, out_ref, crossed_ref.at[:, : out_ref.shape[1]])
-
-
-def own_product(hidden, weight, crossed):
+def own_kernel(hid_ref, weight_ref, crossed_ref, out_ref, *, at):
+    times_columns(hid_ref, weight_ref, out_ref, crossed_ref.at[:, at : at + out_ref.shape[1]])
+
+
+def own_product(hidden, weight, crossed, at=0):
     rows, channels = hidden.shape
     columns = weight.shape[1]
     return pl.pallas_call(
-        own_kernel,
+        functools.partial(own_kernel, at=at),
         out_shape=pltpu.VMEM((rows, columns), BF16),
         in_specs=[VMEM] * 3,
         out_specs=VMEM,
@@ -315,33 +315,6 @@
     )(*(pltpu.with_memory_space_constraint(a, pltpu.VMEM) for a in (hidden, weight, crossed)))
 
 
-def late_kernel(group_ref, weight_ref, *refs, pieces, at):
-    hids, extras = refs[:pieces], refs[pieces : 2 * pieces]
-    parts, (held, sem) = refs[2 * pieces : -2], refs[-2:]
-    width = held.shape[1]
-    cols = pl.ds(pl.multiple_of(group_ref[0] * width, width), width)
-    copy = pltpu.make_async_copy(weight_ref.at[:, cols], held, sem)
-    copy.start()
-    copy.wait()
-    for r in range(pieces):
-        times_columns(hids[r], held, parts[r], extras[r].at[:, at : at + width])
-
-
-def late_product(group, hidden, weight, groups, extra, at, dtype):
-    pieces = len(hidden)
-    channels, width = weight.shape[0], weight.shape[1] // groups
-    rows = sum(h.shape[0] for h in hidden)
-    return pl.pallas_call(
-        functools.partial(late_kernel, pieces=pieces, at=at),
-        out_shape=[pltpu.VMEM((h.shape[0], width), dtype) for h in hidden],
-        in_specs=[SMEM, HBM] + [VMEM] * (2 * pieces),
-        out_specs=[VMEM] * pieces,
-        scratch_shapes=[pltpu.VMEM((channels, width), BF16), pltpu.SemaphoreType.DMA],
-        compiler_params=params(2 * channels * width + 2 * rows * channels + 2 * rows * weight.shape[1] + 6 * rows * width),
-        cost_estimate=pl.CostEstimate(flops=0, bytes_accessed=channels, transcendentals=0),
-    )(group, pltpu.with_memory_space_constraint(weight, pltpu.HBM), *hidden, *extra)
-
-
 def add_kernel(own_ref, other_ref, out_ref):
     other = other_ref[:, : own_ref.shape[1]].astype(F32)
     out_ref[...] = (own_ref[...].astype(F32) + other).astype(BF16)
@@ -356,6 +329,25 @@
         compiler_params=params(4 * own.size + 2 * other.size),
         cost_estimate=pl.CostEstimate(flops=own.size, bytes_accessed=6 * own.size, transcendentals=0),
     )(own, pltpu.with_memory_space_constraint(other, pltpu.VMEM))
+
+
+def last_kernel(weight_ref, *refs, pieces, at):
+    hids, extras, parts = refs[:pieces], refs[pieces : 2 * pieces], refs[2 * pieces :]
+    for hid_ref, extra_ref, part_ref in zip(hids, extras, parts):
+        times_columns(hid_ref, weight_ref, part_ref, extra_ref.at[:, at : at + part_ref.shape[1]])
+
+
+def last_products(hidden, weight, crossed, at):
+    channels, columns = weight.shape
+    rows = sum(h.shape[0] for h in hidden)
+    return pl.pallas_call(
+        functools.partial(last_kernel, pieces=len(hidden), at=at),
+        out_shape=[pltpu.VMEM((h.shape[0], columns), F32) for h in hidden],
+        in_specs=[VMEM] * (1 + 2 * len(hidden)),
+        out_specs=[VMEM] * len(hidden),
+        compiler_params=params(2 * weight.size + 2 * rows * channels + 2 * sum(c.size for c in crossed) + 4 * rows * columns),
+        cost_estimate=pl.CostEstimate(flops=0, bytes_accessed=channels, transcendentals=0),
+    )(*(pltpu.with_memory_space_constraint(a, pltpu.VMEM) for a in (weight, *hidden, *crossed)))
 
 
 def finish_kernel(*refs, at, terms):
@@ -410,7 +402,7 @@
 
     filter_in = exchange(filter_slices(idx, long_filter, count), "ctx", count)
     steps = list(range(1, chips)) + [0]
-    order = jnp.stack([group_of(step, 1 - core) for step in steps] + [group_of(1, core)])
+    order = jnp.stack([group_of(step, which) for which in (1 - core, core) for step in steps])
     slices, weights = gated_slices(idx, key_k, value_v, count, order, out_weight, groups)
     gated_in = exchange(slices, "ctx", count)
     spectrum, mid, back = pl.pallas_call(
@@ -457,26 +449,20 @@
             conv = lax.dynamic_update_slice_in_dim(conv, conv_in[s], src * width, 1)
         idx, conv_in = jnp.zeros_like(idx), [conv]
     arrays = [idx, gain, gate_q, key_k, value_v]
-    *others, own = weights
+    others, owns = weights[:chips], weights[chips:]
+    columns = owns[0].shape[1]
     hid_first, part_first = hidden_products(arrays, others, conv_in, 0, lead)
     crossed = [lax.ppermute(part_first, "ch", swap)]
-    hid_rest, part_rest, sums = hidden_products(arrays, others, conv_in, lead, rows - lead, (own, hid_first))
+    hid_rest, part_rest, sums = hidden_products(arrays, others, conv_in, lead, rows - lead, (owns[0], hid_first))
     crossed.append(lax.ppermute(part_rest, "ch", swap))
-    hidden = [hid_first, hid_rest]
-    first_total = add(sums, crossed[0])
-    arrived = [[to_chip(first_total, 1)], [to_chip(own_product(hid_rest, own, crossed[1]), 1)]]
-    later = list(lax.optimization_barrier((*hidden, first_total))[:2])
+    arrived = [[to_chip(add(sums, crossed[0]), 1)], [to_chip(own_product(hid_rest, owns[0], crossed[1]), 1)]]
     for j, step in enumerate(steps[1:-1]):
-        totals = late_product(
-            group_of(step, core).reshape(1), later, out_weight, groups, crossed, (j + 1) * own.shape[1], BF16
-        )
-        for got, total in zip(arrived, totals):
-            got.append(to_chip(total, step))
-    last_sums = late_product(
-        group_of(0, core).reshape(1), later, out_weight, groups, crossed, (chips - 1) * own.shape[1], F32
-    )
-    first_rows = finish([last_sums[0]] + arrived[0], 0, rows, None)
-    return finish([last_sums[1]] + arrived[1], lead, rows, first_rows)
+        for got, hid, cross in zip(arrived, (hid_first, hid_rest), crossed):
+            got.append(to_chip(own_product(hid, owns[j + 1], cross, (j + 1) * columns), step))
+    last = (chips - 1) * columns
+    sums = last_products((hid_first, hid_rest), owns[-1], crossed, last)
+    out = finish([sums[0]] + arrived[0], 0, rows, None)
+    return finish([sums[1]] + arrived[1], lead, rows, out)
 
 
 def solution(mesh):

time: 89.8 us -> 88.2 us (0.982)
  Pallas kernels: 19.5 us -> 17.5 us
  waiting for transfers between devices: 20.6 us -> 21.9 us
  starting transfers between devices: 46.5 us -> 45.5 us
    pallas_call x2, Pallas kernels: 3.2 us -> 1.6 us  [the longest x1 1 us: last_products(): pl.pallas_call(functools.partial(last_kernel, pieces=len(hidden), at=at),...]
    ppermute x2, waiting for transfers between devices: 13.2 us -> 14.7 us  [to_chip(): lax.ppermute(part, 'ch', [(i, (i + 2 * step) % groups) for i in range(gro...]
    ppermute x21, starting transfers between devices: 44.7 us -> 43.7 us  [exchange(): lax.ppermute(blocks[s], axis, [(i, (i + s) % count) for i in range(count)])]
    pallas_call x2, Pallas kernels: 2.65 us -> 1.68 us  [finish(): pl.pallas_call(functools.partial(finish_kernel, at=at, terms=len(values))...]
  transfers between devices with their start and end apart: 25 -> 25, of which waited for: 8 -> 7; matrix products, arithmetic and copies ran while one was open for 0% -> 0% of each run, Pallas kernels for 15% -> 14%
where the time goes in v4:
time: 88.2 us; the launch traced here: 86.4 us
  starting transfers between devices  45.5 us (52%)
  waiting for transfers between devices  21.9 us (25%)
  Pallas kernels  17.5 us (20%)
  local copies, waits for them, and re-layouts  1.16 us (1%)
    ppermute x21, starting transfers between devices, exchange(): lax.ppermute(blocks[s], axis, [(i, (i + s) % count) for i in range(count)])  43.7 us
    ppermute x2, waiting for transfers between devices, to_chip(): lax.ppermute(part, 'ch', [(i, (i + 2 * step) % groups) for i in range(gro...  14.7 us
    ppermute x21, waiting for transfers between devices, exchange(): lax.ppermute(blocks[s], axis, [(i, (i + s) % count) for i in range(count)])  5.93 us
    pallas_call x1, Pallas kernels, gated_slices(): pl.pallas_call(functools.partial(gate_kernel, count=count), out_shape=[ja...  4.54 us
    pallas_call x2, Pallas kernels, hidden_products(): pl.pallas_call(functools.partial(rows_kernel, at=at, others=len(weights),...  3.32 us
    pallas_call x1, Pallas kernels, local(): pl.pallas_call(functools.partial(conv_kernel, count=count), out_shape=[ja...  3.07 us
    pallas_call x1, Pallas kernels, local(): pl.pallas_call(functools.partial(filter_kernel, count=count), out_shape=[...  2.98 us
  transfers between devices with their start and end apart: 25, of which 7 were waited for; matrix products, arithmetic and copies ran while one was open for 0% of the time, Pallas kernels for 14%

profile of v4, /device:TPU:20, one launch (start us, length us, event | category | flops | bytes accessed | tf_op | source)
XLA Modules:
  0.0 86.4 jit_solution(1432986682534233334)
XLA Ops:
  1.3 1.5 %collective-permute-start = (bf16[384,128]{1,0:T(8,128)(2,1)S(1)}, bf16[384,128]{1,0:T(8,128)(2,1)S(1)}, u32[]{:S(2)}, u32[]{:S(2)}) collective-permute-start(bf16[384,128]{1,0:T(8,128)(2,1)S(1)} %get-tuple-element.47), channel_id=1, source_target_pairs={{0,4},{4,8},{8,12},{12,16},{16,20},{20,24},{24,28},{28,0},{1,5},{5... | collective-permute-start | bytes 294920 | tf_op jit(solution)/shard_map/ppermute | solution.py:144
  2.9 1.6 %collective-permute-start.1 = (bf16[384,128]{1,0:T(8,128)(2,1)S(1)}, bf16[384,128]{1,0:T(8,128)(2,1)S(1)}, u32[]{:S(2)}, u32[]{:S(2)}) collective-permute-start(bf16[384,128]{1,0:T(8,128)(2,1)S(1)} %get-tuple-element.48), channel_id=1, source_target_pairs={{0,8},{4,12},{8,16},{12,20},{16,24},{20,28},{24,0},{28,4},{1,9},{5... | collective-permute-start | bytes 294920 | tf_op jit(solution)/shard_map/ppermute | solution.py:144
  5.7 1.7 %collective-permute-start.3 = (bf16[384,128]{1,0:T(8,128)(2,1)S(1)}, bf16[384,128]{1,0:T(8,128)(2,1)S(1)}, u32[]{:S(2)}, u32[]{:S(2)}) collective-permute-start(bf16[384,128]{1,0:T(8,128)(2,1)S(1)} %get-tuple-element.50), channel_id=1, source_target_pairs={{0,16},{4,20},{8,24},{12,28},{16,0},{20,4},{24,8},{28,12},{1,17},{... | collective-permute-start | bytes 294920 | tf_op jit(solution)/shard_map/ppermute | solution.py:144
  7.4 1.3 %collective-permute-start.4 = (bf16[384,128]{1,0:T(8,128)(2,1)S(1)}, bf16[384,128]{1,0:T(8,128)(2,1)S(1)}, u32[]{:S(2)}, u32[]{:S(2)}) collective-permute-start(bf16[384,128]{1,0:T(8,128)(2,1)S(1)} %get-tuple-element.51), channel_id=1, source_target_pairs={{0,20},{4,24},{8,28},{12,0},{16,4},{20,8},{24,12},{28,16},{1,21},{... | collective-permute-start | bytes 294920 | tf_op jit(solution)/shard_map/ppermute | solution.py:144
  8.7 4.5 %shard_map.100 = (bf16[384,128]{1,0:T(8,128)(2,1)S(1)}, bf16[384,128]{1,0:T(8,128)(2,1)S(1)}, bf16[384,128]{1,0:T(8,128)(2,1)S(1)}, bf16[384,128]{1,0:T(8,128)(2...) custom-call(s32[1]{0:T(128)} %bitcast.idx_ref, ...), custom_call_target="tpu_custom_call" | custom-call | flops 393216 | bytes 11534336 | tf_op jit(solution)/shard_map/pallas_call | solution.py:122
  13.3 1.4 %collective-permute-start.5 = (bf16[384,128]{1,0:T(8,128)(2,1)S(1)}, bf16[384,128]{1,0:T(8,128)(2,1)S(1)}, u32[]{:S(2)}, u32[]{:S(2)}) collective-permute-start(bf16[384,128]{1,0:T(8,128)(2,1)S(1)} %get-tuple-element.52), channel_id=1, source_target_pairs={{0,24},{4,28},{8,0},{12,4},{16,8},{20,12},{24,16},{28,20},{1,25},{... | collective-permute-start | bytes 294920 | tf_op jit(solution)/shard_map/ppermute | solution.py:144
  14.7 1.4 %collective-permute-start.6 = (bf16[384,128]{1,0:T(8,128)(2,1)S(1)}, bf16[384,128]{1,0:T(8,128)(2,1)S(1)}, u32[]{:S(2)}, u32[]{:S(2)}) collective-permute-start(bf16[384,128]{1,0:T(8,128)(2,1)S(1)} %get-tuple-element.53), channel_id=1, source_target_pairs={{0,28},{4,0},{8,4},{12,8},{16,12},{20,16},{24,20},{28,24},{1,29},{... | collective-permute-start | bytes 294920 | tf_op jit(solution)/shard_map/ppermute | solution.py:144
  16.8 4.6 %collective-permute-start.8 = (bf16[384,128]{1,0:T(8,128)(2,1)S(1)}, bf16[384,128]{1,0:T(8,128)(2,1)S(1)}, u32[]{:S(2)}, u32[]{:S(2)}) collective-permute-start(bf16[384,128]{1,0:T(8,128)(2,1)S(1)} %get-tuple-element.59), channel_id=1, source_target_pairs={{0,8},{4,12},{8,16},{12,20},{16,24},{20,28},{24,0},{28,4},{1,9},{5... | collective-permute-start | bytes 294920 | tf_op jit(solution)/shard_map/ppermute | solution.py:144
  21.4 3.8 %collective-permute-start.9 = (bf16[384,128]{1,0:T(8,128)(2,1)S(1)}, bf16[384,128]{1,0:T(8,128)(2,1)S(1)}, u32[]{:S(2)}, u32[]{:S(2)}) collective-permute-start(bf16[384,128]{1,0:T(8,128)(2,1)S(1)} %get-tuple-element.60), channel_id=1, source_target_pairs={{0,12},{4,16},{8,20},{12,24},{16,28},{20,0},{24,4},{28,8},{1,13},{... | collective-permute-start | bytes 294920 | tf_op jit(solution)/shard_map/ppermute | solution.py:144
  25.8 2.7 %collective-permute-start.11 = (bf16[384,128]{1,0:T(8,128)(2,1)S(1)}, bf16[384,128]{1,0:T(8,128)(2,1)S(1)}, u32[]{:S(2)}, u32[]{:S(2)}) collective-permute-start(bf16[384,128]{1,0:T(8,128)(2,1)S(1)} %get-tuple-element.62), channel_id=1, source_target_pairs={{0,20},{4,24},{8,28},{12,0},{16,4},{20,8},{24,12},{28,16},{1,21},{... | collective-permute-start | bytes 294920 | tf_op jit(solution)/shard_map/ppermute | solution.py:144
  28.5 4.1 %collective-permute-start.12 = (bf16[384,128]{1,0:T(8,128)(2,1)S(1)}, bf16[384,128]{1,0:T(8,128)(2,1)S(1)}, u32[]{:S(2)}, u32[]{:S(2)}) collective-permute-start(bf16[384,128]{1,0:T(8,128)(2,1)S(1)} %get-tuple-element.63), channel_id=1, source_target_pairs={{0,24},{4,28},{8,0},{12,4},{16,8},{20,12},{24,16},{28,20},{1,25},{... | collective-permute-start | bytes 294920 | tf_op jit(solution)/shard_map/ppermute | solution.py:144
  32.6 3.0 %shard_map.102 = (bf16[24,256,128]{2,1,0:T(8,128)(2,1)S(1)}, bf16[24,256,256]{2,1,0:T(8,128)(2,1)S(1)}, bf16[24,256,256]{2,1,0:T(8,128)(2,1)S(1)}) custom-call(s32[1]{0:T(128)} %bitcast.idx_ref, bf16[384,192]{1,0:T(8,128)(2,1)S(1)} %copy-done.5, bf16[24,256,256]{2,1,0:T(8,128)(2,1)} %constant.47.clone.mid_hbm, ...), custom_call_target="tpu_custom_call" | custom-call | flops 3000000000 | bytes 8000000 | tf_op jit(solution)/shard_map/pallas_call | solution.py:408
  35.6 1.3 %collective-permute-done.11.refs_5_ = bf16[384,128]{1,0:T(8,128)(2,1)S(1)} collective-permute-done((bf16[384,128]{1,0:T(8,128)(2,1)S(1)}, bf16[384,128]{1,0:T(8,128)(2,1)S(1)}, u32[]{:S(2)}, u32[]{:S(2)}) %collective-permute-start.11) | collective-permute-done | bytes 98336 | tf_op jit(solution)/shard_map/ppermute | solution.py:144
  37.9 3.1 %shard_map.103 = (bf16[384,128]{1,0:T(8,128)(2,1)S(1)}, bf16[384,128]{1,0:T(8,128)(2,1)S(1)}, bf16[384,128]{1,0:T(8,128)(2,1)S(1)}, bf16[384,128]{1,0:T(8,128)(2...) custom-call(s32[1]{0:T(128)} %bitcast.idx_ref, ...), custom_call_target="tpu_custom_call" | custom-call | flops 6000000000 | bytes 12000000 | tf_op jit(solution)/shard_map/pallas_call | solution.py:427
  41.0 1.6 %collective-permute-start.14 = (bf16[384,128]{1,0:T(8,128)(2,1)S(1)}, bf16[384,128]{1,0:T(8,128)(2,1)S(1)}, u32[]{:S(2)}, u32[]{:S(2)}) collective-permute-start(bf16[384,128]{1,0:T(8,128)(2,1)S(1)} %get-tuple-element.66), channel_id=1, source_target_pairs={{0,4},{4,8},{8,12},{12,16},{16,20},{20,24},{24,28},{28,0},{1,5},{5... | collective-permute-start | bytes 294920 | tf_op jit(solution)/shard_map/ppermute | solution.py:144
  42.6 2.7 %collective-permute-start.15 = (bf16[384,128]{1,0:T(8,128)(2,1)S(1)}, bf16[384,128]{1,0:T(8,128)(2,1)S(1)}, u32[]{:S(2)}, u32[]{:S(2)}) collective-permute-start(bf16[384,128]{1,0:T(8,128)(2,1)S(1)} %get-tuple-element.67), channel_id=1, source_target_pairs={{0,8},{4,12},{8,16},{12,20},{16,24},{20,28},{24,0},{28,4},{1,9},{5... | collective-permute-start | bytes 294920 | tf_op jit(solution)/shard_map/ppermute | solution.py:144
  46.5 3.8 %collective-permute-start.18 = (bf16[384,128]{1,0:T(8,128)(2,1)S(1)}, bf16[384,128]{1,0:T(8,128)(2,1)S(1)}, u32[]{:S(2)}, u32[]{:S(2)}) collective-permute-start(bf16[384,128]{1,0:T(8,128)(2,1)S(1)} %get-tuple-element.70), channel_id=1, source_target_pairs={{0,20},{4,24},{8,28},{12,0},{16,4},{20,8},{24,12},{28,16},{1,21},{... | collective-permute-start | bytes 294920 | tf_op jit(solution)/shard_map/ppermute | solution.py:144
  50.8 7.4 %collective-permute-start.20 = (bf16[384,128]{1,0:T(8,128)(2,1)S(1)}, bf16[384,128]{1,0:T(8,128)(2,1)S(1)}, u32[]{:S(2)}, u32[]{:S(2)}) collective-permute-start(bf16[384,128]{1,0:T(8,128)(2,1)S(1)} %get-tuple-element.72), channel_id=1, source_target_pairs={{0,28},{4,0},{8,4},{12,8},{16,12},{20,16},{24,20},{28,24},{1,29},{... | collective-permute-start | bytes 294920 | tf_op jit(solution)/shard_map/ppermute | solution.py:144
  58.2 1.7 %collective-permute-done.19.refs_8_.refs_10_ = bf16[384,128]{1,0:T(8,128)(2,1)S(1)} collective-permute-done((bf16[384,128]{1,0:T(8,128)(2,1)S(1)}, bf16[384,128]{1,0:T(8,128)(2,1)S(1)}, u32[]{:S(2)}, u32[]{:S(2)}) %collective-permute-start.19) | collective-permute-done | bytes 98336 | tf_op jit(solution)/shard_map/ppermute | solution.py:144
  59.9 1.9 %collective-permute-done.20.refs_9_.refs_11_ = bf16[384,128]{1,0:T(8,128)(2,1)S(1)} collective-permute-done((bf16[384,128]{1,0:T(8,128)(2,1)S(1)}, bf16[384,128]{1,0:T(8,128)(2,1)S(1)}, u32[]{:S(2)}, u32[]{:S(2)}) %collective-permute-start.20) | collective-permute-done | bytes 98336 | tf_op jit(solution)/shard_map/ppermute | solution.py:144
  61.8 1.4 %shard_map.104 = (bf16[192,1024]{1,0:T(8,128)(2,1)S(1)}, bf16[192,2048]{1,0:T(8,128)(2,1)S(1)}) custom-call(s32[1]{0:T(128)} %bitcast.idx_ref, f32[1,1024]{1,0:T(1,128)S(1)} %bitcast.6, bf16[384,1024]{1,0:T(8,128)(2,1)S(1)} %copy-done.2, bf16[384,1024]{1,0:T(8,128)(2,1)S(1)} %copy-done, bf16[384,1024]{1,0:T(8,128)(2,1)S(1)} %copy-done.1, ...), custom_call_target="tpu_custom_call" | custom-call | flops 805306368 | bytes 14155776 | tf_op jit(solution)/shard_map/pallas_call | solution.py:289
  63.4 1.9 %shard_map.105 = (bf16[192,1024]{1,0:T(8,128)(2,1)S(1)}, bf16[192,2048]{1,0:T(8,128)(2,1)S(1)}, bf16[192,1024]{1,0:T(8,128)(2,1)S(1)}) custom-call(s32[1]{0:T(128)} %bitcast.idx_ref, f32[1,1024]{1,0:T(1,128)S(1)} %bitcast.7, bf16[384,1024]{1,0:T(8,128)(2,1)S(1)} %copy-done.2, bf16[384,1024]{1,0:T(8,128)(2,1)S(1)} %copy-done, ...), custom_call_target="tpu_custom_call" | custom-call | flops 805306368 | bytes 18350080 | tf_op jit(solution)/shard_map/pallas_call | solution.py:289
  69.9 8.0 %collective-permute-done.24.refs_1_ = bf16[192,1024]{1,0:T(8,128)(2,1)S(1)} collective-permute-done((bf16[192,1024]{1,0:T(8,128)(2,1)S(1)}, bf16[192,1024]{1,0:T(8,128)(2,1)S(1)}, u32[]{:S(2)}, u32[]{:S(2)}) %collective-permute-start.24) | collective-permute-done | bytes 393248 | tf_op jit(solution)/shard_map/ppermute | solution.py:442
  78.8 6.7 %collective-permute-done.23.refs_1_ = bf16[192,1024]{1,0:T(8,128)(2,1)S(1)} collective-permute-done((bf16[192,1024]{1,0:T(8,128)(2,1)S(1)}, bf16[192,1024]{1,0:T(8,128)(2,1)S(1)}, u32[]{:S(2)}, u32[]{:S(2)}) %collective-permute-start.23) | collective-permute-done | bytes 393248 | tf_op jit(solution)/shard_map/ppermute | solution.py:442
  (52 shorter events, 13.0 us)
Async XLA Ops:
  1.3 11.9 %collective-permute-start = (bf16[384,128]{1,0:T(8,128)(2,1)S(1)}, bf16[384,128]{1,0:T(8,128)(2,1)S(1)}, u32[]{:S(2)}, u32[]{:S(2)}) collective-permute-start(bf16[384,128]{1,0:T(8,128)(2,1)S(1)} %get-tuple-element.47), channel_id=1, source_target_pairs={{0,4},{4,8},{8,12},{12,16},{16,20},{20,24},{24,28},{28,0},{1,5},{5... | collective-permute-start | bytes 294920 | tf_op jit(solution)/shard_map/ppermute | solution.py:144
  2.9 11.8 %collective-permute-start.1 = (bf16[384,128]{1,0:T(8,128)(2,1)S(1)}, bf16[384,128]{1,0:T(8,128)(2,1)S(1)}, u32[]{:S(2)}, u32[]{:S(2)}) collective-permute-start(bf16[384,128]{1,0:T(8,128)(2,1)S(1)} %get-tuple-element.48), channel_id=1, source_target_pairs={{0,8},{4,12},{8,16},{12,20},{16,24},{20,28},{24,0},{28,4},{1,9},{5... | collective-permute-start | bytes 294920 | tf_op jit(solution)/shard_map/ppermute | solution.py:144
  4.5 11.6 %collective-permute-start.2 = (bf16[384,128]{1,0:T(8,128)(2,1)S(1)}, bf16[384,128]{1,0:T(8,128)(2,1)S(1)}, u32[]{:S(2)}, u32[]{:S(2)}) collective-permute-start(bf16[384,128]{1,0:T(8,128)(2,1)S(1)} %get-tuple-element.49), channel_id=1, source_target_pairs={{0,12},{4,16},{8,20},{12,24},{16,28},{20,0},{24,4},{28,8},{1,13},{... | collective-permute-start | bytes 294920 | tf_op jit(solution)/shard_map/ppermute | solution.py:144
  5.7 11.1 %collective-permute-start.3 = (bf16[384,128]{1,0:T(8,128)(2,1)S(1)}, bf16[384,128]{1,0:T(8,128)(2,1)S(1)}, u32[]{:S(2)}, u32[]{:S(2)}) collective-permute-start(bf16[384,128]{1,0:T(8,128)(2,1)S(1)} %get-tuple-element.50), channel_id=1, source_target_pairs={{0,16},{4,20},{8,24},{12,28},{16,0},{20,4},{24,8},{28,12},{1,17},{... | collective-permute-start | bytes 294920 | tf_op jit(solution)/shard_map/ppermute | solution.py:144
  7.4 14.0 %collective-permute-start.4 = (bf16[384,128]{1,0:T(8,128)(2,1)S(1)}, bf16[384,128]{1,0:T(8,128)(2,1)S(1)}, u32[]{:S(2)}, u32[]{:S(2)}) collective-permute-start(bf16[384,128]{1,0:T(8,128)(2,1)S(1)} %get-tuple-element.51), channel_id=1, source_target_pairs={{0,20},{4,24},{8,28},{12,0},{16,4},{20,8},{24,12},{28,16},{1,21},{... | collective-permute-start | bytes 294920 | tf_op jit(solution)/shard_map/ppermute | solution.py:144
  13.3 12.0 %collective-permute-start.5 = (bf16[384,128]{1,0:T(8,128)(2,1)S(1)}, bf16[384,128]{1,0:T(8,128)(2,1)S(1)}, u32[]{:S(2)}, u32[]{:S(2)}) collective-permute-start(bf16[384,128]{1,0:T(8,128)(2,1)S(1)} %get-tuple-element.52), channel_id=1, source_target_pairs={{0,24},{4,28},{8,0},{12,4},{16,8},{20,12},{24,16},{28,20},{1,25},{... | collective-permute-start | bytes 294920 | tf_op jit(solution)/shard_map/ppermute | solution.py:144
  14.7 11.1 %collective-permute-start.6 = (bf16[384,128]{1,0:T(8,128)(2,1)S(1)}, bf16[384,128]{1,0:T(8,128)(2,1)S(1)}, u32[]{:S(2)}, u32[]{:S(2)}) collective-permute-start(bf16[384,128]{1,0:T(8,128)(2,1)S(1)} %get-tuple-element.53), channel_id=1, source_target_pairs={{0,28},{4,0},{8,4},{12,8},{16,12},{20,16},{24,20},{28,24},{1,29},{... | collective-permute-start | bytes 294920 | tf_op jit(solution)/shard_map/ppermute | solution.py:144
  16.1 12.4 %collective-permute-start.7 = (bf16[384,128]{1,0:T(8,128)(2,1)S(1)}, bf16[384,128]{1,0:T(8,128)(2,1)S(1)}, u32[]{:S(2)}, u32[]{:S(2)}) collective-permute-start(bf16[384,128]{1,0:T(8,128)(2,1)S(1)} %get-tuple-element.58), channel_id=1, source_target_pairs={{0,4},{4,8},{8,12},{12,16},{16,20},{20,24},{24,28},{28,0},{1,5},{5... | collective-permute-start | bytes 294920 | tf_op jit(solution)/shard_map/ppermute | solution.py:144
  16.8 15.8 %collective-permute-start.8 = (bf16[384,128]{1,0:T(8,128)(2,1)S(1)}, bf16[384,128]{1,0:T(8,128)(2,1)S(1)}, u32[]{:S(2)}, u32[]{:S(2)}) collective-permute-start(bf16[384,128]{1,0:T(8,128)(2,1)S(1)} %get-tuple-element.59), channel_id=1, source_target_pairs={{0,8},{4,12},{8,16},{12,20},{16,24},{20,28},{24,0},{28,4},{1,9},{5... | collective-permute-start | bytes 294920 | tf_op jit(solution)/shard_map/ppermute | solution.py:144
  21.4 14.2 %collective-permute-start.9 = (bf16[384,128]{1,0:T(8,128)(2,1)S(1)}, bf16[384,128]{1,0:T(8,128)(2,1)S(1)}, u32[]{:S(2)}, u32[]{:S(2)}) collective-permute-start(bf16[384,128]{1,0:T(8,128)(2,1)S(1)} %get-tuple-element.60), channel_id=1, source_target_pairs={{0,12},{4,16},{8,20},{12,24},{16,28},{20,0},{24,4},{28,8},{1,13},{... | collective-permute-start | bytes 294920 | tf_op jit(solution)/shard_map/ppermute | solution.py:144
  25.2 10.4 %collective-permute-start.10 = (bf16[384,128]{1,0:T(8,128)(2,1)S(1)}, bf16[384,128]{1,0:T(8,128)(2,1)S(1)}, u32[]{:S(2)}, u32[]{:S(2)}) collective-permute-start(bf16[384,128]{1,0:T(8,128)(2,1)S(1)} %get-tuple-element.61), channel_id=1, source_target_pairs={{0,16},{4,20},{8,24},{12,28},{16,0},{20,4},{24,8},{28,12},{1,17},{... | collective-permute-start | bytes 294920 | tf_op jit(solution)/shard_map/ppermute | solution.py:144
  25.8 11.1 %collective-permute-start.11 = (bf16[384,128]{1,0:T(8,128)(2,1)S(1)}, bf16[384,128]{1,0:T(8,128)(2,1)S(1)}, u32[]{:S(2)}, u32[]{:S(2)}) collective-permute-start(bf16[384,128]{1,0:T(8,128)(2,1)S(1)} %get-tuple-element.62), channel_id=1, source_target_pairs={{0,20},{4,24},{8,28},{12,0},{16,4},{20,8},{24,12},{28,16},{1,21},{... | collective-permute-start | bytes 294920 | tf_op jit(solution)/shard_map/ppermute | solution.py:144
  28.5 8.4 %collective-permute-start.12 = (bf16[384,128]{1,0:T(8,128)(2,1)S(1)}, bf16[384,128]{1,0:T(8,128)(2,1)S(1)}, u32[]{:S(2)}, u32[]{:S(2)}) collective-permute-start(bf16[384,128]{1,0:T(8,128)(2,1)S(1)} %get-tuple-element.63), channel_id=1, source_target_pairs={{0,24},{4,28},{8,0},{12,4},{16,8},{20,12},{24,16},{28,20},{1,25},{... | collective-permute-start | bytes 294920 | tf_op jit(solution)/shard_map/ppermute | solution.py:144
  32.6 5.3 %collective-permute-start.13 = (bf16[384,128]{1,0:T(8,128)(2,1)S(1)}, bf16[384,128]{1,0:T(8,128)(2,1)S(1)}, u32[]{:S(2)}, u32[]{:S(2)}) collective-permute-start(bf16[384,128]{1,0:T(8,128)(2,1)S(1)} %get-tuple-element.64), channel_id=1, source_target_pairs={{0,28},{4,0},{8,4},{12,8},{16,12},{20,16},{24,20},{28,24},{1,29},{... | collective-permute-start | bytes 294920 | tf_op jit(solution)/shard_map/ppermute | solution.py:144
  41.0 9.3 %collective-permute-start.14 = (bf16[384,128]{1,0:T(8,128)(2,1)S(1)}, bf16[384,128]{1,0:T(8,128)(2,1)S(1)}, u32[]{:S(2)}, u32[]{:S(2)}) collective-permute-start(bf16[384,128]{1,0:T(8,128)(2,1)S(1)} %get-tuple-element.66), channel_id=1, source_target_pairs={{0,4},{4,8},{8,12},{12,16},{16,20},{20,24},{24,28},{28,0},{1,5},{5... | collective-permute-start | bytes 294920 | tf_op jit(solution)/shard_map/ppermute | solution.py:144
  42.6 8.2 %collective-permute-start.15 = (bf16[384,128]{1,0:T(8,128)(2,1)S(1)}, bf16[384,128]{1,0:T(8,128)(2,1)S(1)}, u32[]{:S(2)}, u32[]{:S(2)}) collective-permute-start(bf16[384,128]{1,0:T(8,128)(2,1)S(1)} %get-tuple-element.67), channel_id=1, source_target_pairs={{0,8},{4,12},{8,16},{12,20},{16,24},{20,28},{24,0},{28,4},{1,9},{5... | collective-permute-start | bytes 294920 | tf_op jit(solution)/shard_map/ppermute | solution.py:144
  45.3 12.9 %collective-permute-start.16 = (bf16[384,128]{1,0:T(8,128)(2,1)S(1)}, bf16[384,128]{1,0:T(8,128)(2,1)S(1)}, u32[]{:S(2)}, u32[]{:S(2)}) collective-permute-start(bf16[384,128]{1,0:T(8,128)(2,1)S(1)} %get-tuple-element.68), channel_id=1, source_target_pairs={{0,12},{4,16},{8,20},{12,24},{16,28},{20,0},{24,4},{28,8},{1,13},{... | collective-permute-start | bytes 294920 | tf_op jit(solution)/shard_map/ppermute | solution.py:144
  46.0 12.2 %collective-permute-start.17 = (bf16[384,128]{1,0:T(8,128)(2,1)S(1)}, bf16[384,128]{1,0:T(8,128)(2,1)S(1)}, u32[]{:S(2)}, u32[]{:S(2)}) collective-permute-start(bf16[384,128]{1,0:T(8,128)(2,1)S(1)} %get-tuple-element.69), channel_id=1, source_target_pairs={{0,16},{4,20},{8,24},{12,28},{16,0},{20,4},{24,8},{28,12},{1,17},{... | collective-permute-start | bytes 294920 | tf_op jit(solution)/shard_map/ppermute | solution.py:144
  46.5 11.7 %collective-permute-start.18 = (bf16[384,128]{1,0:T(8,128)(2,1)S(1)}, bf16[384,128]{1,0:T(8,128)(2,1)S(1)}, u32[]{:S(2)}, u32[]{:S(2)}) collective-permute-start(bf16[384,128]{1,0:T(8,128)(2,1)S(1)} %get-tuple-element.70), channel_id=1, source_target_pairs={{0,20},{4,24},{8,28},{12,0},{16,4},{20,8},{24,12},{28,16},{1,21},{... | collective-permute-start | bytes 294920 | tf_op jit(solution)/shard_map/ppermute | solution.py:144
  50.3 9.6 %collective-permute-start.19 = (bf16[384,128]{1,0:T(8,128)(2,1)S(1)}, bf16[384,128]{1,0:T(8,128)(2,1)S(1)}, u32[]{:S(2)}, u32[]{:S(2)}) collective-permute-start(bf16[384,128]{1,0:T(8,128)(2,1)S(1)} %get-tuple-element.71), channel_id=1, source_target_pairs={{0,24},{4,28},{8,0},{12,4},{16,8},{20,12},{24,16},{28,20},{1,25},{... | collective-permute-start | bytes 294920 | tf_op jit(solution)/shard_map/ppermute | solution.py:144
  50.8 11.0 %collective-permute-start.20 = (bf16[384,128]{1,0:T(8,128)(2,1)S(1)}, bf16[384,128]{1,0:T(8,128)(2,1)S(1)}, u32[]{:S(2)}, u32[]{:S(2)}) collective-permute-start(bf16[384,128]{1,0:T(8,128)(2,1)S(1)} %get-tuple-element.72), channel_id=1, source_target_pairs={{0,28},{4,0},{8,4},{12,8},{16,12},{20,16},{24,20},{28,24},{1,29},{... | collective-permute-start | bytes 294920 | tf_op jit(solution)/shard_map/ppermute | solution.py:144
  63.3 2.5 %collective-permute-start.21 = (bf16[192,2048]{1,0:T(8,128)(2,1)S(1)}, bf16[192,2048]{1,0:T(8,128)(2,1)S(1)}, u32[]{:S(2)}, u32[]{:S(2)}) collective-permute-start(bf16[192,2048]{1,0:T(8,128)(2,1)S(1)} %get-tuple-element.76), channel_id=1, source_target_pairs={{0,1},{1,0},{2,3},{3,2},{4,5},{5,4},{6,7},{7,6},{8,9},{9,8},{10,11... | collective-permute-start | bytes 2359304 | tf_op jit(solution)/shard_map/ppermute | solution.py:455
  65.9 12.0 %collective-permute-start.24 = (bf16[192,1024]{1,0:T(8,128)(2,1)S(1)}, bf16[192,1024]{1,0:T(8,128)(2,1)S(1)}, u32[]{:S(2)}, u32[]{:S(2)}) collective-permute-start(bf16[192,1024]{1,0:T(8,128)(2,1)S(1)} %shard_map.108), channel_id=1, source_target_pairs={{0,2},{1,3},{2,0},{3,1},{4,6},{5,7},{6,4},{7,5},{8,10},{9,11},{10,... | collective-permute-start | bytes 1179656 | tf_op jit(solution)/shard_map/ppermute | solution.py:442
  68.3 17.1 %collective-permute-start.23 = (bf16[192,1024]{1,0:T(8,128)(2,1)S(1)}, bf16[192,1024]{1,0:T(8,128)(2,1)S(1)}, u32[]{:S(2)}, u32[]{:S(2)}) collective-permute-start(bf16[192,1024]{1,0:T(8,128)(2,1)S(1)} %shard_map.107), channel_id=1, source_target_pairs={{0,2},{1,3},{2,0},{3,1},{4,6},{5,7},{6,4},{7,5},{8,10},{9,11},{10,... | collective-permute-start | bytes 1179656 | tf_op jit(solution)/shard_map/ppermute | solution.py:442
  (8 other events, 128.4 us)

commit v5 on v4

--- a/solution.py
+++ b/solution.py
@@ -19,6 +19,20 @@
 
 def params(nbytes):
     return pltpu.CompilerParams(vmem_limit_bytes=int(min(nbytes + 4 * 2**20, 58 * 2**20)))
+
+
+def filter_order(count):
+    return list(range(count))
+
+
+def gated_order(count):
+    return list(range(count))
+
+
+def conv_order(count):
+    if count < 4:
+        return list(range(count))
+    return [0, count // 2, 1, count - 1, *sorted(set(range(2, count - 1)) - {count // 2}, key=lambda s: (abs(2 * s - count), s))]
 
 
 def tables(total, inner):
@@ -43,18 +57,18 @@
 
 def split_kernel(idx_ref, array_ref, *outs, count):
     width = outs[0].shape[1]
-    for s in range(count):
+    for j, s in enumerate(filter_order(count)):
         at = pl.ds(pl.multiple_of(lax.rem(idx_ref[0] + s, count) * width, width), width)
-        outs[s][...] = array_ref[:, at]
-
-
-def filter_slices(idx, value, count):
+        outs[j][...] = array_ref[:, at]
+
+
+def filter_slices(idx, value, count, order):
     rows, channels = value.shape
     width = channels // count
     if width % 128:
         return [
             lax.dynamic_slice_in_dim(value, lax.rem(idx[0] + s, count) * width, width, 1)
-            for s in range(count)
+            for s in order(count)
         ]
     return pl.pallas_call(
         functools.partial(split_kernel, count=count),
@@ -81,9 +95,9 @@
         copy.start()
     for copy in copies[:2]:
         copy.wait()
-    for s in range(count):
+    for j, s in enumerate(gated_order(count)):
         at = pl.ds(pl.multiple_of(lax.rem(idx_ref[0] + s, count) * width, width), width)
-        outs[s][...] = (key_ref[:, at].astype(F32) * value_ref[:, at].astype(F32)).astype(BF16)
+        outs[j][...] = (key_ref[:, at].astype(F32) * value_ref[:, at].astype(F32)).astype(BF16)
     for copy in copies[2:]:
         copy.wait()
 
@@ -110,7 +124,7 @@
     cost = pl.CostEstimate(flops=rows * channels, bytes_accessed=limit, transcendentals=0)
     if width % 128:
         gated = (key_k.astype(F32) * value_v.astype(F32)).astype(BF16)
-        return filter_slices(idx, gated, count), pl.pallas_call(
+        return filter_slices(idx, gated, count, gated_order), pl.pallas_call(
             plain_kernel,
             out_shape=columns,
             in_specs=[SMEM, HBM],
@@ -138,18 +152,20 @@
     return outs[:count], outs[count:]
 
 
-def exchange(blocks, axis, count):
-    out = [blocks[0]]
-    for s in range(1, count):
-        out.append(lax.ppermute(blocks[s], axis, [(i, (i + s) % count) for i in range(count)]))
+def exchange(blocks, axis, order):
+    count = len(blocks)
+    out = []
+    for s, block in zip(order, blocks):
+        perm = [(i, (i + s) % count) for i in range(count)]
+        out.append(lax.ppermute(block, axis, perm) if s else block)
     return out
 
 
-def gather_positions(me, blocks, spot, count):
+def gather_positions(me, blocks, spot, count, order):
     outer_here = blocks[0].shape[0] // spot.shape[1]
-    for s in range(count):
+    for j, s in enumerate(order(count)):
         src = lax.rem(me + count - s, count)
-        spot[pl.ds(src * outer_here, outer_here)] = blocks[s][...].reshape(outer_here, *spot.shape[1:])
+        spot[pl.ds(src * outer_here, outer_here)] = blocks[j][...].reshape(outer_here, *spot.shape[1:])
 
 
 def halves(tile):
@@ -195,7 +211,7 @@
     copies.append(pltpu.make_async_copy(back_hbm, back_ref, sems.at[parts]))
     for copy in copies:
         copy.start()
-    gather_positions(idx_ref[0], blocks, spot, count)
+    gather_positions(idx_ref[0], blocks, spot, count, filter_order)
     forward_first(first_ref, spot, mixed)
 
     for p in range(parts):
@@ -214,7 +230,7 @@
 def conv_kernel(idx_ref, first_ref, mid_ref, back_ref, last_ref, filt_ref, *refs, count):
     blocks, outs, (spot, mixed) = refs[:count], refs[count : 2 * count], refs[2 * count :]
     me = idx_ref[0]
-    gather_positions(me, blocks, spot, count)
+    gather_positions(me, blocks, spot, count, gated_order)
     forward_first(first_ref, spot, mixed)
     outer, _, inner, width = mixed.shape
 
@@ -236,20 +252,20 @@
 
     for_each(inner // (2 * SUB), ending)
     here = outer // count
-    for s in range(count):
+    for j, s in enumerate(conv_order(count)):
         dst = lax.rem(me + s, count)
-        outs[s][...] = spot[pl.ds(dst * here, here)].reshape(here * inner, width)
+        outs[j][...] = spot[pl.ds(dst * here, here)].reshape(here * inner, width)
 
 
 def hidden_rows(idx_ref, gain_ref, gate_ref, key_ref, value_ref, blocks, out_ref, at):
     me, count = idx_ref[0], len(blocks)
     width = blocks[0].shape[1]
     rows = slice(at, at + out_ref.shape[0])
-    for s in range(count):
+    for j, s in enumerate(conv_order(count)):
         src = lax.rem(me + count - s, count)
         cols = pl.ds(pl.multiple_of(src * width, width), width)
         gated = (key_ref[rows, cols].astype(F32) * value_ref[rows, cols].astype(F32)).astype(BF16).astype(F32)
-        total = blocks[s][rows, :].astype(F32) + gain_ref[:, cols] * gated
+        total = blocks[j][rows, :].astype(F32) + gain_ref[:, cols] * gated
         out_ref[:, cols] = (gate_ref[rows, cols].astype(F32) * total).astype(BF16)
 
 
@@ -400,11 +416,11 @@
     def group_of(step, which):
         return lax.rem(chip + step, chips) * 2 + which
 
-    filter_in = exchange(filter_slices(idx, long_filter, count), "ctx", count)
+    filter_in = exchange(filter_slices(idx, long_filter, count, filter_order), "ctx", filter_order(count))
     steps = list(range(1, chips)) + [0]
     order = jnp.stack([group_of(step, which) for which in (1 - core, core) for step in steps])
     slices, weights = gated_slices(idx, key_k, value_v, count, order, out_weight, groups)
-    gated_in = exchange(slices, "ctx", count)
+    gated_in = exchange(slices, "ctx", gated_order(count))
     spectrum, mid, back = pl.pallas_call(
         functools.partial(filter_kernel, count=count),
         out_shape=[
@@ -433,7 +449,7 @@
         compiler_params=params(2 * table + 7 * signal),
         cost_estimate=pl.CostEstimate(flops=6 * 10**9, bytes_accessed=12 * 10**6, transcendentals=0),
     )(idx, first, mid, back, last, spectrum, *gated_in)
-    conv_in = exchange(conv_out, "ctx", count)
+    conv_in = exchange(conv_out, "ctx", conv_order(count))
 
     swap = [(i, i ^ 1) for i in range(groups)]
     lead = rows // 32 * 16
@@ -444,9 +460,9 @@
     gain = skip_gain[None, :]
     if width % 128:
         conv = jnp.zeros((rows, channels), BF16)
-        for s in range(count):
+        for j, s in enumerate(conv_order(count)):
             src = lax.rem(idx[0] + count - s, count)
-            conv = lax.dynamic_update_slice_in_dim(conv, conv_in[s], src * width, 1)
+            conv = lax.dynamic_update_slice_in_dim(conv, conv_in[j], src * width, 1)
         idx, conv_in = jnp.zeros_like(idx), [conv]
     arrays = [idx, gain, gate_q, key_k, value_v]
     others, owns = weights[:chips], weights[chips:]

time: 88.2 us -> 86.8 us (0.984); the launches traced: 86.4 us -> 86.7 us
  waiting for transfers between devices: 21.9 us -> 29.9 us
  starting transfers between devices: 45.5 us -> 37.8 us
    ppermute x21, waiting for transfers between devices: 5.93 us -> 13.9 us  [exchange(): out.append(lax.ppermute(block, axis, perm) if s else block)]
    ppermute x21, starting transfers between devices: 43.7 us -> 36 us  [exchange(): out.append(lax.ppermute(block, axis, perm) if s else block)]
  transfers between devices with their start and end apart: 25 -> 25, of which waited for: 7 -> 8; matrix products, arithmetic and copies ran while one was open for 0% -> 0% of each run, Pallas kernels for 14% -> 14%
where the time goes in v5:
time: 86.8 us; the launch traced here: 86.7 us
  starting transfers between devices  37.8 us (44%)
  waiting for transfers between devices  29.9 us (34%)
  Pallas kernels  17.5 us (20%)
  local copies, waits for them, and re-layouts  1.16 us (1%)
    ppermute x21, starting transfers between devices, exchange(): out.append(lax.ppermute(block, axis, perm) if s else block)  36 us
    ppermute x2, waiting for transfers between devices, to_chip(): lax.ppermute(part, 'ch', [(i, (i + 2 * step) % groups) for i in range(gro...  14.7 us
    ppermute x21, waiting for transfers between devices, exchange(): out.append(lax.ppermute(block, axis, perm) if s else block)  13.9 us
    pallas_call x1, Pallas kernels, gated_slices(): pl.pallas_call(functools.partial(gate_kernel, count=count), out_shape=[ja...  4.54 us
    pallas_call x2, Pallas kernels, hidden_products(): pl.pallas_call(functools.partial(rows_kernel, at=at, others=len(weights),...  3.31 us
    pallas_call x1, Pallas kernels, local(): pl.pallas_call(functools.partial(conv_kernel, count=count), out_shape=[ja...  3.07 us
    pallas_call x1, Pallas kernels, local(): pl.pallas_call(functools.partial(filter_kernel, count=count), out_shape=[...  2.98 us
  transfers between devices with their start and end apart: 25, of which 8 were waited for; matrix products, arithmetic and copies ran while one was open for 0% of the time, Pallas kernels for 14%

profile of v5, /device:TPU:20, one launch (start us, length us, event | category | flops | bytes accessed | tf_op | source)
XLA Modules:
  0.0 86.7 jit_solution(2457045209284122484)
XLA Ops:
  1.3 1.5 %collective-permute-start = (bf16[384,128]{1,0:T(8,128)(2,1)S(1)}, bf16[384,128]{1,0:T(8,128)(2,1)S(1)}, u32[]{:S(2)}, u32[]{:S(2)}) collective-permute-start(bf16[384,128]{1,0:T(8,128)(2,1)S(1)} %get-tuple-element.47), channel_id=1, source_target_pairs={{0,4},{4,8},{8,12},{12,16},{16,20},{20,24},{24,28},{28,0},{1,5},{5... | collective-permute-start | bytes 294920 | tf_op jit(solution)/shard_map/ppermute | solution.py:160
  2.9 1.6 %collective-permute-start.1 = (bf16[384,128]{1,0:T(8,128)(2,1)S(1)}, bf16[384,128]{1,0:T(8,128)(2,1)S(1)}, u32[]{:S(2)}, u32[]{:S(2)}) collective-permute-start(bf16[384,128]{1,0:T(8,128)(2,1)S(1)} %get-tuple-element.48), channel_id=1, source_target_pairs={{0,8},{4,12},{8,16},{12,20},{16,24},{20,28},{24,0},{28,4},{1,9},{5... | collective-permute-start | bytes 294920 | tf_op jit(solution)/shard_map/ppermute | solution.py:160
  5.7 1.7 %collective-permute-start.3 = (bf16[384,128]{1,0:T(8,128)(2,1)S(1)}, bf16[384,128]{1,0:T(8,128)(2,1)S(1)}, u32[]{:S(2)}, u32[]{:S(2)}) collective-permute-start(bf16[384,128]{1,0:T(8,128)(2,1)S(1)} %get-tuple-element.50), channel_id=1, source_target_pairs={{0,16},{4,20},{8,24},{12,28},{16,0},{20,4},{24,8},{28,12},{1,17},{... | collective-permute-start | bytes 294920 | tf_op jit(solution)/shard_map/ppermute | solution.py:160
  7.4 1.3 %collective-permute-start.4 = (bf16[384,128]{1,0:T(8,128)(2,1)S(1)}, bf16[384,128]{1,0:T(8,128)(2,1)S(1)}, u32[]{:S(2)}, u32[]{:S(2)}) collective-permute-start(bf16[384,128]{1,0:T(8,128)(2,1)S(1)} %get-tuple-element.51), channel_id=1, source_target_pairs={{0,20},{4,24},{8,28},{12,0},{16,4},{20,8},{24,12},{28,16},{1,21},{... | collective-permute-start | bytes 294920 | tf_op jit(solution)/shard_map/ppermute | solution.py:160
  8.7 4.5 %shard_map.100 = (bf16[384,128]{1,0:T(8,128)(2,1)S(1)}, bf16[384,128]{1,0:T(8,128)(2,1)S(1)}, bf16[384,128]{1,0:T(8,128)(2,1)S(1)}, bf16[384,128]{1,0:T(8,128)(2...) custom-call(s32[1]{0:T(128)} %bitcast.idx_ref, ...), custom_call_target="tpu_custom_call" | custom-call | flops 393216 | bytes 11534336 | tf_op jit(solution)/shard_map/pallas_call | solution.py:136
  13.3 1.4 %collective-permute-start.5 = (bf16[384,128]{1,0:T(8,128)(2,1)S(1)}, bf16[384,128]{1,0:T(8,128)(2,1)S(1)}, u32[]{:S(2)}, u32[]{:S(2)}) collective-permute-start(bf16[384,128]{1,0:T(8,128)(2,1)S(1)} %get-tuple-element.52), channel_id=1, source_target_pairs={{0,24},{4,28},{8,0},{12,4},{16,8},{20,12},{24,16},{28,20},{1,25},{... | collective-permute-start | bytes 294920 | tf_op jit(solution)/shard_map/ppermute | solution.py:160
  14.7 1.4 %collective-permute-start.6 = (bf16[384,128]{1,0:T(8,128)(2,1)S(1)}, bf16[384,128]{1,0:T(8,128)(2,1)S(1)}, u32[]{:S(2)}, u32[]{:S(2)}) collective-permute-start(bf16[384,128]{1,0:T(8,128)(2,1)S(1)} %get-tuple-element.53), channel_id=1, source_target_pairs={{0,28},{4,0},{8,4},{12,8},{16,12},{20,16},{24,20},{28,24},{1,29},{... | collective-permute-start | bytes 294920 | tf_op jit(solution)/shard_map/ppermute | solution.py:160
  16.8 4.6 %collective-permute-start.8 = (bf16[384,128]{1,0:T(8,128)(2,1)S(1)}, bf16[384,128]{1,0:T(8,128)(2,1)S(1)}, u32[]{:S(2)}, u32[]{:S(2)}) collective-permute-start(bf16[384,128]{1,0:T(8,128)(2,1)S(1)} %get-tuple-element.59), channel_id=1, source_target_pairs={{0,8},{4,12},{8,16},{12,20},{16,24},{20,28},{24,0},{28,4},{1,9},{5... | collective-permute-start | bytes 294920 | tf_op jit(solution)/shard_map/ppermute | solution.py:160
  21.4 3.8 %collective-permute-start.9 = (bf16[384,128]{1,0:T(8,128)(2,1)S(1)}, bf16[384,128]{1,0:T(8,128)(2,1)S(1)}, u32[]{:S(2)}, u32[]{:S(2)}) collective-permute-start(bf16[384,128]{1,0:T(8,128)(2,1)S(1)} %get-tuple-element.60), channel_id=1, source_target_pairs={{0,12},{4,16},{8,20},{12,24},{16,28},{20,0},{24,4},{28,8},{1,13},{... | collective-permute-start | bytes 294920 | tf_op jit(solution)/shard_map/ppermute | solution.py:160
  25.8 2.7 %collective-permute-start.11 = (bf16[384,128]{1,0:T(8,128)(2,1)S(1)}, bf16[384,128]{1,0:T(8,128)(2,1)S(1)}, u32[]{:S(2)}, u32[]{:S(2)}) collective-permute-start(bf16[384,128]{1,0:T(8,128)(2,1)S(1)} %get-tuple-element.62), channel_id=1, source_target_pairs={{0,20},{4,24},{8,28},{12,0},{16,4},{20,8},{24,12},{28,16},{1,21},{... | collective-permute-start | bytes 294920 | tf_op jit(solution)/shard_map/ppermute | solution.py:160
  28.5 4.1 %collective-permute-start.12 = (bf16[384,128]{1,0:T(8,128)(2,1)S(1)}, bf16[384,128]{1,0:T(8,128)(2,1)S(1)}, u32[]{:S(2)}, u32[]{:S(2)}) collective-permute-start(bf16[384,128]{1,0:T(8,128)(2,1)S(1)} %get-tuple-element.63), channel_id=1, source_target_pairs={{0,24},{4,28},{8,0},{12,4},{16,8},{20,12},{24,16},{28,20},{1,25},{... | collective-permute-start | bytes 294920 | tf_op jit(solution)/shard_map/ppermute | solution.py:160
  32.6 3.0 %shard_map.102 = (bf16[24,256,128]{2,1,0:T(8,128)(2,1)S(1)}, bf16[24,256,256]{2,1,0:T(8,128)(2,1)S(1)}, bf16[24,256,256]{2,1,0:T(8,128)(2,1)S(1)}) custom-call(s32[1]{0:T(128)} %bitcast.idx_ref, bf16[384,192]{1,0:T(8,128)(2,1)S(1)} %copy-done.5, bf16[24,256,256]{2,1,0:T(8,128)(2,1)} %constant.47.clone.mid_hbm, ...), custom_call_target="tpu_custom_call" | custom-call | flops 3000000000 | bytes 8000000 | tf_op jit(solution)/shard_map/pallas_call | solution.py:424
  37.9 3.1 %shard_map.103 = (bf16[384,128]{1,0:T(8,128)(2,1)S(1)}, bf16[384,128]{1,0:T(8,128)(2,1)S(1)}, bf16[384,128]{1,0:T(8,128)(2,1)S(1)}, bf16[384,128]{1,0:T(8,128)(2...) custom-call(s32[1]{0:T(128)} %bitcast.idx_ref, ...), custom_call_target="tpu_custom_call" | custom-call | flops 6000000000 | bytes 12000000 | tf_op jit(solution)/shard_map/pallas_call | solution.py:443
  41.6 2.5 %collective-permute-start.15 = (bf16[384,128]{1,0:T(8,128)(2,1)S(1)}, bf16[384,128]{1,0:T(8,128)(2,1)S(1)}, u32[]{:S(2)}, u32[]{:S(2)}) collective-permute-start(bf16[384,128]{1,0:T(8,128)(2,1)S(1)} %get-tuple-element.67), channel_id=1, source_target_pairs={{0,4},{4,8},{8,12},{12,16},{16,20},{20,24},{24,28},{28,0},{1,5},{5... | collective-permute-start | bytes 294920 | tf_op jit(solution)/shard_map/ppermute | solution.py:160
  44.0 2.2 %collective-permute-start.16 = (bf16[384,128]{1,0:T(8,128)(2,1)S(1)}, bf16[384,128]{1,0:T(8,128)(2,1)S(1)}, u32[]{:S(2)}, u32[]{:S(2)}) collective-permute-start(bf16[384,128]{1,0:T(8,128)(2,1)S(1)} %get-tuple-element.68), channel_id=1, source_target_pairs={{0,28},{4,0},{8,4},{12,8},{16,12},{20,16},{24,20},{28,24},{1,29},{... | collective-permute-start | bytes 294920 | tf_op jit(solution)/shard_map/ppermute | solution.py:160
  46.2 1.7 %collective-permute-start.17 = (bf16[384,128]{1,0:T(8,128)(2,1)S(1)}, bf16[384,128]{1,0:T(8,128)(2,1)S(1)}, u32[]{:S(2)}, u32[]{:S(2)}) collective-permute-start(bf16[384,128]{1,0:T(8,128)(2,1)S(1)} %get-tuple-element.69), channel_id=1, source_target_pairs={{0,12},{4,16},{8,20},{12,24},{16,28},{20,0},{24,4},{28,8},{1,13},{... | collective-permute-start | bytes 294920 | tf_op jit(solution)/shard_map/ppermute | solution.py:160
  47.9 2.1 %collective-permute-start.18 = (bf16[384,128]{1,0:T(8,128)(2,1)S(1)}, bf16[384,128]{1,0:T(8,128)(2,1)S(1)}, u32[]{:S(2)}, u32[]{:S(2)}) collective-permute-start(bf16[384,128]{1,0:T(8,128)(2,1)S(1)} %get-tuple-element.70), channel_id=1, source_target_pairs={{0,20},{4,24},{8,28},{12,0},{16,4},{20,8},{24,12},{28,16},{1,21},{... | collective-permute-start | bytes 294920 | tf_op jit(solution)/shard_map/ppermute | solution.py:160
  50.4 7.0 %collective-permute-done.15.refs_4_.refs_6_ = bf16[384,128]{1,0:T(8,128)(2,1)S(1)} collective-permute-done((bf16[384,128]{1,0:T(8,128)(2,1)S(1)}, bf16[384,128]{1,0:T(8,128)(2,1)S(1)}, u32[]{:S(2)}, u32[]{:S(2)}) %collective-permute-start.15) | collective-permute-done | bytes 98336 | tf_op jit(solution)/shard_map/ppermute | solution.py:160
  57.5 2.4 %collective-permute-done.19.refs_8_.refs_10_ = bf16[384,128]{1,0:T(8,128)(2,1)S(1)} collective-permute-done((bf16[384,128]{1,0:T(8,128)(2,1)S(1)}, bf16[384,128]{1,0:T(8,128)(2,1)S(1)}, u32[]{:S(2)}, u32[]{:S(2)}) %collective-permute-start.19) | collective-permute-done | bytes 98336 | tf_op jit(solution)/shard_map/ppermute | solution.py:160
  59.9 2.2 %collective-permute-done.20.refs_9_.refs_11_ = bf16[384,128]{1,0:T(8,128)(2,1)S(1)} collective-permute-done((bf16[384,128]{1,0:T(8,128)(2,1)S(1)}, bf16[384,128]{1,0:T(8,128)(2,1)S(1)}, u32[]{:S(2)}, u32[]{:S(2)}) %collective-permute-start.20) | collective-permute-done | bytes 98336 | tf_op jit(solution)/shard_map/ppermute | solution.py:160
  62.1 1.4 %shard_map.104 = (bf16[192,1024]{1,0:T(8,128)(2,1)S(1)}, bf16[192,2048]{1,0:T(8,128)(2,1)S(1)}) custom-call(s32[1]{0:T(128)} %bitcast.idx_ref, f32[1,1024]{1,0:T(1,128)S(1)} %bitcast.6, bf16[384,1024]{1,0:T(8,128)(2,1)S(1)} %copy-done.2, bf16[384,1024]{1,0:T(8,128)(2,1)S(1)} %copy-done, bf16[384,1024]{1,0:T(8,128)(2,1)S(1)} %copy-done.1, ...), custom_call_target="tpu_custom_call" | custom-call | flops 805306368 | bytes 14155776 | tf_op jit(solution)/shard_map/pallas_call | solution.py:305
  63.6 1.9 %shard_map.105 = (bf16[192,1024]{1,0:T(8,128)(2,1)S(1)}, bf16[192,2048]{1,0:T(8,128)(2,1)S(1)}, bf16[192,1024]{1,0:T(8,128)(2,1)S(1)}) custom-call(s32[1]{0:T(128)} %bitcast.idx_ref, f32[1,1024]{1,0:T(1,128)S(1)} %bitcast.7, bf16[384,1024]{1,0:T(8,128)(2,1)S(1)} %copy-done.2, bf16[384,1024]{1,0:T(8,128)(2,1)S(1)} %copy-done, ...), custom_call_target="tpu_custom_call" | custom-call | flops 805306368 | bytes 18350080 | tf_op jit(solution)/shard_map/pallas_call | solution.py:305
  70.2 8.0 %collective-permute-done.24.refs_1_ = bf16[192,1024]{1,0:T(8,128)(2,1)S(1)} collective-permute-done((bf16[192,1024]{1,0:T(8,128)(2,1)S(1)}, bf16[192,1024]{1,0:T(8,128)(2,1)S(1)}, u32[]{:S(2)}, u32[]{:S(2)}) %collective-permute-start.24) | collective-permute-done | bytes 393248 | tf_op jit(solution)/shard_map/ppermute | solution.py:458
  79.0 6.6 %collective-permute-done.23.refs_1_ = bf16[192,1024]{1,0:T(8,128)(2,1)S(1)} collective-permute-done((bf16[192,1024]{1,0:T(8,128)(2,1)S(1)}, bf16[192,1024]{1,0:T(8,128)(2,1)S(1)}, u32[]{:S(2)}, u32[]{:S(2)}) %collective-permute-start.23) | collective-permute-done | bytes 393248 | tf_op jit(solution)/shard_map/ppermute | solution.py:458
  (52 shorter events, 13.6 us)
Async XLA Ops:
  1.3 11.9 %collective-permute-start = (bf16[384,128]{1,0:T(8,128)(2,1)S(1)}, bf16[384,128]{1,0:T(8,128)(2,1)S(1)}, u32[]{:S(2)}, u32[]{:S(2)}) collective-permute-start(bf16[384,128]{1,0:T(8,128)(2,1)S(1)} %get-tuple-element.47), channel_id=1, source_target_pairs={{0,4},{4,8},{8,12},{12,16},{16,20},{20,24},{24,28},{28,0},{1,5},{5... | collective-permute-start | bytes 294920 | tf_op jit(solution)/shard_map/ppermute | solution.py:160
  2.9 11.8 %collective-permute-start.1 = (bf16[384,128]{1,0:T(8,128)(2,1)S(1)}, bf16[384,128]{1,0:T(8,128)(2,1)S(1)}, u32[]{:S(2)}, u32[]{:S(2)}) collective-permute-start(bf16[384,128]{1,0:T(8,128)(2,1)S(1)} %get-tuple-element.48), channel_id=1, source_target_pairs={{0,8},{4,12},{8,16},{12,20},{16,24},{20,28},{24,0},{28,4},{1,9},{5... | collective-permute-start | bytes 294920 | tf_op jit(solution)/shard_map/ppermute | solution.py:160
  4.5 11.6 %collective-permute-start.2 = (bf16[384,128]{1,0:T(8,128)(2,1)S(1)}, bf16[384,128]{1,0:T(8,128)(2,1)S(1)}, u32[]{:S(2)}, u32[]{:S(2)}) collective-permute-start(bf16[384,128]{1,0:T(8,128)(2,1)S(1)} %get-tuple-element.49), channel_id=1, source_target_pairs={{0,12},{4,16},{8,20},{12,24},{16,28},{20,0},{24,4},{28,8},{1,13},{... | collective-permute-start | bytes 294920 | tf_op jit(solution)/shard_map/ppermute | solution.py:160
  5.7 11.1 %collective-permute-start.3 = (bf16[384,128]{1,0:T(8,128)(2,1)S(1)}, bf16[384,128]{1,0:T(8,128)(2,1)S(1)}, u32[]{:S(2)}, u32[]{:S(2)}) collective-permute-start(bf16[384,128]{1,0:T(8,128)(2,1)S(1)} %get-tuple-element.50), channel_id=1, source_target_pairs={{0,16},{4,20},{8,24},{12,28},{16,0},{20,4},{24,8},{28,12},{1,17},{... | collective-permute-start | bytes 294920 | tf_op jit(solution)/shard_map/ppermute | solution.py:160
  7.4 14.0 %collective-permute-start.4 = (bf16[384,128]{1,0:T(8,128)(2,1)S(1)}, bf16[384,128]{1,0:T(8,128)(2,1)S(1)}, u32[]{:S(2)}, u32[]{:S(2)}) collective-permute-start(bf16[384,128]{1,0:T(8,128)(2,1)S(1)} %get-tuple-element.51), channel_id=1, source_target_pairs={{0,20},{4,24},{8,28},{12,0},{16,4},{20,8},{24,12},{28,16},{1,21},{... | collective-permute-start | bytes 294920 | tf_op jit(solution)/shard_map/ppermute | solution.py:160
  13.3 12.0 %collective-permute-start.5 = (bf16[384,128]{1,0:T(8,128)(2,1)S(1)}, bf16[384,128]{1,0:T(8,128)(2,1)S(1)}, u32[]{:S(2)}, u32[]{:S(2)}) collective-permute-start(bf16[384,128]{1,0:T(8,128)(2,1)S(1)} %get-tuple-element.52), channel_id=1, source_target_pairs={{0,24},{4,28},{8,0},{12,4},{16,8},{20,12},{24,16},{28,20},{1,25},{... | collective-permute-start | bytes 294920 | tf_op jit(solution)/shard_map/ppermute | solution.py:160
  14.7 11.1 %collective-permute-start.6 = (bf16[384,128]{1,0:T(8,128)(2,1)S(1)}, bf16[384,128]{1,0:T(8,128)(2,1)S(1)}, u32[]{:S(2)}, u32[]{:S(2)}) collective-permute-start(bf16[384,128]{1,0:T(8,128)(2,1)S(1)} %get-tuple-element.53), channel_id=1, source_target_pairs={{0,28},{4,0},{8,4},{12,8},{16,12},{20,16},{24,20},{28,24},{1,29},{... | collective-permute-start | bytes 294920 | tf_op jit(solution)/shard_map/ppermute | solution.py:160
  16.1 12.4 %collective-permute-start.7 = (bf16[384,128]{1,0:T(8,128)(2,1)S(1)}, bf16[384,128]{1,0:T(8,128)(2,1)S(1)}, u32[]{:S(2)}, u32[]{:S(2)}) collective-permute-start(bf16[384,128]{1,0:T(8,128)(2,1)S(1)} %get-tuple-element.58), channel_id=1, source_target_pairs={{0,4},{4,8},{8,12},{12,16},{16,20},{20,24},{24,28},{28,0},{1,5},{5... | collective-permute-start | bytes 294920 | tf_op jit(solution)/shard_map/ppermute | solution.py:160
  16.8 15.8 %collective-permute-start.8 = (bf16[384,128]{1,0:T(8,128)(2,1)S(1)}, bf16[384,128]{1,0:T(8,128)(2,1)S(1)}, u32[]{:S(2)}, u32[]{:S(2)}) collective-permute-start(bf16[384,128]{1,0:T(8,128)(2,1)S(1)} %get-tuple-element.59), channel_id=1, source_target_pairs={{0,8},{4,12},{8,16},{12,20},{16,24},{20,28},{24,0},{28,4},{1,9},{5... | collective-permute-start | bytes 294920 | tf_op jit(solution)/shard_map/ppermute | solution.py:160
  21.4 14.2 %collective-permute-start.9 = (bf16[384,128]{1,0:T(8,128)(2,1)S(1)}, bf16[384,128]{1,0:T(8,128)(2,1)S(1)}, u32[]{:S(2)}, u32[]{:S(2)}) collective-permute-start(bf16[384,128]{1,0:T(8,128)(2,1)S(1)} %get-tuple-element.60), channel_id=1, source_target_pairs={{0,12},{4,16},{8,20},{12,24},{16,28},{20,0},{24,4},{28,8},{1,13},{... | collective-permute-start | bytes 294920 | tf_op jit(solution)/shard_map/ppermute | solution.py:160
  25.2 10.4 %collective-permute-start.10 = (bf16[384,128]{1,0:T(8,128)(2,1)S(1)}, bf16[384,128]{1,0:T(8,128)(2,1)S(1)}, u32[]{:S(2)}, u32[]{:S(2)}) collective-permute-start(bf16[384,128]{1,0:T(8,128)(2,1)S(1)} %get-tuple-element.61), channel_id=1, source_target_pairs={{0,16},{4,20},{8,24},{12,28},{16,0},{20,4},{24,8},{28,12},{1,17},{... | collective-permute-start | bytes 294920 | tf_op jit(solution)/shard_map/ppermute | solution.py:160
  25.8 11.1 %collective-permute-start.11 = (bf16[384,128]{1,0:T(8,128)(2,1)S(1)}, bf16[384,128]{1,0:T(8,128)(2,1)S(1)}, u32[]{:S(2)}, u32[]{:S(2)}) collective-permute-start(bf16[384,128]{1,0:T(8,128)(2,1)S(1)} %get-tuple-element.62), channel_id=1, source_target_pairs={{0,20},{4,24},{8,28},{12,0},{16,4},{20,8},{24,12},{28,16},{1,21},{... | collective-permute-start | bytes 294920 | tf_op jit(solution)/shard_map/ppermute | solution.py:160
  28.5 8.4 %collective-permute-start.12 = (bf16[384,128]{1,0:T(8,128)(2,1)S(1)}, bf16[384,128]{1,0:T(8,128)(2,1)S(1)}, u32[]{:S(2)}, u32[]{:S(2)}) collective-permute-start(bf16[384,128]{1,0:T(8,128)(2,1)S(1)} %get-tuple-element.63), channel_id=1, source_target_pairs={{0,24},{4,28},{8,0},{12,4},{16,8},{20,12},{24,16},{28,20},{1,25},{... | collective-permute-start | bytes 294920 | tf_op jit(solution)/shard_map/ppermute | solution.py:160
  32.6 5.3 %collective-permute-start.13 = (bf16[384,128]{1,0:T(8,128)(2,1)S(1)}, bf16[384,128]{1,0:T(8,128)(2,1)S(1)}, u32[]{:S(2)}, u32[]{:S(2)}) collective-permute-start(bf16[384,128]{1,0:T(8,128)(2,1)S(1)} %get-tuple-element.64), channel_id=1, source_target_pairs={{0,28},{4,0},{8,4},{12,8},{16,12},{20,16},{24,20},{28,24},{1,29},{... | collective-permute-start | bytes 294920 | tf_op jit(solution)/shard_map/ppermute | solution.py:160
  41.0 9.0 %collective-permute-start.14 = (bf16[384,128]{1,0:T(8,128)(2,1)S(1)}, bf16[384,128]{1,0:T(8,128)(2,1)S(1)}, u32[]{:S(2)}, u32[]{:S(2)}) collective-permute-start(bf16[384,128]{1,0:T(8,128)(2,1)S(1)} %get-tuple-element.66), channel_id=1, source_target_pairs={{0,16},{4,20},{8,24},{12,28},{16,0},{20,4},{24,8},{28,12},{1,17},{... | collective-permute-start | bytes 294920 | tf_op jit(solution)/shard_map/ppermute | solution.py:160
  41.6 15.9 %collective-permute-start.15 = (bf16[384,128]{1,0:T(8,128)(2,1)S(1)}, bf16[384,128]{1,0:T(8,128)(2,1)S(1)}, u32[]{:S(2)}, u32[]{:S(2)}) collective-permute-start(bf16[384,128]{1,0:T(8,128)(2,1)S(1)} %get-tuple-element.67), channel_id=1, source_target_pairs={{0,4},{4,8},{8,12},{12,16},{16,20},{20,24},{24,28},{28,0},{1,5},{5... | collective-permute-start | bytes 294920 | tf_op jit(solution)/shard_map/ppermute | solution.py:160
  44.0 13.4 %collective-permute-start.16 = (bf16[384,128]{1,0:T(8,128)(2,1)S(1)}, bf16[384,128]{1,0:T(8,128)(2,1)S(1)}, u32[]{:S(2)}, u32[]{:S(2)}) collective-permute-start(bf16[384,128]{1,0:T(8,128)(2,1)S(1)} %get-tuple-element.68), channel_id=1, source_target_pairs={{0,28},{4,0},{8,4},{12,8},{16,12},{20,16},{24,20},{28,24},{1,29},{... | collective-permute-start | bytes 294920 | tf_op jit(solution)/shard_map/ppermute | solution.py:160
  46.2 11.2 %collective-permute-start.17 = (bf16[384,128]{1,0:T(8,128)(2,1)S(1)}, bf16[384,128]{1,0:T(8,128)(2,1)S(1)}, u32[]{:S(2)}, u32[]{:S(2)}) collective-permute-start(bf16[384,128]{1,0:T(8,128)(2,1)S(1)} %get-tuple-element.69), channel_id=1, source_target_pairs={{0,12},{4,16},{8,20},{12,24},{16,28},{20,0},{24,4},{28,8},{1,13},{... | collective-permute-start | bytes 294920 | tf_op jit(solution)/shard_map/ppermute | solution.py:160
  47.9 9.5 %collective-permute-start.18 = (bf16[384,128]{1,0:T(8,128)(2,1)S(1)}, bf16[384,128]{1,0:T(8,128)(2,1)S(1)}, u32[]{:S(2)}, u32[]{:S(2)}) collective-permute-start(bf16[384,128]{1,0:T(8,128)(2,1)S(1)} %get-tuple-element.70), channel_id=1, source_target_pairs={{0,20},{4,24},{8,28},{12,0},{16,4},{20,8},{24,12},{28,16},{1,21},{... | collective-permute-start | bytes 294920 | tf_op jit(solution)/shard_map/ppermute | solution.py:160
  50.0 9.8 %collective-permute-start.19 = (bf16[384,128]{1,0:T(8,128)(2,1)S(1)}, bf16[384,128]{1,0:T(8,128)(2,1)S(1)}, u32[]{:S(2)}, u32[]{:S(2)}) collective-permute-start(bf16[384,128]{1,0:T(8,128)(2,1)S(1)} %get-tuple-element.71), channel_id=1, source_target_pairs={{0,8},{4,12},{8,16},{12,20},{16,24},{20,28},{24,0},{28,4},{1,9},{5... | collective-permute-start | bytes 294920 | tf_op jit(solution)/shard_map/ppermute | solution.py:160
  57.4 4.6 %collective-permute-start.20 = (bf16[384,128]{1,0:T(8,128)(2,1)S(1)}, bf16[384,128]{1,0:T(8,128)(2,1)S(1)}, u32[]{:S(2)}, u32[]{:S(2)}) collective-permute-start(bf16[384,128]{1,0:T(8,128)(2,1)S(1)} %get-tuple-element.72), channel_id=1, source_target_pairs={{0,24},{4,28},{8,0},{12,4},{16,8},{20,12},{24,16},{28,20},{1,25},{... | collective-permute-start | bytes 294920 | tf_op jit(solution)/shard_map/ppermute | solution.py:160
  63.5 2.5 %collective-permute-start.21 = (bf16[192,2048]{1,0:T(8,128)(2,1)S(1)}, bf16[192,2048]{1,0:T(8,128)(2,1)S(1)}, u32[]{:S(2)}, u32[]{:S(2)}) collective-permute-start(bf16[192,2048]{1,0:T(8,128)(2,1)S(1)} %get-tuple-element.76), channel_id=1, source_target_pairs={{0,1},{1,0},{2,3},{3,2},{4,5},{5,4},{6,7},{7,6},{8,9},{9,8},{10,11... | collective-permute-start | bytes 2359304 | tf_op jit(solution)/shard_map/ppermute | solution.py:471
  66.1 12.0 %collective-permute-start.24 = (bf16[192,1024]{1,0:T(8,128)(2,1)S(1)}, bf16[192,1024]{1,0:T(8,128)(2,1)S(1)}, u32[]{:S(2)}, u32[]{:S(2)}) collective-permute-start(bf16[192,1024]{1,0:T(8,128)(2,1)S(1)} %shard_map.108), channel_id=1, source_target_pairs={{0,2},{1,3},{2,0},{3,1},{4,6},{5,7},{6,4},{7,5},{8,10},{9,11},{10,... | collective-permute-start | bytes 1179656 | tf_op jit(solution)/shard_map/ppermute | solution.py:458
  68.6 17.1 %collective-permute-start.23 = (bf16[192,1024]{1,0:T(8,128)(2,1)S(1)}, bf16[192,1024]{1,0:T(8,128)(2,1)S(1)}, u32[]{:S(2)}, u32[]{:S(2)}) collective-permute-start(bf16[192,1024]{1,0:T(8,128)(2,1)S(1)} %shard_map.107), channel_id=1, source_target_pairs={{0,2},{1,3},{2,0},{3,1},{4,6},{5,7},{6,4},{7,5},{8,10},{9,11},{10,... | collective-permute-start | bytes 1179656 | tf_op jit(solution)/shard_map/ppermute | solution.py:458
  (8 other events, 129.4 us)

commit v6 on v5

--- a/solution.py
+++ b/solution.py
@@ -367,15 +367,20 @@
 
 
 def finish_kernel(*refs, at, terms):
-    values, (out_ref, held, sem) = refs[:terms], refs[-3:]
-    total = values[0][...]
-    for value in values[1:]:
-        total = total + value[...].astype(F32)
-    held[...] = total.astype(BF16)
-    rows = held.shape[0]
-    copy = pltpu.make_async_copy(held, out_ref.at[pl.ds(at, rows), :], sem)
-    copy.start()
-    copy.wait()
+    values, (out_ref, held, sems) = refs[:terms], refs[-3:]
+    parts = sems.shape[0]
+    rows = held.shape[0] // parts
+    copies = []
+    for p in range(parts):
+        block = pl.ds(p * rows, rows)
+        total = values[0][block, :]
+        for value in values[1:]:
+            total = total + value[block, :].astype(F32)
+        held[block, :] = total.astype(BF16)
+        copies.append(pltpu.make_async_copy(held.at[block, :], out_ref.at[pl.ds(at + p * rows, rows), :], sems.at[p]))
+        copies[-1].start()
+    for copy in copies:
+        copy.wait()
 
 
 def finish(values, at, rows, buffer):
@@ -386,7 +391,7 @@
         out_shape=jax.ShapeDtypeStruct((rows, columns), BF16),
         in_specs=[VMEM] * len(values) + [HBM] * len(aliased),
         out_specs=HBM,
-        scratch_shapes=[pltpu.VMEM((here, columns), BF16), pltpu.SemaphoreType.DMA],
+        scratch_shapes=[pltpu.VMEM((here, columns), BF16), pltpu.SemaphoreType.DMA((4 if here % 64 == 0 else 1,))],
         input_output_aliases={len(values): 0} if aliased else {},
         compiler_params=params(4 * here * columns * (len(values) + 2)),
         cost_estimate=pl.CostEstimate(flops=0, bytes_accessed=columns, transcendentals=0),

time: 86.8 us -> 86.8 us (level)
  no operation moved by 1% of the time
where the time goes in v6:
time: 86.8 us; the launch traced here: 86.6 us
  starting transfers between devices  37.8 us (44%)
  waiting for transfers between devices  29.9 us (34%)
  Pallas kernels  17.4 us (20%)
  local copies, waits for them, and re-layouts  1.16 us (1%)
    ppermute x21, starting transfers between devices, exchange(): out.append(lax.ppermute(block, axis, perm) if s else block)  36 us
    ppermute x2, waiting for transfers between devices, to_chip(): lax.ppermute(part, 'ch', [(i, (i + 2 * step) % groups) for i in range(gro...  14.7 us
    ppermute x21, waiting for transfers between devices, exchange(): out.append(lax.ppermute(block, axis, perm) if s else block)  13.9 us
    pallas_call x1, Pallas kernels, gated_slices(): pl.pallas_call(functools.partial(gate_kernel, count=count), out_shape=[ja...  4.54 us
    pallas_call x2, Pallas kernels, hidden_products(): pl.pallas_call(functools.partial(rows_kernel, at=at, others=len(weights),...  3.31 us
    pallas_call x1, Pallas kernels, local(): pl.pallas_call(functools.partial(conv_kernel, count=count), out_shape=[ja...  3.07 us
    pallas_call x1, Pallas kernels, local(): pl.pallas_call(functools.partial(filter_kernel, count=count), out_shape=[...  2.98 us
  transfers between devices with their start and end apart: 25, of which 8 were waited for; matrix products, arithmetic and copies ran while one was open for 0% of the time, Pallas kernels for 14%

profile of v6, /device:TPU:20, one launch (start us, length us, event | category | flops | bytes accessed | tf_op | source)
XLA Modules:
  0.0 86.6 jit_solution(700453061332989406)
XLA Ops:
  1.3 1.5 %collective-permute-start = (bf16[384,128]{1,0:T(8,128)(2,1)S(1)}, bf16[384,128]{1,0:T(8,128)(2,1)S(1)}, u32[]{:S(2)}, u32[]{:S(2)}) collective-permute-start(bf16[384,128]{1,0:T(8,128)(2,1)S(1)} %get-tuple-element.47), channel_id=1, source_target_pairs={{0,4},{4,8},{8,12},{12,16},{16,20},{20,24},{24,28},{28,0},{1,5},{5... | collective-permute-start | bytes 294920 | tf_op jit(solution)/shard_map/ppermute | solution.py:160
  2.9 1.6 %collective-permute-start.1 = (bf16[384,128]{1,0:T(8,128)(2,1)S(1)}, bf16[384,128]{1,0:T(8,128)(2,1)S(1)}, u32[]{:S(2)}, u32[]{:S(2)}) collective-permute-start(bf16[384,128]{1,0:T(8,128)(2,1)S(1)} %get-tuple-element.48), channel_id=1, source_target_pairs={{0,8},{4,12},{8,16},{12,20},{16,24},{20,28},{24,0},{28,4},{1,9},{5... | collective-permute-start | bytes 294920 | tf_op jit(solution)/shard_map/ppermute | solution.py:160
  5.7 1.7 %collective-permute-start.3 = (bf16[384,128]{1,0:T(8,128)(2,1)S(1)}, bf16[384,128]{1,0:T(8,128)(2,1)S(1)}, u32[]{:S(2)}, u32[]{:S(2)}) collective-permute-start(bf16[384,128]{1,0:T(8,128)(2,1)S(1)} %get-tuple-element.50), channel_id=1, source_target_pairs={{0,16},{4,20},{8,24},{12,28},{16,0},{20,4},{24,8},{28,12},{1,17},{... | collective-permute-start | bytes 294920 | tf_op jit(solution)/shard_map/ppermute | solution.py:160
  7.4 1.3 %collective-permute-start.4 = (bf16[384,128]{1,0:T(8,128)(2,1)S(1)}, bf16[384,128]{1,0:T(8,128)(2,1)S(1)}, u32[]{:S(2)}, u32[]{:S(2)}) collective-permute-start(bf16[384,128]{1,0:T(8,128)(2,1)S(1)} %get-tuple-element.51), channel_id=1, source_target_pairs={{0,20},{4,24},{8,28},{12,0},{16,4},{20,8},{24,12},{28,16},{1,21},{... | collective-permute-start | bytes 294920 | tf_op jit(solution)/shard_map/ppermute | solution.py:160
  8.7 4.5 %shard_map.100 = (bf16[384,128]{1,0:T(8,128)(2,1)S(1)}, bf16[384,128]{1,0:T(8,128)(2,1)S(1)}, bf16[384,128]{1,0:T(8,128)(2,1)S(1)}, bf16[384,128]{1,0:T(8,128)(2...) custom-call(s32[1]{0:T(128)} %bitcast.idx_ref, ...), custom_call_target="tpu_custom_call" | custom-call | flops 393216 | bytes 11534336 | tf_op jit(solution)/shard_map/pallas_call | solution.py:136
  13.3 1.4 %collective-permute-start.5 = (bf16[384,128]{1,0:T(8,128)(2,1)S(1)}, bf16[384,128]{1,0:T(8,128)(2,1)S(1)}, u32[]{:S(2)}, u32[]{:S(2)}) collective-permute-start(bf16[384,128]{1,0:T(8,128)(2,1)S(1)} %get-tuple-element.52), channel_id=1, source_target_pairs={{0,24},{4,28},{8,0},{12,4},{16,8},{20,12},{24,16},{28,20},{1,25},{... | collective-permute-start | bytes 294920 | tf_op jit(solution)/shard_map/ppermute | solution.py:160
  14.7 1.4 %collective-permute-start.6 = (bf16[384,128]{1,0:T(8,128)(2,1)S(1)}, bf16[384,128]{1,0:T(8,128)(2,1)S(1)}, u32[]{:S(2)}, u32[]{:S(2)}) collective-permute-start(bf16[384,128]{1,0:T(8,128)(2,1)S(1)} %get-tuple-element.53), channel_id=1, source_target_pairs={{0,28},{4,0},{8,4},{12,8},{16,12},{20,16},{24,20},{28,24},{1,29},{... | collective-permute-start | bytes 294920 | tf_op jit(solution)/shard_map/ppermute | solution.py:160
  16.8 4.6 %collective-permute-start.8 = (bf16[384,128]{1,0:T(8,128)(2,1)S(1)}, bf16[384,128]{1,0:T(8,128)(2,1)S(1)}, u32[]{:S(2)}, u32[]{:S(2)}) collective-permute-start(bf16[384,128]{1,0:T(8,128)(2,1)S(1)} %get-tuple-element.59), channel_id=1, source_target_pairs={{0,8},{4,12},{8,16},{12,20},{16,24},{20,28},{24,0},{28,4},{1,9},{5... | collective-permute-start | bytes 294920 | tf_op jit(solution)/shard_map/ppermute | solution.py:160
  21.4 3.8 %collective-permute-start.9 = (bf16[384,128]{1,0:T(8,128)(2,1)S(1)}, bf16[384,128]{1,0:T(8,128)(2,1)S(1)}, u32[]{:S(2)}, u32[]{:S(2)}) collective-permute-start(bf16[384,128]{1,0:T(8,128)(2,1)S(1)} %get-tuple-element.60), channel_id=1, source_target_pairs={{0,12},{4,16},{8,20},{12,24},{16,28},{20,0},{24,4},{28,8},{1,13},{... | collective-permute-start | bytes 294920 | tf_op jit(solution)/shard_map/ppermute | solution.py:160
  25.8 2.7 %collective-permute-start.11 = (bf16[384,128]{1,0:T(8,128)(2,1)S(1)}, bf16[384,128]{1,0:T(8,128)(2,1)S(1)}, u32[]{:S(2)}, u32[]{:S(2)}) collective-permute-start(bf16[384,128]{1,0:T(8,128)(2,1)S(1)} %get-tuple-element.62), channel_id=1, source_target_pairs={{0,20},{4,24},{8,28},{12,0},{16,4},{20,8},{24,12},{28,16},{1,21},{... | collective-permute-start | bytes 294920 | tf_op jit(solution)/shard_map/ppermute | solution.py:160
  28.5 4.1 %collective-permute-start.12 = (bf16[384,128]{1,0:T(8,128)(2,1)S(1)}, bf16[384,128]{1,0:T(8,128)(2,1)S(1)}, u32[]{:S(2)}, u32[]{:S(2)}) collective-permute-start(bf16[384,128]{1,0:T(8,128)(2,1)S(1)} %get-tuple-element.63), channel_id=1, source_target_pairs={{0,24},{4,28},{8,0},{12,4},{16,8},{20,12},{24,16},{28,20},{1,25},{... | collective-permute-start | bytes 294920 | tf_op jit(solution)/shard_map/ppermute | solution.py:160
  32.6 3.0 %shard_map.102 = (bf16[24,256,128]{2,1,0:T(8,128)(2,1)S(1)}, bf16[24,256,256]{2,1,0:T(8,128)(2,1)S(1)}, bf16[24,256,256]{2,1,0:T(8,128)(2,1)S(1)}) custom-call(s32[1]{0:T(128)} %bitcast.idx_ref, bf16[384,192]{1,0:T(8,128)(2,1)S(1)} %copy-done.5, bf16[24,256,256]{2,1,0:T(8,128)(2,1)} %constant.47.clone.mid_hbm, ...), custom_call_target="tpu_custom_call" | custom-call | flops 3000000000 | bytes 8000000 | tf_op jit(solution)/shard_map/pallas_call | solution.py:429
  37.9 3.1 %shard_map.103 = (bf16[384,128]{1,0:T(8,128)(2,1)S(1)}, bf16[384,128]{1,0:T(8,128)(2,1)S(1)}, bf16[384,128]{1,0:T(8,128)(2,1)S(1)}, bf16[384,128]{1,0:T(8,128)(2...) custom-call(s32[1]{0:T(128)} %bitcast.idx_ref, ...), custom_call_target="tpu_custom_call" | custom-call | flops 6000000000 | bytes 12000000 | tf_op jit(solution)/shard_map/pallas_call | solution.py:448
  41.6 2.5 %collective-permute-start.15 = (bf16[384,128]{1,0:T(8,128)(2,1)S(1)}, bf16[384,128]{1,0:T(8,128)(2,1)S(1)}, u32[]{:S(2)}, u32[]{:S(2)}) collective-permute-start(bf16[384,128]{1,0:T(8,128)(2,1)S(1)} %get-tuple-element.67), channel_id=1, source_target_pairs={{0,4},{4,8},{8,12},{12,16},{16,20},{20,24},{24,28},{28,0},{1,5},{5... | collective-permute-start | bytes 294920 | tf_op jit(solution)/shard_map/ppermute | solution.py:160
  44.0 2.2 %collective-permute-start.16 = (bf16[384,128]{1,0:T(8,128)(2,1)S(1)}, bf16[384,128]{1,0:T(8,128)(2,1)S(1)}, u32[]{:S(2)}, u32[]{:S(2)}) collective-permute-start(bf16[384,128]{1,0:T(8,128)(2,1)S(1)} %get-tuple-element.68), channel_id=1, source_target_pairs={{0,28},{4,0},{8,4},{12,8},{16,12},{20,16},{24,20},{28,24},{1,29},{... | collective-permute-start | bytes 294920 | tf_op jit(solution)/shard_map/ppermute | solution.py:160
  46.2 1.7 %collective-permute-start.17 = (bf16[384,128]{1,0:T(8,128)(2,1)S(1)}, bf16[384,128]{1,0:T(8,128)(2,1)S(1)}, u32[]{:S(2)}, u32[]{:S(2)}) collective-permute-start(bf16[384,128]{1,0:T(8,128)(2,1)S(1)} %get-tuple-element.69), channel_id=1, source_target_pairs={{0,12},{4,16},{8,20},{12,24},{16,28},{20,0},{24,4},{28,8},{1,13},{... | collective-permute-start | bytes 294920 | tf_op jit(solution)/shard_map/ppermute | solution.py:160
  47.9 2.1 %collective-permute-start.18 = (bf16[384,128]{1,0:T(8,128)(2,1)S(1)}, bf16[384,128]{1,0:T(8,128)(2,1)S(1)}, u32[]{:S(2)}, u32[]{:S(2)}) collective-permute-start(bf16[384,128]{1,0:T(8,128)(2,1)S(1)} %get-tuple-element.70), channel_id=1, source_target_pairs={{0,20},{4,24},{8,28},{12,0},{16,4},{20,8},{24,12},{28,16},{1,21},{... | collective-permute-start | bytes 294920 | tf_op jit(solution)/shard_map/ppermute | solution.py:160
  50.4 7.0 %collective-permute-done.15.refs_4_.refs_6_ = bf16[384,128]{1,0:T(8,128)(2,1)S(1)} collective-permute-done((bf16[384,128]{1,0:T(8,128)(2,1)S(1)}, bf16[384,128]{1,0:T(8,128)(2,1)S(1)}, u32[]{:S(2)}, u32[]{:S(2)}) %collective-permute-start.15) | collective-permute-done | bytes 98336 | tf_op jit(solution)/shard_map/ppermute | solution.py:160
  57.5 2.4 %collective-permute-done.19.refs_8_.refs_10_ = bf16[384,128]{1,0:T(8,128)(2,1)S(1)} collective-permute-done((bf16[384,128]{1,0:T(8,128)(2,1)S(1)}, bf16[384,128]{1,0:T(8,128)(2,1)S(1)}, u32[]{:S(2)}, u32[]{:S(2)}) %collective-permute-start.19) | collective-permute-done | bytes 98336 | tf_op jit(solution)/shard_map/ppermute | solution.py:160
  59.9 2.2 %collective-permute-done.20.refs_9_.refs_11_ = bf16[384,128]{1,0:T(8,128)(2,1)S(1)} collective-permute-done((bf16[384,128]{1,0:T(8,128)(2,1)S(1)}, bf16[384,128]{1,0:T(8,128)(2,1)S(1)}, u32[]{:S(2)}, u32[]{:S(2)}) %collective-permute-start.20) | collective-permute-done | bytes 98336 | tf_op jit(solution)/shard_map/ppermute | solution.py:160
  62.1 1.4 %shard_map.104 = (bf16[192,1024]{1,0:T(8,128)(2,1)S(1)}, bf16[192,2048]{1,0:T(8,128)(2,1)S(1)}) custom-call(s32[1]{0:T(128)} %bitcast.idx_ref, f32[1,1024]{1,0:T(1,128)S(1)} %bitcast.6, bf16[384,1024]{1,0:T(8,128)(2,1)S(1)} %copy-done.2, bf16[384,1024]{1,0:T(8,128)(2,1)S(1)} %copy-done, bf16[384,1024]{1,0:T(8,128)(2,1)S(1)} %copy-done.1, ...), custom_call_target="tpu_custom_call" | custom-call | flops 805306368 | bytes 14155776 | tf_op jit(solution)/shard_map/pallas_call | solution.py:305
  63.6 1.9 %shard_map.105 = (bf16[192,1024]{1,0:T(8,128)(2,1)S(1)}, bf16[192,2048]{1,0:T(8,128)(2,1)S(1)}, bf16[192,1024]{1,0:T(8,128)(2,1)S(1)}) custom-call(s32[1]{0:T(128)} %bitcast.idx_ref, f32[1,1024]{1,0:T(1,128)S(1)} %bitcast.7, bf16[384,1024]{1,0:T(8,128)(2,1)S(1)} %copy-done.2, bf16[384,1024]{1,0:T(8,128)(2,1)S(1)} %copy-done, ...), custom_call_target="tpu_custom_call" | custom-call | flops 805306368 | bytes 18350080 | tf_op jit(solution)/shard_map/pallas_call | solution.py:305
  70.2 8.0 %collective-permute-done.24.refs_1_ = bf16[192,1024]{1,0:T(8,128)(2,1)S(1)} collective-permute-done((bf16[192,1024]{1,0:T(8,128)(2,1)S(1)}, bf16[192,1024]{1,0:T(8,128)(2,1)S(1)}, u32[]{:S(2)}, u32[]{:S(2)}) %collective-permute-start.24) | collective-permute-done | bytes 393248 | tf_op jit(solution)/shard_map/ppermute | solution.py:463
  79.0 6.7 %collective-permute-done.23.refs_1_ = bf16[192,1024]{1,0:T(8,128)(2,1)S(1)} collective-permute-done((bf16[192,1024]{1,0:T(8,128)(2,1)S(1)}, bf16[192,1024]{1,0:T(8,128)(2,1)S(1)}, u32[]{:S(2)}, u32[]{:S(2)}) %collective-permute-start.23) | collective-permute-done | bytes 393248 | tf_op jit(solution)/shard_map/ppermute | solution.py:463
  (52 shorter events, 13.5 us)
Async XLA Ops:
  1.3 11.9 %collective-permute-start = (bf16[384,128]{1,0:T(8,128)(2,1)S(1)}, bf16[384,128]{1,0:T(8,128)(2,1)S(1)}, u32[]{:S(2)}, u32[]{:S(2)}) collective-permute-start(bf16[384,128]{1,0:T(8,128)(2,1)S(1)} %get-tuple-element.47), channel_id=1, source_target_pairs={{0,4},{4,8},{8,12},{12,16},{16,20},{20,24},{24,28},{28,0},{1,5},{5... | collective-permute-start | bytes 294920 | tf_op jit(solution)/shard_map/ppermute | solution.py:160
  2.9 11.8 %collective-permute-start.1 = (bf16[384,128]{1,0:T(8,128)(2,1)S(1)}, bf16[384,128]{1,0:T(8,128)(2,1)S(1)}, u32[]{:S(2)}, u32[]{:S(2)}) collective-permute-start(bf16[384,128]{1,0:T(8,128)(2,1)S(1)} %get-tuple-element.48), channel_id=1, source_target_pairs={{0,8},{4,12},{8,16},{12,20},{16,24},{20,28},{24,0},{28,4},{1,9},{5... | collective-permute-start | bytes 294920 | tf_op jit(solution)/shard_map/ppermute | solution.py:160
  4.5 11.6 %collective-permute-start.2 = (bf16[384,128]{1,0:T(8,128)(2,1)S(1)}, bf16[384,128]{1,0:T(8,128)(2,1)S(1)}, u32[]{:S(2)}, u32[]{:S(2)}) collective-permute-start(bf16[384,128]{1,0:T(8,128)(2,1)S(1)} %get-tuple-element.49), channel_id=1, source_target_pairs={{0,12},{4,16},{8,20},{12,24},{16,28},{20,0},{24,4},{28,8},{1,13},{... | collective-permute-start | bytes 294920 | tf_op jit(solution)/shard_map/ppermute | solution.py:160
  5.7 11.1 %collective-permute-start.3 = (bf16[384,128]{1,0:T(8,128)(2,1)S(1)}, bf16[384,128]{1,0:T(8,128)(2,1)S(1)}, u32[]{:S(2)}, u32[]{:S(2)}) collective-permute-start(bf16[384,128]{1,0:T(8,128)(2,1)S(1)} %get-tuple-element.50), channel_id=1, source_target_pairs={{0,16},{4,20},{8,24},{12,28},{16,0},{20,4},{24,8},{28,12},{1,17},{... | collective-permute-start | bytes 294920 | tf_op jit(solution)/shard_map/ppermute | solution.py:160
  7.4 14.0 %collective-permute-start.4 = (bf16[384,128]{1,0:T(8,128)(2,1)S(1)}, bf16[384,128]{1,0:T(8,128)(2,1)S(1)}, u32[]{:S(2)}, u32[]{:S(2)}) collective-permute-start(bf16[384,128]{1,0:T(8,128)(2,1)S(1)} %get-tuple-element.51), channel_id=1, source_target_pairs={{0,20},{4,24},{8,28},{12,0},{16,4},{20,8},{24,12},{28,16},{1,21},{... | collective-permute-start | bytes 294920 | tf_op jit(solution)/shard_map/ppermute | solution.py:160
  13.3 12.0 %collective-permute-start.5 = (bf16[384,128]{1,0:T(8,128)(2,1)S(1)}, bf16[384,128]{1,0:T(8,128)(2,1)S(1)}, u32[]{:S(2)}, u32[]{:S(2)}) collective-permute-start(bf16[384,128]{1,0:T(8,128)(2,1)S(1)} %get-tuple-element.52), channel_id=1, source_target_pairs={{0,24},{4,28},{8,0},{12,4},{16,8},{20,12},{24,16},{28,20},{1,25},{... | collective-permute-start | bytes 294920 | tf_op jit(solution)/shard_map/ppermute | solution.py:160
  14.7 11.1 %collective-permute-start.6 = (bf16[384,128]{1,0:T(8,128)(2,1)S(1)}, bf16[384,128]{1,0:T(8,128)(2,1)S(1)}, u32[]{:S(2)}, u32[]{:S(2)}) collective-permute-start(bf16[384,128]{1,0:T(8,128)(2,1)S(1)} %get-tuple-element.53), channel_id=1, source_target_pairs={{0,28},{4,0},{8,4},{12,8},{16,12},{20,16},{24,20},{28,24},{1,29},{... | collective-permute-start | bytes 294920 | tf_op jit(solution)/shard_map/ppermute | solution.py:160
  16.1 12.4 %collective-permute-start.7 = (bf16[384,128]{1,0:T(8,128)(2,1)S(1)}, bf16[384,128]{1,0:T(8,128)(2,1)S(1)}, u32[]{:S(2)}, u32[]{:S(2)}) collective-permute-start(bf16[384,128]{1,0:T(8,128)(2,1)S(1)} %get-tuple-element.58), channel_id=1, source_target_pairs={{0,4},{4,8},{8,12},{12,16},{16,20},{20,24},{24,28},{28,0},{1,5},{5... | collective-permute-start | bytes 294920 | tf_op jit(solution)/shard_map/ppermute | solution.py:160
  16.8 15.8 %collective-permute-start.8 = (bf16[384,128]{1,0:T(8,128)(2,1)S(1)}, bf16[384,128]{1,0:T(8,128)(2,1)S(1)}, u32[]{:S(2)}, u32[]{:S(2)}) collective-permute-start(bf16[384,128]{1,0:T(8,128)(2,1)S(1)} %get-tuple-element.59), channel_id=1, source_target_pairs={{0,8},{4,12},{8,16},{12,20},{16,24},{20,28},{24,0},{28,4},{1,9},{5... | collective-permute-start | bytes 294920 | tf_op jit(solution)/shard_map/ppermute | solution.py:160
  21.4 14.2 %collective-permute-start.9 = (bf16[384,128]{1,0:T(8,128)(2,1)S(1)}, bf16[384,128]{1,0:T(8,128)(2,1)S(1)}, u32[]{:S(2)}, u32[]{:S(2)}) collective-permute-start(bf16[384,128]{1,0:T(8,128)(2,1)S(1)} %get-tuple-element.60), channel_id=1, source_target_pairs={{0,12},{4,16},{8,20},{12,24},{16,28},{20,0},{24,4},{28,8},{1,13},{... | collective-permute-start | bytes 294920 | tf_op jit(solution)/shard_map/ppermute | solution.py:160
  25.2 10.4 %collective-permute-start.10 = (bf16[384,128]{1,0:T(8,128)(2,1)S(1)}, bf16[384,128]{1,0:T(8,128)(2,1)S(1)}, u32[]{:S(2)}, u32[]{:S(2)}) collective-permute-start(bf16[384,128]{1,0:T(8,128)(2,1)S(1)} %get-tuple-element.61), channel_id=1, source_target_pairs={{0,16},{4,20},{8,24},{12,28},{16,0},{20,4},{24,8},{28,12},{1,17},{... | collective-permute-start | bytes 294920 | tf_op jit(solution)/shard_map/ppermute | solution.py:160
  25.8 11.1 %collective-permute-start.11 = (bf16[384,128]{1,0:T(8,128)(2,1)S(1)}, bf16[384,128]{1,0:T(8,128)(2,1)S(1)}, u32[]{:S(2)}, u32[]{:S(2)}) collective-permute-start(bf16[384,128]{1,0:T(8,128)(2,1)S(1)} %get-tuple-element.62), channel_id=1, source_target_pairs={{0,20},{4,24},{8,28},{12,0},{16,4},{20,8},{24,12},{28,16},{1,21},{... | collective-permute-start | bytes 294920 | tf_op jit(solution)/shard_map/ppermute | solution.py:160
  28.5 8.4 %collective-permute-start.12 = (bf16[384,128]{1,0:T(8,128)(2,1)S(1)}, bf16[384,128]{1,0:T(8,128)(2,1)S(1)}, u32[]{:S(2)}, u32[]{:S(2)}) collective-permute-start(bf16[384,128]{1,0:T(8,128)(2,1)S(1)} %get-tuple-element.63), channel_id=1, source_target_pairs={{0,24},{4,28},{8,0},{12,4},{16,8},{20,12},{24,16},{28,20},{1,25},{... | collective-permute-start | bytes 294920 | tf_op jit(solution)/shard_map/ppermute | solution.py:160
  32.6 5.3 %collective-permute-start.13 = (bf16[384,128]{1,0:T(8,128)(2,1)S(1)}, bf16[384,128]{1,0:T(8,128)(2,1)S(1)}, u32[]{:S(2)}, u32[]{:S(2)}) collective-permute-start(bf16[384,128]{1,0:T(8,128)(2,1)S(1)} %get-tuple-element.64), channel_id=1, source_target_pairs={{0,28},{4,0},{8,4},{12,8},{16,12},{20,16},{24,20},{28,24},{1,29},{... | collective-permute-start | bytes 294920 | tf_op jit(solution)/shard_map/ppermute | solution.py:160
  41.0 9.0 %collective-permute-start.14 = (bf16[384,128]{1,0:T(8,128)(2,1)S(1)}, bf16[384,128]{1,0:T(8,128)(2,1)S(1)}, u32[]{:S(2)}, u32[]{:S(2)}) collective-permute-start(bf16[384,128]{1,0:T(8,128)(2,1)S(1)} %get-tuple-element.66), channel_id=1, source_target_pairs={{0,16},{4,20},{8,24},{12,28},{16,0},{20,4},{24,8},{28,12},{1,17},{... | collective-permute-start | bytes 294920 | tf_op jit(solution)/shard_map/ppermute | solution.py:160
  41.6 15.9 %collective-permute-start.15 = (bf16[384,128]{1,0:T(8,128)(2,1)S(1)}, bf16[384,128]{1,0:T(8,128)(2,1)S(1)}, u32[]{:S(2)}, u32[]{:S(2)}) collective-permute-start(bf16[384,128]{1,0:T(8,128)(2,1)S(1)} %get-tuple-element.67), channel_id=1, source_target_pairs={{0,4},{4,8},{8,12},{12,16},{16,20},{20,24},{24,28},{28,0},{1,5},{5... | collective-permute-start | bytes 294920 | tf_op jit(solution)/shard_map/ppermute | solution.py:160
  44.0 13.4 %collective-permute-start.16 = (bf16[384,128]{1,0:T(8,128)(2,1)S(1)}, bf16[384,128]{1,0:T(8,128)(2,1)S(1)}, u32[]{:S(2)}, u32[]{:S(2)}) collective-permute-start(bf16[384,128]{1,0:T(8,128)(2,1)S(1)} %get-tuple-element.68), channel_id=1, source_target_pairs={{0,28},{4,0},{8,4},{12,8},{16,12},{20,16},{24,20},{28,24},{1,29},{... | collective-permute-start | bytes 294920 | tf_op jit(solution)/shard_map/ppermute | solution.py:160
  46.2 11.2 %collective-permute-start.17 = (bf16[384,128]{1,0:T(8,128)(2,1)S(1)}, bf16[384,128]{1,0:T(8,128)(2,1)S(1)}, u32[]{:S(2)}, u32[]{:S(2)}) collective-permute-start(bf16[384,128]{1,0:T(8,128)(2,1)S(1)} %get-tuple-element.69), channel_id=1, source_target_pairs={{0,12},{4,16},{8,20},{12,24},{16,28},{20,0},{24,4},{28,8},{1,13},{... | collective-permute-start | bytes 294920 | tf_op jit(solution)/shard_map/ppermute | solution.py:160
  47.9 9.5 %collective-permute-start.18 = (bf16[384,128]{1,0:T(8,128)(2,1)S(1)}, bf16[384,128]{1,0:T(8,128)(2,1)S(1)}, u32[]{:S(2)}, u32[]{:S(2)}) collective-permute-start(bf16[384,128]{1,0:T(8,128)(2,1)S(1)} %get-tuple-element.70), channel_id=1, source_target_pairs={{0,20},{4,24},{8,28},{12,0},{16,4},{20,8},{24,12},{28,16},{1,21},{... | collective-permute-start | bytes 294920 | tf_op jit(solution)/shard_map/ppermute | solution.py:160
  50.0 9.8 %collective-permute-start.19 = (bf16[384,128]{1,0:T(8,128)(2,1)S(1)}, bf16[384,128]{1,0:T(8,128)(2,1)S(1)}, u32[]{:S(2)}, u32[]{:S(2)}) collective-permute-start(bf16[384,128]{1,0:T(8,128)(2,1)S(1)} %get-tuple-element.71), channel_id=1, source_target_pairs={{0,8},{4,12},{8,16},{12,20},{16,24},{20,28},{24,0},{28,4},{1,9},{5... | collective-permute-start | bytes 294920 | tf_op jit(solution)/shard_map/ppermute | solution.py:160
  57.4 4.6 %collective-permute-start.20 = (bf16[384,128]{1,0:T(8,128)(2,1)S(1)}, bf16[384,128]{1,0:T(8,128)(2,1)S(1)}, u32[]{:S(2)}, u32[]{:S(2)}) collective-permute-start(bf16[384,128]{1,0:T(8,128)(2,1)S(1)} %get-tuple-element.72), channel_id=1, source_target_pairs={{0,24},{4,28},{8,0},{12,4},{16,8},{20,12},{24,16},{28,20},{1,25},{... | collective-permute-start | bytes 294920 | tf_op jit(solution)/shard_map/ppermute | solution.py:160
  63.5 2.5 %collective-permute-start.21 = (bf16[192,2048]{1,0:T(8,128)(2,1)S(1)}, bf16[192,2048]{1,0:T(8,128)(2,1)S(1)}, u32[]{:S(2)}, u32[]{:S(2)}) collective-permute-start(bf16[192,2048]{1,0:T(8,128)(2,1)S(1)} %get-tuple-element.76), channel_id=1, source_target_pairs={{0,1},{1,0},{2,3},{3,2},{4,5},{5,4},{6,7},{7,6},{8,9},{9,8},{10,11... | collective-permute-start | bytes 2359304 | tf_op jit(solution)/shard_map/ppermute | solution.py:476
  66.1 12.0 %collective-permute-start.24 = (bf16[192,1024]{1,0:T(8,128)(2,1)S(1)}, bf16[192,1024]{1,0:T(8,128)(2,1)S(1)}, u32[]{:S(2)}, u32[]{:S(2)}) collective-permute-start(bf16[192,1024]{1,0:T(8,128)(2,1)S(1)} %shard_map.108), channel_id=1, source_target_pairs={{0,2},{1,3},{2,0},{3,1},{4,6},{5,7},{6,4},{7,5},{8,10},{9,11},{10,... | collective-permute-start | bytes 1179656 | tf_op jit(solution)/shard_map/ppermute | solution.py:463
  68.6 17.1 %collective-permute-start.23 = (bf16[192,1024]{1,0:T(8,128)(2,1)S(1)}, bf16[192,1024]{1,0:T(8,128)(2,1)S(1)}, u32[]{:S(2)}, u32[]{:S(2)}) collective-permute-start(bf16[192,1024]{1,0:T(8,128)(2,1)S(1)} %shard_map.107), channel_id=1, source_target_pairs={{0,2},{1,3},{2,0},{3,1},{4,6},{5,7},{6,4},{7,5},{8,10},{9,11},{10,... | collective-permute-start | bytes 1179656 | tf_op jit(solution)/shard_map/ppermute | solution.py:463
  (8 other events, 129.4 us)
